TPU v7x, 256 devices: a whole 4x4x8 slice. The times are simulated.
256 devices in a mesh: wide: 32 (over y, z), bulk: 8 (over x, core).
Axes of the slice: x: 4, y: 4, z: 8, core: 2. Of those that a mesh axis runs over, the one named last changes fastest.
Arguments:
- waveforms: bfloat16 [8, 128, 10240], P('bulk', 'wide'), may hold values from -20 to 20
- owner_of: int32 [8, 128], P('bulk', 'wide'), may hold values from 0 to 31, as said below
- lengths: int32 [8, 128], P('bulk', 'wide'), may hold values from 2560 to 10240, as said below
- cotangent: bfloat16 [8, 32, 2048, 512], P('bulk', 'wide'), may hold values from -0.029907227 to 0.029907227
- conv_first: bfloat16 [10, 512], replicated, may hold values from -2 to 2
- norm_gain: float32 [512], replicated, may hold values from 0.1 to 1.9
- norm_bias: float32 [512], replicated, may hold values from -2 to 2
- conv_second: bfloat16 [1536, 512], replicated, may hold values from -0.15625 to 0.15625
Outputs:
- grad_second: float32 [1536, 512], P('wide', 'bulk')
- grad_first: float32 [10, 512], replicated
- grad_gain: float32 [512], replicated
- grad_bias: float32 [512], replicated
Inputs may be any that keep to these rules, and one draw needn't show every extreme that they name: `owner_of`: within each replica group every owner index is named by exactly 4 utterances, whose lengths sum to exactly 20480. Utterance l * 4 + s (loader l, slot s) has owner l XOR m[s], where the 4 values m[s] depend on the group and the slot only and are distinct. `lengths`: every length is a multiple of 10.
All inputs are finite; a program needn't handle non-finite values.
Results may differ from a plain program's by a relative error of at most 0.0049.
Values may be sent and summed in bfloat16 or wider, within the bound.
No kernel may reach another device: no remote copies, remote signals or barrier semaphores. Data moves between devices by JAX's collectives and lax.ppermute only.
A program may use at most 128 MiB of HBM per device.

v0:
```python
import jax
import jax.numpy as jnp
from jax import lax
from jax.sharding import PartitionSpec as P


def gelu_value(values):
    return 0.5 * values * (1.0 + lax.erf(values * 0.7071067811865476))


def gelu_slope(values):
    return (
        0.5 * (1.0 + lax.erf(values * 0.7071067811865476))
        + values * jnp.exp(-0.5 * values * values) * 0.3989422804014327
    )


def plan_offsets(table_owner, table_len):
    row_index = jnp.arange(table_owner.shape[0], dtype=jnp.int32)
    before = (row_index[None, :] < row_index[:, None]) & (
        table_owner[None, :] == table_owner[:, None]
    )
    offsets = jnp.sum(jnp.where(before, table_len[None, :], 0), axis=1)
    ranking = jnp.sum(before.astype(jnp.int32), axis=1)
    return (offsets, ranking)


def segment_mask(frame_count, begin, length):
    frame_index = jnp.arange(frame_count, dtype=jnp.int32)
    inside = (frame_index[None, :] >= begin[:, None]) & (
        frame_index[None, :] < (begin + length)[:, None]
    )
    return inside.astype(jnp.float32)


def owner_terms(
    stream, seg_start, seg_size, cot_rows, conv_first, norm_gain, norm_bias, conv_second
):
    highest = lax.Precision.HIGHEST
    capacity = stream.shape[0]
    early_count = capacity // 5
    late_count = capacity // 10
    channels = conv_first.shape[1]
    padded = jnp.concatenate([stream, jnp.zeros((5,), stream.dtype)])
    five_rows = padded.reshape(early_count + 1, 5)
    early_taps = jnp.concatenate([five_rows[:-1], five_rows[1:]], axis=1)
    early_pre = jnp.dot(early_taps, conv_first, preferred_element_type=jnp.float32)
    member = segment_mask(early_count, seg_start // 5, seg_size // 5 - 1)
    early_valid = jnp.sum(member, axis=0)[:, None]
    seg_counts = (seg_size // 5 - 1).astype(jnp.float32)[:, None]
    seg_means = jnp.dot(member, early_pre, precision=highest) / seg_counts
    centered = (early_pre - jnp.dot(member.T, seg_means, precision=highest)) * early_valid
    seg_spread = jnp.dot(member, centered * centered, precision=highest) / seg_counts
    inv_scale = lax.rsqrt(seg_spread + 1e-05)
    frame_scale = jnp.dot(member.T, inv_scale, precision=highest)
    normed = centered * frame_scale
    act_in = normed * norm_gain + norm_bias
    early_act = (gelu_value(act_in) * early_valid).astype(jnp.bfloat16)
    padded_rows = jnp.concatenate([early_act, jnp.zeros((1, channels), jnp.bfloat16)])
    late_taps = jnp.concatenate(
        [
            padded_rows[0:early_count:2],
            padded_rows[1:early_count:2],
            padded_rows[2 : early_count + 1 : 2],
        ],
        axis=1,
    )
    late_pre = jnp.dot(late_taps, conv_second, preferred_element_type=jnp.float32)
    late_valid = jnp.sum(segment_mask(late_count, seg_start // 10, seg_size // 10 - 1), axis=0)[
        :, None
    ]
    late_grad = (cot_rows.astype(jnp.float32) * gelu_slope(late_pre) * late_valid).astype(
        jnp.bfloat16
    )
    contract = (((1,), (1,)), ((), ()))
    back_zero = lax.dot_general(
        late_grad, conv_second[0:channels], contract, preferred_element_type=jnp.float32
    )
    back_one = lax.dot_general(
        late_grad,
        conv_second[channels : 2 * channels],
        contract,
        preferred_element_type=jnp.float32,
    )
    back_two = lax.dot_general(
        late_grad,
        conv_second[2 * channels : 3 * channels],
        contract,
        preferred_element_type=jnp.float32,
    )
    even_rows = back_zero + jnp.concatenate([jnp.zeros((1, channels), jnp.float32), back_two[:-1]])
    early_back = jnp.stack([even_rows, back_one], axis=1).reshape(early_count, channels)
    act_grad = early_back * gelu_slope(act_in) * early_valid
    grad_bias = jnp.sum(act_grad, axis=0)
    grad_gain = jnp.sum(act_grad * normed, axis=0)
    scaled = act_grad * norm_gain
    first_mean = jnp.dot(member, scaled, precision=highest) / seg_counts
    cross_mean = jnp.dot(member, scaled * normed, precision=highest) / seg_counts
    spread_back = jnp.dot(member.T, first_mean, precision=highest) + normed * jnp.dot(
        member.T, cross_mean, precision=highest
    )
    early_grad = ((scaled - spread_back) * frame_scale).astype(jnp.bfloat16)
    grad_first = lax.dot_general(
        early_taps, early_grad, (((0,), (0,)), ((), ())), preferred_element_type=jnp.float32
    )
    return (late_taps, late_grad, grad_first, grad_gain, grad_bias)


def per_device(
    waveforms, owner_of, lengths, cotangent, conv_first, norm_gain, norm_bias, conv_second
):
    table_owner, table_len = (
        lax.all_gather(owner_of[0], "wide", axis=0, tiled=True),
        lax.all_gather(lengths[0], "wide", axis=0, tiled=True),
    )
    offsets, ranking = plan_offsets(table_owner, table_len)
    my_owner = lax.axis_index("wide")
    slot_count = waveforms.shape[1]
    longest = waveforms.shape[2]
    capacity = cotangent.shape[2] * 10
    positions = jnp.arange(longest, dtype=jnp.int32)
    slot_index = jnp.arange(slot_count, dtype=jnp.int32)
    xor_masks = table_owner[:slot_count]
    sources = jnp.bitwise_xor(my_owner, xor_masks)
    global_rows = sources * slot_count + slot_index
    gathered = lax.all_gather(waveforms[0], "wide", axis=0, tiled=True)
    owned = jnp.take(gathered, global_rows, axis=0)
    row_offsets = offsets[global_rows]
    row_lengths = table_len[global_rows]
    row_ranks = ranking[global_rows]
    buffer = jnp.zeros((capacity + longest,), jnp.bfloat16)
    for slot_pos in range(slot_count):
        samples = jnp.where(
            positions < row_lengths[slot_pos], owned[slot_pos], jnp.zeros((), jnp.bfloat16)
        )
        window = lax.dynamic_slice_in_dim(buffer, row_offsets[slot_pos], longest) + samples
        buffer = lax.dynamic_update_slice_in_dim(buffer, window, row_offsets[slot_pos], 0)
    matches = slot_index[:, None] == row_ranks[None, :]
    seg_start = jnp.sum(jnp.where(matches, row_offsets[None, :], 0), axis=1)
    seg_size = jnp.sum(jnp.where(matches, row_lengths[None, :], 0), axis=1)
    stream = buffer[:capacity]
    late_taps, late_grad, grad_first, grad_gain, grad_bias = owner_terms(
        stream, seg_start, seg_size, cotangent[0, 0], conv_first, norm_gain, norm_bias, conv_second
    )
    partial_rows = lax.psum_scatter(
        lax.dot_general(
            late_taps, late_grad, (((0,), (0,)), ((), ())), preferred_element_type=jnp.float32
        ),
        "wide",
        scatter_dimension=0,
        tiled=True,
    )
    grad_second = lax.psum_scatter(partial_rows, "bulk", scatter_dimension=1, tiled=True)
    grad_first, grad_gain, grad_bias = lax.psum(
        (grad_first, grad_gain, grad_bias), ("wide", "bulk")
    )
    return (grad_second, grad_first, grad_gain, grad_bias)


def solution(mesh):
    placed = (
        P("bulk", "wide", None),
        P("bulk", "wide"),
        P("bulk", "wide"),
        P("bulk", "wide", None, None),
        P(),
        P(),
        P(),
        P(),
    )
    return jax.shard_map(
        per_device,
        mesh=mesh,
        in_specs=placed,
        out_specs=(P("wide", "bulk"), P(), P(), P()),
        check_vma=False,
    )
```

profile of v0, /device:TPU:32, one launch (start us, length us, event | category | flops | bytes accessed | tf_op | source)
XLA Modules:
  0.0 518.4 jit_solution(2598624127636322522)
XLA Ops:
  12.4 22.9 %all-reduce.4 = (s32[128]{0:T(128)S(1)}, s32[128]{0:T(128)S(1)}) all-reduce(s32[128]{0:T(128)S(1)} %bitcast_dynamic-update-slice_fusion.1, s32[128]{0:T(128)S(1)} %bitcast_dynamic-update-slice_fusion), channel_id=2, replica_groups=mesh['wide'=32,'bulk'=8] {'wide'}, use_global_device_ids=true, to_apply=%add.2 | all-reduce | flops 256 | bytes 2048 | tf_op jit(solution)/shard_map/all_gather | solution.py:114
  46.8 51.5 %all-gather.5.cloned.1.call-done = bf16[1,128,10240]{2,0,1:T(2,128)(2,1)} async-done(((bf16[1,4,10240]{2,0,1:T(2,128)(2,1)}), bf16[1,128,10240]{2,0,1:T(2,128)(2,1)}) %all-gather.5.cloned.1.call-update) | async-done | bytes 2621456 | tf_op jit(solution)/shard_map/all_gather | solution.py:126
  98.3 4.0 copy.30
  114.9 2.9 convolution_divide_fusion
  117.7 5.6 %subtract_multiply_fusion = f32[4096,512]{1,0:T(8,128)S(1)} fusion(f32[4096,512]{1,0:T(8,128)S(1)} %fusion.45, f32[4,512]{1,0:T(4,128)S(1)} %convolution_divide_fusion, f32[4096]{0:T(1024)S(1)} %convert_reduce_fusion, s32[4]{0:T(128)S(1)} %get-tuple-element.22, s32[4]{0:T(128)S(1)} %get-tuple-element.23), kind=kOutput, calls=%fused_computation.21 | convolution fusion | flops 104906752 | bytes 16801824 | tf_op jit(solution)/shard_map/dot_general | solution.py:52
  123.4 3.0 fusion.35
  126.4 9.9 %multiply_convert_fusion.1 = (bf16[4096,512]{1,0:T(8,128)(2,1)}, f32[4096,512]{1,0:T(8,128)}, f32[4096,512]{1,0:T(8,128)}) fusion(f32[512]{0:T(512)S(1)} %copy-done.9, f32[512]{0:T(512)S(1)} %copy-done.7, f32[4096]{0:T(1024)S(1)} %convert_reduce_fusion, f32[4096,512]{1,0:T(8,128)S(1)} %subtract_multiply_fusion, f32[4,512]{1,0:T(4,128)S(1)} %fusion.35, ...), kind=kOutput, calls=%fused_computation.16 | convolution fusion | flops 119586816 | bytes 29388832 | tf_op jit(solution)/shard_map/dot_general | solution.py:55
  136.3 20.5 %slice.114 = bf16[2048,512]{1,0:T(8,128)(2,1)} slice(bf16[4096,512]{1,0:T(8,128)(2,1)} %get-tuple-element.20), slice={[1:4096:2], [0:512:1]} | slice | bytes 4194304 | tf_op jit(solution)/shard_map/slice | solution.py:63
  156.8 20.4 %slice.113 = bf16[2048,512]{1,0:T(8,128)(2,1)} slice(bf16[4096,512]{1,0:T(8,128)(2,1)} %get-tuple-element.20), slice={[0:4096:2], [0:512:1]} | slice | bytes 4194304 | tf_op jit(solution)/shard_map/slice | solution.py:62
  177.2 3.7 concatenate.17
  181.0 20.7 %slice.115 = bf16[2048,512]{1,0:T(8,128)(2,1)} slice(bf16[4097,512]{1,0:T(8,128)(2,1)} %concatenate.17), slice={[2:4097:2], [0:512:1]} | slice | bytes 4194304 | tf_op jit(solution)/shard_map/slice | solution.py:64
  201.7 7.9 %fusion.19 = bf16[2048,512]{1,0:T(8,128)(2,1)S(1)} fusion(bf16[1,1,2048,512]{3,2,1,0:T(8,128)(2,1)} %param.11, f32[2048]{0:T(1024)S(1)} %convert_reduce_fusion.2, bf16[1536,512]{1,0:T(8,128)(2,1)} %param.15, bf16[2048,512]{1,0:T(8,128)(2,1)} %slice.115, bf16[2048,512]{1,0:T(8,128)(2,1)} %slice.114, bf16[2048,512]{1,0:T(8,128)(2,1)} %slice.113), kind=kOutput, calls=%fused_computation.33 | convolution fusion | flops 3252682752 | bytes 12066816 | tf_op jit(solution)/shard_map/dot_general | solution.py:68
  209.6 4.9 fusion.22
  215.0 2.5 convolution_bitcast_fusion
  221.2 16.5 %copy.25 = f32[2048,2,512]{2,1,0:T(2,128)} copy(f32[2048,2,512]{2,0,1:T(8,128)S(1)} %pad_maximum_fusion) | data formatting | bytes 16777216 | tf_op jit(solution)/shard_map/stack | solution.py:92
  237.7 10.9 %reshape.97 = f32[4096,512]{1,0:T(8,128)} reshape(f32[2048,2,512]{2,1,0:T(2,128)} %copy.25) | data formatting | bytes 16777216 | tf_op jit(solution)/shard_map/reshape | solution.py:92
  248.6 10.5 %fusion.71 = (f32[512]{0:T(512)S(1)}, f32[512]{0:T(512)S(1)}, f32[4096,512]{1,0:T(8,128)S(1)}) fusion(f32[4096,512]{1,0:T(8,128)} %get-tuple-element.21, f32[4096]{0:T(1024)S(1)} %convert_reduce_fusion, f32[4096,512]{1,0:T(8,128)} %reshape.97, f32[512]{0:T(512)S(1)} %copy-done.9, f32[512]{0:T(512)S(1)} %copy-done.7), kind=kLoop, calls=%fused_computation.105 | loop fusion | flops 31456256 | bytes 25190400 | tf_op jit(solution)/shard_map/reduce_sum | solution.py:94
  259.1 3.1 fusion.26
  262.2 6.0 %fusion.63 = f32[4096,512]{1,0:T(8,128)} fusion(f32[4,512]{1,0:T(4,128)S(1)} %fusion.26, s32[4]{0:T(128)S(1)} %get-tuple-element.22, s32[4]{0:T(128)S(1)} %get-tuple-element.23), kind=kOutput, calls=%fused_computation.103 | convolution fusion | flops 100712448 | bytes 8396832 | tf_op jit(solution)/shard_map/dot_general | solution.py:99
  268.2 3.5 fusion.38
  271.7 12.4 %multiply_convert_fusion = bf16[4096,512]{1,0:T(8,128)(2,1)} fusion(f32[4096,512]{1,0:T(8,128)} %get-tuple-element.41, f32[4096,512]{1,0:T(8,128)} %fusion.63, f32[4096,512]{1,0:T(8,128)S(1)} %bitcast.43, f32[4096,512]{1,0:T(8,128)} %copy-done.2, f32[4,512]{1,0:T(4,128)S(1)} %fusion.38, f32[512]{0:T(512)S(1)} %copy-done.7, s32[4]{0:T(128)S(1)} %get-tuple-element.22, ...), kind=kOutput, calls=%fused_computation.13 | convolution fusion | flops 113295360 | bytes 37759008 | tf_op jit(solution)/shard_map/dot_general | solution.py:99
  284.1 146.3 %reduce-scatter.5.cloned.1.call-done = f32[48,512]{1,0:T(8,128)} async-done(((f32[1536,512]{1,0:T(8,128)}), f32[48,512]{1,0:T(8,128)}) %reduce-scatter.5.cloned.1.call-update) | async-done | bytes 98320 | tf_op jit(solution)/shard_map/reduce_scatter | solution.py:145
  432.1 2.8 fusion.44
  435.0 75.3 %all-reduce.5 = (f32[10,512]{1,0:T(8,128)}, f32[512]{0:T(512)}, f32[512]{0:T(512)}) all-reduce(f32[10,512]{1,0:T(8,128)S(1)} %fusion.44, f32[512]{0:T(512)S(1)} %get-tuple-element.5, f32[512]{0:T(512)S(1)} %get-tuple-element.4), channel_id=1, replica_groups=mesh['wide'=32,'bulk'=8] {'wide','bulk'}, use_global_device_ids=true, to_apply=%region_8.9 | all-reduce | flops 6144 | bytes 49152 | tf_op jit(solution)/shard_map/psum | solution.py:154
  (75 shorter events, 28.1 us)
Async XLA Ops:
  7.2 106.4 %copy-start = (bf16[10,512]{1,0:T(8,128)(2,1)S(1)}, bf16[10,512]{1,0:T(8,128)(2,1)}, u32[]{:S(2)}) copy-start(bf16[10,512]{1,0:T(8,128)(2,1)} %param.12) | copy-start | bytes 30724
  7.2 101.2 %copy-start.8 = (pred[20485]{0:T(1024)(128)(4,1)S(1)}, pred[20485]{0:T(1024)(128)(4,1)}, u32[]{:S(2)}) copy-start(pred[20485]{0:T(1024)(128)(4,1)} %constant.30.clone.1) | copy-start | bytes 61459
  7.2 91.1 %all-gather.5.cloned.1.call-start = ((), (), s32[]{:S(2)}) async-start(), calls=%async_computation.3 | async-start | bytes 5406720 | tf_op jit(solution)/shard_map/all_gather | solution.py:126
  8.9 421.5 %reduce-scatter.5.cloned.1.call-start = ((), (), s32[]{:S(2)}) async-start(), calls=%async_computation.2 | async-start | bytes 3244032 | tf_op jit(solution)/shard_map/reduce_scatter | solution.py:145
  123.3 3.1 copy-start.7
  123.3 3.1 copy-start.9
  201.7 7.9 %copy-start.3 = (bf16[2048,512]{1,0:T(8,128)(2,1)S(1)}, bf16[2048,512]{1,0:T(8,128)(2,1)}, u32[]{:S(2)}) copy-start(bf16[2048,512]{1,0:T(8,128)(2,1)} %slice.114) | copy-start | bytes 6291460
  201.7 7.9 %copy-start.4 = (bf16[2048,512]{1,0:T(8,128)(2,1)S(1)}, bf16[2048,512]{1,0:T(8,128)(2,1)}, u32[]{:S(2)}) copy-start(bf16[2048,512]{1,0:T(8,128)(2,1)} %slice.113) | copy-start | bytes 6291460
  201.7 7.9 %copy-start.5 = (bf16[2048,512]{1,0:T(8,128)(2,1)S(1)}, bf16[2048,512]{1,0:T(8,128)(2,1)}, u32[]{:S(2)}) copy-start(bf16[2048,512]{1,0:T(8,128)(2,1)} %slice.115) | copy-start | bytes 6291460
  214.5 295.7 %reduce-scatter.7.cloned.1.call-start = ((), (), s32[]{:S(2)}) async-start(), calls=%async_computation.4 | async-start | bytes 294912
  215.0 2.5 copy-start.6
  259.1 9.1 %copy-start.2 = (f32[4096,512]{1,0:T(8,128)}, f32[4096,512]{1,0:T(8,128)S(1)}, u32[]{:S(2)}) copy-start(f32[4096,512]{1,0:T(8,128)S(1)} %get-tuple-element.19) | copy-start | bytes 25165828
  259.1 9.1 %slice-start = ((s8[8388608]{0:T(1024)(128)(4,1)}), s8[4194304]{0:T(1024)(128)(4,1)S(1)}, s32[]{:S(2)}) async-start(s8[8388608]{0:T(1024)(128)(4,1)} %bitcast.42), calls=%async_computation.5 | async-start | bytes 8388608
  262.2 6.0 %slice-start.1 = ((s8[8388608]{0:T(1024)(128)(4,1)}), s8[4194304]{0:T(1024)(128)(4,1)S(1)}, s32[]{:S(2)}) async-start(s8[8388608]{0:T(1024)(128)(4,1)} %bitcast.42), calls=%async_computation.6 | async-start | bytes 8388608
  271.7 240.0 %copy-start.1 = (bf16[10,512]{1,0:T(8,128)(2,1)S(1)}, bf16[10,512]{1,0:T(8,128)(2,1)}, u32[]{:S(2)}) copy-start(bf16[10,512]{1,0:T(8,128)(2,1)} %param.12) | copy-start | bytes 30724
Sparse Core Ops, SparseCore 0:
  10.6 87.6 all-gather.4
  214.7 215.6 reduce-scatter.4
  433.0 32.1 reduce-scatter.6
where the time goes:
time: 527 us; the launch traced here: 518 us
  waiting for transfers between devices  198 us (38%)
  local copies, waits for them, and re-layouts  116 us (22%)
  blocking collectives  98.2 us (19%)
  matrix products  68.4 us (13%)
  between operations  22.7 us (4%)
  other arithmetic  15 us (3%)
    reduce_scatter x1, waiting for transfers between devices, per_device(): lax.psum_scatter(lax.dot_general(late_taps, late_grad, (((0,), (0,)), (()...  146 us
    psum x1, blocking collectives, per_device(): lax.psum((grad_first, grad_gain, grad_bias), ('wide', 'bulk'))  75.3 us
    all_gather x1, waiting for transfers between devices, per_device(): gathered = lax.all_gather(waveforms[0], 'wide', axis=0, tiled=True)  51.5 us
    all_gather x1, blocking collectives, per_device(): lax.all_gather(lengths[0], 'wide', axis=0, tiled=True)  22.9 us
    slice x1, local copies, waits for them, and re-layouts, owner_terms(): padded_rows[2:early_count + 1:2]  20.7 us
    slice x1, local copies, waits for them, and re-layouts, owner_terms(): padded_rows[1:early_count:2]  20.5 us
    slice x1, local copies, waits for them, and re-layouts, owner_terms(): padded_rows[0:early_count:2]  20.4 us
    another operation x1, local copies, waits for them, and re-layouts, owner_terms(): jnp.stack([even_rows, back_one], axis=1).reshape(early_count, channels)  16.5 us
  transfers between devices with their start and end apart: 3, of which 2 were waited for; matrix products, arithmetic and copies ran while one was open for 15% of the time, Pallas kernels for 0%

commit v1 on v0

v1 whole, which is shorter than its diff:
```python
import functools

import jax
import jax.numpy as jnp
from jax import lax
from jax.experimental import pallas as pl
from jax.experimental.pallas import tpu as pltpu
from jax.sharding import PartitionSpec as P

F32 = jnp.float32
BF16 = jnp.bfloat16
HIGHEST = lax.Precision.HIGHEST
SLOTS = 4
TAPS = 10
GRAN = 1024
ROWS = 2048
CH = 512
BLK = 256


def dot(a, b, precision=None):
    return jnp.dot(a, b, preferred_element_type=F32, precision=precision)


def dot_t(a, b, precision=None):
    return lax.dot_general(
        a, b, (((0,), (0,)), ((), ())), preferred_element_type=F32, precision=precision
    )


def cdf_slope(v):
    e = jnp.exp2(v * v * (-0.5 * 1.4426950408889634))
    d = 1.0 + jnp.abs(v) * (0.3275911 * 0.7071067811865476)
    r = pl.reciprocal(d, approx=True)
    t = r * (2.0 - d * r)
    poly = 0.5 * 1.061405429
    for c in (-1.453152027, 1.421413741, -0.284496736, 0.254829592):
        poly = poly * t + 0.5 * c
    tail = poly * t * e
    cdf = jnp.where(v < 0.0, tail, 1.0 - tail)
    return cdf, cdf + v * (e * 0.3989422804014327)


def plan(sc):
    size = [sc[s] for s in range(SLOTS)]
    src = [sc[SLOTS + s] for s in range(SLOTS)]
    rank, off = [], []
    for s in range(SLOTS):
        before = [(src[q] < src[s]).astype(jnp.int32) for q in range(SLOTS) if q != s]
        sizes = [size[q] for q in range(SLOTS) if q != s]
        rank.append(sum(before))
        off.append(sum(b * n for b, n in zip(before, sizes)))
    out = []
    for r in range(SLOTS):
        hit = [(rank[s] == r).astype(jnp.int32) for s in range(SLOTS)]
        out.append(
            (
                sum(h * s for s, h in enumerate(hit)),
                sum(h * o for o, h in zip(off, hit)),
                sum(h * n for n, h in zip(size, hit)),
            )
        )
    return out


def by_lane(values, index):
    out = values[0]
    for s in range(1, len(values)):
        out = jnp.where(index == s, values[s], out)
    return out


def forward_kernel(
    sc, u, cot, wst, gain, bias, w2,
    lg, sl, keep, send, xs, nst, tc, im,
    buf, xd, xbig, wbig, acc,
):
    step = pl.program_id(0)
    segs = plan(sc)

    @pl.when(step == 0)
    def _():
        buf[pl.ds(ROWS, 8), :] = jnp.zeros((8, 128), F32)
        for slot, off, _n in segs:
            buf[pl.ds(off, GRAN), :] = u[pl.ds(pl.multiple_of(slot * GRAN, GRAN), GRAN), :]
        src = lax.broadcasted_iota(jnp.int32, (128, 256), 0)
        tap = lax.broadcasted_iota(jnp.int32, (128, 256), 1) % 16
        r0 = ((tap == src) & (src < TAPS)).astype(F32).astype(BF16)
        r1 = ((tap == src + TAPS) & (src < 5)).astype(F32).astype(BF16)
        one = (lax.broadcasted_iota(jnp.int32, (1, 256), 1) % 16 == 15).astype(F32)
        lane = lax.broadcasted_iota(jnp.int32, (1, 256), 1)
        starts = [o for _s, o, _n in segs]
        ends = [o + n for _s, o, n in segs]
        lo_big, hi_big = by_lane(starts, lane // 64), by_lane(ends, lane // 64)
        lane1 = lane[:, :128]
        odd = (lane1 // 16) % 2
        lo_d = by_lane(starts, lane1 // 32)
        hi_all = by_lane(ends, lane1 // 32)
        hi_d = hi_all - odd
        count = (hi_d - lo_d).astype(F32)

        sums = jnp.zeros((1, 128), F32)
        for rb in range(ROWS // BLK):
            base = rb * BLK
            b0 = buf[pl.ds(base, BLK), :].astype(BF16)
            b1 = buf[pl.ds(base + 1, BLK), :].astype(BF16)
            xr = dot(b0, r0) + dot(b1, r1) + one
            row = lax.broadcasted_iota(jnp.int32, (BLK, 1), 0) + base
            xbig[pl.ds(base, BLK), :] = jnp.where((row >= lo_big) & (row < hi_big), xr, 0.0).astype(BF16)
            x1 = xr[:, :128]
            raw = jnp.where((row >= lo_d) & (row < hi_d), x1, 0.0)
            sums = sums + jnp.sum(raw, axis=0, keepdims=True)
            xd[pl.ds(base, BLK), :] = x1
            full = jnp.where((row >= lo_d) & (row < hi_all), x1, 0.0)
            xs[0, pl.ds(base, BLK), :] = jnp.where(odd == 0, full, 0.0).astype(BF16)
            xs[1, pl.ds(base, BLK), :] = jnp.where(odd == 1, full, 0.0).astype(BF16)
        xbig[pl.ds(ROWS, 16), :] = jnp.zeros((16, 256), BF16)
        mu = sums / count
        moment = jnp.zeros((128, 128), F32)
        for rb in range(ROWS // BLK):
            base = rb * BLK
            row = lax.broadcasted_iota(jnp.int32, (BLK, 1), 0) + base
            d = jnp.where((row >= lo_d) & (row < hi_d), xd[pl.ds(base, BLK), :] - mu, 0.0)
            moment = moment + dot_t(d, d, HIGHEST)
        ri = lax.broadcasted_iota(jnp.int32, (128, 128), 0)
        ci = lax.broadcasted_iota(jnp.int32, (128, 128), 1)
        moment = jnp.where(ri // 16 == ci // 16, moment, 0.0)
        wrow = wst[...]
        v = dot(moment, wrow, HIGHEST)
        block8 = (
            lax.broadcasted_iota(jnp.int32, (8, 128), 0)
            == lax.broadcasted_iota(jnp.int32, (8, 128), 1) // 16
        ).astype(F32)
        u8 = dot(block8 * mu, wrow, HIGHEST)
        q8 = dot(block8, v * wrow, HIGHEST)
        tcol = jnp.sum(jnp.where(ri == ci, sums, 0.0), axis=1, keepdims=True)
        tc[...] = jnp.broadcast_to(tcol, (128, 128))
        e15 = (lax.broadcasted_iota(jnp.int32, (16, 1), 0) == 15).astype(F32)
        for s, (_slot, _off, n) in enumerate(segs):
            n_even = n.astype(F32)
            n_odd = n_even - 1.0
            n_all = n_even + n_odd
            ue, uo = u8[2 * s : 2 * s + 1], u8[2 * s + 1 : 2 * s + 2]
            mean = (n_even * ue + n_odd * uo) / n_all
            de, do = ue - mean, uo - mean
            spread = (
                q8[2 * s : 2 * s + 1] + q8[2 * s + 1 : 2 * s + 2]
                + n_even * de * de + n_odd * do * do
            ) / n_all
            inv = lax.rsqrt(spread + 1e-05)
            a = gain[...] * inv
            b = bias[...] - a * mean
            im[s : s + 1, :] = inv
            im[4 + s : 5 + s, :] = mean
            for g, dev in enumerate((de, do)):
                at = 32 * s + 16 * g
                nst[at : at + 16, :] = v[at : at + 16] + tcol[at : at + 16] * dev
                f = wrow[at : at + 16] * a + e15 * b
                p0 = f.astype(BF16)
                f = f - p0.astype(F32)
                p1 = f.astype(BF16)
                f = f - p1.astype(F32)
                cols = pl.ds(g * CH, CH)
                wbig[64 * s : 64 * s + 16, cols] = p0
                wbig[64 * s + 16 : 64 * s + 32, cols] = p1
                wbig[64 * s + 32 : 64 * s + 48, cols] = f.astype(BF16)
                wbig[64 * s + 48 : 64 * s + 64, cols] = jnp.zeros((16, CH), BF16)
        acc[...] = jnp.zeros_like(acc)

    base = pl.multiple_of(step * BLK, BLK)
    pre_e = dot(xbig[pl.ds(base, BLK + 16), :], wbig[:, :CH])
    pre_o = dot(xbig[pl.ds(base, BLK), :], wbig[:, CH:])
    c_e, s_e = cdf_slope(pre_e)
    act_e = pre_e * c_e
    c_o, s_o = cdf_slope(pre_o)
    sl[0] = s_e[:BLK]
    sl[1] = s_o
    taps = jnp.concatenate(
        [act_e[:BLK].astype(BF16), (pre_o * c_o).astype(BF16), act_e[1 : BLK + 1].astype(BF16)], axis=1
    )
    late = dot(taps, w2[...])
    _c, slope = cdf_slope(late)
    row = lax.broadcasted_iota(jnp.int32, (BLK, 1), 0) + base
    drop = row == segs[0][1] + segs[0][2] - 1
    for _s, off, n in segs[1:]:
        drop = drop | (row == off + n - 1)
    grad = jnp.where(drop, 0.0, cot[...].astype(F32) * slope).astype(BF16)
    lg[...] = grad
    acc[...] += dot_t(grad, taps)

    @pl.when(step == pl.num_programs(0) - 1)
    def _():
        core = sc[8]
        for x in range(4):
            mine = pl.ds(pl.multiple_of(x * 128 + core * 64, 64), 64)
            other = pl.ds(pl.multiple_of(x * 128 + (1 - core) * 64, 64), 64)
            keep[x] = acc[mine, :]
            send[x] = acc[other, :].astype(BF16)


def backward_kernel(sc, lg, sl, xs, wt, wst, gain, nst, tc, im, out, acc, carry):
    step = pl.program_id(0)

    @pl.when(step == 0)
    def _():
        acc[...] = jnp.zeros_like(acc)
        carry[...] = jnp.zeros_like(carry)

    grad = lg[...]
    third = dot(grad, wt[:, 2 * CH :])
    row = lax.broadcasted_iota(jnp.int32, (BLK, 1), 0)
    shifted = jnp.where(row == 0, carry[0:1, :], pltpu.roll(third, 1, 0))
    carry[0:1, :] = third[BLK - 1 : BLK]
    ag_e = (dot(grad, wt[:, :CH]) + shifted) * sl[0]
    ag_o = dot(grad, wt[:, CH : 2 * CH]) * sl[1]
    total = acc[...]
    for part, ag in ((xs[0], ag_e), (xs[1], ag_o)):
        high = ag.astype(BF16)
        low = (ag - high.astype(F32)).astype(BF16)
        total = total + dot_t(part, high) + dot_t(part, low)
    acc[...] = total

    @pl.when(step == pl.num_programs(0) - 1)
    def _():
        segs = plan(sc)
        z = jnp.zeros((32, CH), F32)
        g_bias = jnp.zeros((1, CH), F32)
        g_gain = jnp.zeros((1, CH), F32)
        g = gain[...]
        for s, (_slot, _off, n) in enumerate(segs):
            at = 32 * s
            a = acc[at : at + 32, :]
            inv, mean = im[s : s + 1, :], im[4 + s : 5 + s, :]
            count = 2.0 * n.astype(F32) - 1.0
            s1 = a[15:16] + a[31:32]
            s2 = inv * (jnp.sum(a * wst[at : at + 32, :], axis=0, keepdims=True) - mean * s1)
            first = g * s1 / count
            cross = g * s2 / count
            z = z + inv * (
                g * a - first * tc[at : at + 32, 0:1] - (cross * inv) * nst[at : at + 32, :]
            )
            g_bias = g_bias + s1
            g_gain = g_gain + s2
        out[0:10, :] = z[0:10] + z[21:31]
        out[10:11, :] = g_gain
        out[11:12, :] = g_bias
        out[12:16, :] = jnp.zeros((4, CH), F32)


def full(shape):
    return pl.BlockSpec(shape, lambda i, sc: (0,) * len(shape))


def forward(sc, u, cot, wst, gain, bias, w2):
    shapes = [
        ((ROWS, CH), BF16, pl.BlockSpec((BLK, CH), lambda i, sc: (i, 0))),
        ((2, ROWS, CH), F32, pl.BlockSpec((2, BLK, CH), lambda i, sc: (0, i, 0))),
        ((4, 64, 3 * CH), F32, None),
        ((4, 64, 3 * CH), BF16, None),
        ((2, ROWS, 128), BF16, None),
        ((128, CH), F32, None),
        ((128, 128), F32, None),
        ((8, CH), F32, None),
    ]
    return pl.pallas_call(
        forward_kernel,
        grid_spec=pltpu.PrefetchScalarGridSpec(
            num_scalar_prefetch=1,
            grid=(ROWS // BLK,),
            in_specs=[
                full((SLOTS * GRAN, 128)),
                pl.BlockSpec((BLK, CH), lambda i, sc: (i, 0)),
                full((128, CH)), full((1, CH)), full((1, CH)), full((3 * CH, CH)),
            ],
            out_specs=[full(s) if b is None else b for s, _d, b in shapes],
            scratch_shapes=[
                pltpu.VMEM((ROWS + GRAN, 128), F32),
                pltpu.VMEM((ROWS, 128), F32),
                pltpu.VMEM((ROWS + 16, 256), BF16),
                pltpu.VMEM((256, 2 * CH), BF16),
                pltpu.VMEM((CH, 3 * CH), F32),
            ],
        ),
        out_shape=[jax.ShapeDtypeStruct(s, d) for s, d, _b in shapes],
        compiler_params=pltpu.CompilerParams(vmem_limit_bytes=50 * 2**20),
        cost_estimate=pl.CostEstimate(flops=8 * 10**9, bytes_accessed=20 * 10**6, transcendentals=0),
        name="forward_window",
    )(sc, u, cot, wst, gain, bias, w2)


def backward(sc, lg, sl, xs, wt, wst, gain, nst, tc, im):
    return pl.pallas_call(
        backward_kernel,
        grid_spec=pltpu.PrefetchScalarGridSpec(
            num_scalar_prefetch=1,
            grid=(ROWS // BLK,),
            in_specs=[
                pl.BlockSpec((BLK, CH), lambda i, sc: (i, 0)),
                pl.BlockSpec((2, BLK, CH), lambda i, sc: (0, i, 0)),
                pl.BlockSpec((2, BLK, 128), lambda i, sc: (0, i, 0)),
                full((CH, 3 * CH)), full((128, CH)), full((1, CH)),
                full((128, CH)), full((128, 128)), full((8, CH)),
            ],
            out_specs=full((16, CH)),
            scratch_shapes=[pltpu.VMEM((128, CH), F32), pltpu.VMEM((8, CH), F32)],
        ),
        out_shape=jax.ShapeDtypeStruct((16, CH), F32),
        compiler_params=pltpu.CompilerParams(vmem_limit_bytes=40 * 2**20),
        cost_estimate=pl.CostEstimate(flops=5 * 10**9, bytes_accessed=14 * 10**6, transcendentals=0),
        name="backward_window",
    )(sc, lg, sl, xs, wt, wst, gain, nst, tc, im)


def swap(value, axis, bit):
    count = 8 if axis == "bulk" else 32
    return lax.ppermute(value, axis, [(i, i ^ bit) for i in range(count)])


def route(rows, sizes, masks):
    units = sizes // TAPS
    extra = jnp.stack([(units // 32).astype(BF16), (units % 32).astype(BF16)], axis=1)
    value = jnp.concatenate([rows, jnp.pad(extra, ((0, 0), (0, 126)))], axis=1)
    for bit in (1, 2, 4, 8, 16):
        moved = swap(value, "wide", bit)
        value = jnp.where(((masks & bit) != 0)[:, None], moved, value)
    tail = value[:, -128:-126].astype(F32)
    return value[:, :-128], (tail[:, 0] * 32.0 + tail[:, 1]).astype(jnp.int32)


def window_inputs(conv_first):
    w = conv_first.astype(F32)
    even = jnp.pad(w, ((0, 6), (0, 0)))
    odd = jnp.pad(w, ((5, 1), (0, 0)))
    return jnp.tile(jnp.concatenate([even, odd], axis=0), (SLOTS, 1))


def halve(pair, bit, axis, dtype, mask):
    low, high = pair
    flag = bit == 1
    mine = jnp.where(flag, high, low)
    other = jnp.where(flag, low, high).astype(dtype)
    return mine + swap(other, axis, mask).astype(F32)


def local(rows, units, sources, core, cot, conv_first, norm_gain, norm_bias, conv_second):
    u = jnp.pad(rows.reshape(SLOTS * GRAN, TAPS).astype(F32), ((0, 0), (0, 128 - TAPS)))
    sc = jnp.concatenate([units, sources, jnp.full((8,), core, jnp.int32)])
    wst = window_inputs(conv_first)
    gain, bias = norm_gain[None, :], norm_bias[None, :]
    lg, sl, keep, send, xs, nst, tc, im = forward(sc, u, cot, wst, gain, bias, conv_second)
    small = backward(sc, lg, sl, xs, conv_second.T, wst, gain, nst, tc, im)
    return keep, send, small


def per_device(waveforms, owner_of, lengths, cotangent, conv_first, norm_gain, norm_bias, conv_second):
    me = lax.axis_index("wide")
    place = lax.axis_index("bulk")
    masks = jnp.bitwise_xor(owner_of[0], me)
    rows, units = route(waveforms[0], lengths[0], masks)
    keep, send, small = local(
        rows, units, jnp.bitwise_xor(masks, me), place % 2, cotangent[0, 0],
        conv_first, norm_gain, norm_bias, conv_second,
    )
    total = keep + swap(send, "bulk", 1).astype(F32)

    x, y, z = place // 2, me // 8, me % 8
    t = total.reshape(2, 2, 64, 3 * CH)
    t = halve((t[:, 0], t[:, 1]), x % 2, "bulk", BF16, 2)
    q = [t[:, :, 384 * k : 384 * (k + 1)] for k in range(4)]
    t = halve(
        (jnp.stack([q[0], q[2]]), jnp.stack([q[1], q[3]])), y % 2, "wide", BF16, 8
    )
    t = halve((t[:, 0], t[:, 1]), x // 2, "bulk", BF16, 4)
    t = halve((t[0], t[1]), y // 2, "wide", F32, 16)
    t = t.T.reshape(8, 48, 64)
    t = t.reshape(4, 2, 48, 64)
    t = halve((t[:, 0], t[:, 1]), z % 2, "wide", F32, 1)
    t = t.reshape(2, 2, 48, 64)
    t = halve((t[:, 0], t[:, 1]), (z // 2) % 2, "wide", F32, 2)
    grad_second = halve((t[0], t[1]), z // 4, "wide", F32, 4)

    for axis, mask in (("bulk", 1), ("bulk", 2), ("bulk", 4), ("wide", 1), ("wide", 2), ("wide", 4), ("wide", 8), ("wide", 16)):
        small = small + swap(small, axis, mask)
    return (grad_second, small[:10], small[10], small[11])


def solution(mesh):
    placed = (
        P("bulk", "wide", None),
        P("bulk", "wide"),
        P("bulk", "wide"),
        P("bulk", "wide", None, None),
        P(),
        P(),
        P(),
        P(),
    )
    return jax.shard_map(
        per_device,
        mesh=mesh,
        in_specs=placed,
        out_specs=(P("wide", "bulk"), P(), P(), P()),
        check_vma=False,
    )
```

time: 527 us -> 160 us (0.30); the launches traced: 518 us -> 159 us
  waiting for transfers between devices: 198 us -> 45 us
  local copies, waits for them, and re-layouts: 116 us -> 13.8 us
  blocking collectives: 98.2 us -> 0 us
  matrix products: 68.4 us -> 0 us
  starting transfers between devices: 0.53 us -> 52.4 us
  Pallas kernels: 0 us -> 35.6 us
  between operations: 22.7 us -> 0.93 us
    reduce_scatter x1 -> x0, waiting for transfers between devices: 146 us -> none  [per_device(): lax.psum_scatter(lax.dot_general(late_taps, late_grad, (((0,), (0,)), (()...]
    psum x1 -> x0, blocking collectives: 75.3 us -> none  [per_device(): lax.psum((grad_first, grad_gain, grad_bias), ('wide', 'bulk'))]
    dot_general x15 -> x0, matrix products: 68.4 us -> none  [the longest x1 12.4 us: owner_terms(): jnp.dot(member.T, cross_mean, precision=highest)]
    slice x11 -> x2, local copies, waits for them, and re-layouts: 68.4 us -> 0.62 us  [the longest x1 0.59 us: per_device(): return (grad_second, small[:10], small[10], small[11])]
    ppermute x0 -> x21, starting transfers between devices: none -> 52.4 us  [swap(): return lax.ppermute(value, axis, [(i, i ^ bit) for i in range(count)])]
    all_gather x1 -> x0, waiting for transfers between devices: 51.5 us -> none  [per_device(): gathered = lax.all_gather(waveforms[0], 'wide', axis=0, tiled=True)]
    ppermute x0 -> x21, waiting for transfers between devices: none -> 45 us  [swap(): return lax.ppermute(value, axis, [(i, i ^ bit) for i in range(count)])]
    pallas_call x0 -> x2, Pallas kernels: none -> 35.6 us  [the longest x1 27.9 us: forward(): pl.pallas_call(forward_kernel, grid_spec=pltpu.PrefetchScalarGridSpec(num...]
  transfers between devices with their start and end apart: 3 -> 21, of which waited for: 2 -> 17; matrix products, arithmetic and copies ran while one was open for 15% -> 3% of each run, Pallas kernels for 0% -> 5%
where the time goes in v1:
time: 160 us; the launch traced here: 159 us
  starting transfers between devices  52.4 us (33%)
  waiting for transfers between devices  45 us (28%)
  Pallas kernels  35.6 us (22%)
  local copies, waits for them, and re-layouts  13.8 us (9%)
  other arithmetic  11.3 us (7%)
    ppermute x21, starting transfers between devices, swap(): return lax.ppermute(value, axis, [(i, i ^ bit) for i in range(count)])  52.4 us
    ppermute x21, waiting for transfers between devices, swap(): return lax.ppermute(value, axis, [(i, i ^ bit) for i in range(count)])  45 us
    pallas_call x1, Pallas kernels, forward(): pl.pallas_call(forward_kernel, grid_spec=pltpu.PrefetchScalarGridSpec(num...  27.9 us
    unnamed x18, local copies, waits for them, and re-layouts  10.2 us
    pallas_call x1, Pallas kernels, backward(): pl.pallas_call(backward_kernel, grid_spec=pltpu.PrefetchScalarGridSpec(nu...  7.75 us
    add x6, other arithmetic, halve(): return mine + swap(other, axis, mask).astype(F32)  3.22 us
  transfers between devices with their start and end apart: 21, of which 17 were waited for; matrix products, arithmetic and copies ran while one was open for 3% of the time, Pallas kernels for 5%

profile of v1, /device:TPU:32, one launch (start us, length us, event | category | flops | bytes accessed | tf_op | source)
XLA Modules:
  0.0 159.0 jit_solution(11318616403034311137)
XLA Ops:
  7.9 3.4 %collective-permute-start.1 = (bf16[4,10368]{1,0:T(4,128)(2,1)S(1)}, bf16[4,10368]{1,0:T(4,128)(2,1)S(1)}, u32[]{:S(2)}, u32[]{:S(2)}) collective-permute-start(bf16[4,10368]{1,0:T(4,128)(2,1)S(1)} %broadcast_select_fusion.1), channel_id=1, source_target_pairs={{0,16},{8,24},{16,0},{24,8},{32,48},{40,56},{48,32},{56,40},{64,80... | collective-permute-start | bytes 248840 | tf_op jit(solution)/shard_map/ppermute | solution.py:316
  11.3 2.5 %collective-permute-done.1 = bf16[4,10368]{1,0:T(4,128)(2,1)S(1)} collective-permute-done((bf16[4,10368]{1,0:T(4,128)(2,1)S(1)}, bf16[4,10368]{1,0:T(4,128)(2,1)S(1)}, u32[]{:S(2)}, u32[]{:S(2)}) %collective-permute-start.1) | collective-permute-done | bytes 82976 | tf_op jit(solution)/shard_map/ppermute | solution.py:316
  13.9 6.0 %collective-permute-start.2 = (bf16[4,10368]{1,0:T(4,128)(2,1)S(1)}, bf16[4,10368]{1,0:T(4,128)(2,1)S(1)}, u32[]{:S(2)}, u32[]{:S(2)}) collective-permute-start(bf16[4,10368]{1,0:T(4,128)(2,1)S(1)} %broadcast_select_fusion.2), channel_id=1, source_target_pairs={{0,32},{8,40},{16,48},{24,56},{32,0},{40,8},{48,16},{56,24},{64,96... | collective-permute-start | bytes 248840 | tf_op jit(solution)/shard_map/ppermute | solution.py:316
  19.9 2.7 %collective-permute-done.2 = bf16[4,10368]{1,0:T(4,128)(2,1)S(1)} collective-permute-done((bf16[4,10368]{1,0:T(4,128)(2,1)S(1)}, bf16[4,10368]{1,0:T(4,128)(2,1)S(1)}, u32[]{:S(2)}, u32[]{:S(2)}) %collective-permute-start.2) | collective-permute-done | bytes 82976 | tf_op jit(solution)/shard_map/ppermute | solution.py:316
  27.4 3.8 %collective-permute-start.4 = (bf16[4,10368]{1,0:T(4,128)(2,1)S(1)}, bf16[4,10368]{1,0:T(4,128)(2,1)S(1)}, u32[]{:S(2)}, u32[]{:S(2)}) collective-permute-start(bf16[4,10368]{1,0:T(4,128)(2,1)S(1)} %broadcast_select_fusion.4), channel_id=1, source_target_pairs={{0,128},{8,136},{16,144},{24,152},{32,160},{40,168},{48,176},{56,1... | collective-permute-start | bytes 248840 | tf_op jit(solution)/shard_map/ppermute | solution.py:316
  31.3 2.4 %collective-permute-done.4 = bf16[4,10368]{1,0:T(4,128)(2,1)S(1)} collective-permute-done((bf16[4,10368]{1,0:T(4,128)(2,1)S(1)}, bf16[4,10368]{1,0:T(4,128)(2,1)S(1)}, u32[]{:S(2)}, u32[]{:S(2)}) %collective-permute-start.4) | collective-permute-done | bytes 82976 | tf_op jit(solution)/shard_map/ppermute | solution.py:316
  33.8 2.4 %convert_element_type.76 = bf16[4096,10]{1,0:T(8,128)(2,1)S(1)} reshape(bf16[4,10240]{1,0:T(4,128)(2,1)S(1)} %slice.93) | data formatting | bytes 163840 | tf_op jit(solution)/shard_map/convert_element_type | solution.py:346
  38.1 27.9 %forward_window.1 = (bf16[2048,512]{1,0:T(8,128)(2,1)}, f32[2,2048,512]{2,1,0:T(8,128)}, f32[4,64,1536]{2,1,0:T(8,128)S(1)}, bf16[4,64,1536]{2,1,0:T(8,128)(2,1)...) custom-call(s32[16]{0:T(128)S(1)} %pad_add_fusion.sc, ...), custom_call_target="tpu_custom_call" | custom-call | flops 8000000000 | bytes 20000000 | tf_op jit(solution)/shard_map/forward_window/pallas_call | solution.py:265
  67.0 2.4 %collective-permute-done.5 = bf16[4,64,1536]{2,1,0:T(8,128)(2,1)} collective-permute-done((bf16[4,64,1536]{2,1,0:T(8,128)(2,1)S(1)}, bf16[4,64,1536]{2,1,0:T(8,128)(2,1)}, u32[]{:S(2)}, u32[]{:S(2)}) %collective-permute-start.5) | collective-permute-done | bytes 786464 | tf_op jit(solution)/shard_map/ppermute | solution.py:316
  73.7 9.7 %collective-permute-done.6 = bf16[2,64,1536]{2,1,0:T(8,128)(2,1)S(1)} collective-permute-done((bf16[2,64,1536]{2,1,0:T(8,128)(2,1)S(1)}, bf16[2,64,1536]{2,1,0:T(8,128)(2,1)S(1)}, u32[]{:S(2)}, u32[]{:S(2)}) %collective-permute-start.6) | collective-permute-done | bytes 393248 | tf_op jit(solution)/shard_map/ppermute | solution.py:316
  88.4 2.9 %collective-permute-done.7 = bf16[2,2,64,384]{3,2,0,1:T(8,128)(2,1)} collective-permute-done((bf16[2,2,64,384]{3,2,0,1:T(8,128)(2,1)S(1)}, bf16[2,2,64,384]{3,2,0,1:T(8,128)(2,1)}, u32[]{:S(2)}, u32[]{:S(2)}) %collective-permute-start.7) | collective-permute-done | bytes 196640 | tf_op jit(solution)/shard_map/ppermute | solution.py:316
  92.4 3.1 %collective-permute-start.8 = (bf16[2,64,384]{2,1,0:T(8,128)(2,1)S(1)}, bf16[2,64,384]{2,1,0:T(8,128)(2,1)S(1)}, u32[]{:S(2)}, u32[]{:S(2)}) collective-permute-start(bf16[2,64,384]{2,1,0:T(8,128)(2,1)S(1)} %fusion.2), channel_id=1, source_target_pairs={{0,4},{1,5},{2,6},{3,7},{4,0},{5,1},{6,2},{7,3},{8,12},{9,13},{10,... | collective-permute-start | bytes 294920 | tf_op jit(solution)/shard_map/ppermute | solution.py:316
  95.5 3.4 %copy-done.2 = f32[2,2048,512]{2,1,0:T(8,128)S(1)} copy-done((f32[2,2048,512]{2,1,0:T(8,128)S(1)}, f32[2,2048,512]{2,1,0:T(8,128)}, u32[]{:S(2)}) %copy-start.2) | copy-done | bytes 8388632
  101.7 7.7 %backward_window.1 = f32[16,512]{1,0:T(8,128)S(1)} custom-call(s32[16]{0:T(128)S(1)} %pad_add_fusion.sc, bf16[2048,512]{1,0:T(8,128)(2,1)S(1)} %copy-done.3, f32[2,2048,512]{2,1,0:T(8,128)S(1)} %copy-done.2, bf16[2,2048,128]{2,1,0:T(8,128)(2,1)S(1)} %copy-done.5, bf16[512,1536]{1,0:T(8,128)(2,1)S(1)} %bitcast.106, f32[128,512]{1,0:T(8,128)S(1)} %bitcast.108, ...), custom_call_target="tpu_custom_call" | custom-call | flops 5000000000 | bytes 14000000 | tf_op jit(solution)/shard_map/backward_window/pallas_call | solution.py:292
  111.3 3.3 %collective-permute-done.14 = f32[16,512]{1,0:T(8,128)S(1)} collective-permute-done((f32[16,512]{1,0:T(8,128)S(1)}, f32[16,512]{1,0:T(8,128)S(1)}, u32[]{:S(2)}, u32[]{:S(2)}) %collective-permute-start.14) | collective-permute-done | bytes 32800 | tf_op jit(solution)/shard_map/ppermute | solution.py:316
  115.3 3.6 %collective-permute-start.9 = (f32[64,384]{1,0:T(8,128)S(1)}, f32[64,384]{1,0:T(8,128)S(1)}, u32[]{:S(2)}, u32[]{:S(2)}) collective-permute-start(f32[64,384]{1,0:T(8,128)S(1)} %select_bitcast_fusion), channel_id=1, source_target_pairs={{0,128},{8,136},{16,144},{24,152},{32,160},{40,168},{48,176},{56,1... | collective-permute-start | bytes 294920 | tf_op jit(solution)/shard_map/ppermute | solution.py:316
  120.1 2.9 %collective-permute-start.16 = (f32[16,512]{1,0:T(8,128)S(1)}, f32[16,512]{1,0:T(8,128)S(1)}, u32[]{:S(2)}, u32[]{:S(2)}) collective-permute-start(f32[16,512]{1,0:T(8,128)S(1)} %add.136), channel_id=1, source_target_pairs={{0,8},{8,0},{16,24},{24,16},{32,40},{40,32},{48,56},{56,48},{64,72... | collective-permute-start | bytes 98312 | tf_op jit(solution)/shard_map/ppermute | solution.py:316
  127.1 2.6 %collective-permute-done.17 = f32[16,512]{1,0:T(8,128)S(1)} collective-permute-done((f32[16,512]{1,0:T(8,128)S(1)}, f32[16,512]{1,0:T(8,128)S(1)}, u32[]{:S(2)}, u32[]{:S(2)}) %collective-permute-start.17) | collective-permute-done | bytes 32800 | tf_op jit(solution)/shard_map/ppermute | solution.py:316
  129.7 4.8 %collective-permute-start.18 = (f32[16,512]{1,0:T(8,128)S(1)}, f32[16,512]{1,0:T(8,128)S(1)}, u32[]{:S(2)}, u32[]{:S(2)}) collective-permute-start(f32[16,512]{1,0:T(8,128)S(1)} %add.138), channel_id=1, source_target_pairs={{0,32},{8,40},{16,48},{24,56},{32,0},{40,8},{48,16},{56,24},{64,96... | collective-permute-start | bytes 98312 | tf_op jit(solution)/shard_map/ppermute | solution.py:316
  141.5 3.6 %collective-permute-start.20 = (f32[16,512]{1,0:T(8,128)S(1)}, f32[16,512]{1,0:T(8,128)S(1)}, u32[]{:S(2)}, u32[]{:S(2)}) collective-permute-start(f32[16,512]{1,0:T(8,128)S(1)} %add.140), channel_id=1, source_target_pairs={{0,128},{8,136},{16,144},{24,152},{32,160},{40,168},{48,176},{56,1... | collective-permute-start | bytes 98312 | tf_op jit(solution)/shard_map/ppermute | solution.py:316
  145.2 2.2 %collective-permute-start.11 = (f32[2,48,64]{2,1,0:T(8,128)S(1)}, f32[2,48,64]{2,1,0:T(8,128)S(1)}, u32[]{:S(2)}, u32[]{:S(2)}) collective-permute-start(f32[2,48,64]{2,1,0:T(8,128)S(1)} %select_bitcast_fusion.1), channel_id=1, source_target_pairs={{0,16},{8,24},{16,0},{24,8},{32,48},{40,56},{48,32},{56,40},{64,80... | collective-permute-start | bytes 73736 | tf_op jit(solution)/shard_map/ppermute | solution.py:316
  147.4 3.1 %collective-permute-done.11 = f32[2,48,64]{2,1,0:T(8,128)S(1)} collective-permute-done((f32[2,48,64]{2,1,0:T(8,128)S(1)}, f32[2,48,64]{2,1,0:T(8,128)S(1)}, u32[]{:S(2)}, u32[]{:S(2)}) %collective-permute-start.11) | collective-permute-done | bytes 24608 | tf_op jit(solution)/shard_map/ppermute | solution.py:316
  150.6 4.6 %collective-permute-start.12 = (f32[48,64]{1,0:T(8,128)S(1)}, f32[48,64]{1,0:T(8,128)S(1)}, u32[]{:S(2)}, u32[]{:S(2)}) collective-permute-start(f32[48,64]{1,0:T(8,128)S(1)} %select_bitcast_fusion.2), channel_id=1, source_target_pairs={{0,32},{8,40},{16,48},{24,56},{32,0},{40,8},{48,16},{56,24},{64,96... | collective-permute-start | bytes 36872 | tf_op jit(solution)/shard_map/ppermute | solution.py:316
  155.8 2.7 %collective-permute-done.12 = f32[48,64]{1,0:T(8,128)S(1)} collective-permute-done((f32[48,64]{1,0:T(8,128)S(1)}, f32[48,64]{1,0:T(8,128)S(1)}, u32[]{:S(2)}, u32[]{:S(2)}) %collective-permute-start.12) | collective-permute-done | bytes 12320 | tf_op jit(solution)/shard_map/ppermute | solution.py:316
  (87 shorter events, 44.3 us)
Async XLA Ops:
  2.4 4.5 %collective-permute-start = (bf16[4,10368]{1,0:T(4,128)(2,1)S(1)}, bf16[4,10368]{1,0:T(4,128)(2,1)S(1)}, u32[]{:S(2)}, u32[]{:S(2)}) collective-permute-start(bf16[4,10368]{1,0:T(4,128)(2,1)S(1)} %fusion.4), channel_id=1, source_target_pairs={{0,8},{8,0},{16,24},{24,16},{32,40},{40,32},{48,56},{56,48},{64,72... | collective-permute-start | bytes 248840 | tf_op jit(solution)/shard_map/ppermute | solution.py:316
  7.9 5.9 %collective-permute-start.1 = (bf16[4,10368]{1,0:T(4,128)(2,1)S(1)}, bf16[4,10368]{1,0:T(4,128)(2,1)S(1)}, u32[]{:S(2)}, u32[]{:S(2)}) collective-permute-start(bf16[4,10368]{1,0:T(4,128)(2,1)S(1)} %broadcast_select_fusion.1), channel_id=1, source_target_pairs={{0,16},{8,24},{16,0},{24,8},{32,48},{40,56},{48,32},{56,40},{64,80... | collective-permute-start | bytes 248840 | tf_op jit(solution)/shard_map/ppermute | solution.py:316
  13.9 8.8 %collective-permute-start.2 = (bf16[4,10368]{1,0:T(4,128)(2,1)S(1)}, bf16[4,10368]{1,0:T(4,128)(2,1)S(1)}, u32[]{:S(2)}, u32[]{:S(2)}) collective-permute-start(bf16[4,10368]{1,0:T(4,128)(2,1)S(1)} %broadcast_select_fusion.2), channel_id=1, source_target_pairs={{0,32},{8,40},{16,48},{24,56},{32,0},{40,8},{48,16},{56,24},{64,96... | collective-permute-start | bytes 248840 | tf_op jit(solution)/shard_map/ppermute | solution.py:316
  22.8 4.5 %collective-permute-start.3 = (bf16[4,10368]{1,0:T(4,128)(2,1)S(1)}, bf16[4,10368]{1,0:T(4,128)(2,1)S(1)}, u32[]{:S(2)}, u32[]{:S(2)}) collective-permute-start(bf16[4,10368]{1,0:T(4,128)(2,1)S(1)} %broadcast_select_fusion.3), channel_id=1, source_target_pairs={{0,64},{8,72},{16,80},{24,88},{32,96},{40,104},{48,112},{56,120},{... | collective-permute-start | bytes 248840 | tf_op jit(solution)/shard_map/ppermute | solution.py:316
  27.4 6.2 %collective-permute-start.4 = (bf16[4,10368]{1,0:T(4,128)(2,1)S(1)}, bf16[4,10368]{1,0:T(4,128)(2,1)S(1)}, u32[]{:S(2)}, u32[]{:S(2)}) collective-permute-start(bf16[4,10368]{1,0:T(4,128)(2,1)S(1)} %broadcast_select_fusion.4), channel_id=1, source_target_pairs={{0,128},{8,136},{16,144},{24,152},{32,160},{40,168},{48,176},{56,1... | collective-permute-start | bytes 248840 | tf_op jit(solution)/shard_map/ppermute | solution.py:316
  36.2 1.8 %copy-start = (f32[512]{0:T(512)S(1)}, f32[512]{0:T(512)}, u32[]{:S(2)}) copy-start(f32[512]{0:T(512)} %param.14) | copy-start | bytes 6148
  67.0 2.4 %collective-permute-start.5 = (bf16[4,64,1536]{2,1,0:T(8,128)(2,1)S(1)}, bf16[4,64,1536]{2,1,0:T(8,128)(2,1)}, u32[]{:S(2)}, u32[]{:S(2)}) collective-permute-start(bf16[4,64,1536]{2,1,0:T(8,128)(2,1)S(1)} %get-tuple-element.13), channel_id=1, source_target_pairs={{0,1},{1,0},{2,3},{3,2},{4,5},{5,4},{6,7},{7,6},{8,9},{9,8},{10,11... | collective-permute-start | bytes 2359304 | tf_op jit(solution)/shard_map/ppermute | solution.py:316
  71.9 11.4 %collective-permute-start.6 = (bf16[2,64,1536]{2,1,0:T(8,128)(2,1)S(1)}, bf16[2,64,1536]{2,1,0:T(8,128)(2,1)S(1)}, u32[]{:S(2)}, u32[]{:S(2)}) collective-permute-start(bf16[2,64,1536]{2,1,0:T(8,128)(2,1)S(1)} %fusion), channel_id=1, source_target_pairs={{0,2},{1,3},{2,0},{3,1},{4,6},{5,7},{6,4},{7,5},{8,10},{9,11},{10,... | collective-permute-start | bytes 1179656 | tf_op jit(solution)/shard_map/ppermute | solution.py:316
  85.0 6.3 %collective-permute-start.7 = (bf16[2,2,64,384]{3,2,0,1:T(8,128)(2,1)S(1)}, bf16[2,2,64,384]{3,2,0,1:T(8,128)(2,1)}, u32[]{:S(2)}, u32[]{:S(2)}) collective-permute-start(bf16[2,2,64,384]{3,2,0,1:T(8,128)(2,1)S(1)} %select_convert_fusion.1), channel_id=1, source_target_pairs={{0,64},{8,72},{16,80},{24,88},{32,96},{40,104},{48,112},{56,120},{... | collective-permute-start | bytes 589832 | tf_op jit(solution)/shard_map/ppermute | solution.py:316
  92.4 22.9 %collective-permute-start.8 = (bf16[2,64,384]{2,1,0:T(8,128)(2,1)S(1)}, bf16[2,64,384]{2,1,0:T(8,128)(2,1)S(1)}, u32[]{:S(2)}, u32[]{:S(2)}) collective-permute-start(bf16[2,64,384]{2,1,0:T(8,128)(2,1)S(1)} %fusion.2), channel_id=1, source_target_pairs={{0,4},{1,5},{2,6},{3,7},{4,0},{5,1},{6,2},{7,3},{8,12},{9,13},{10,... | collective-permute-start | bytes 294920 | tf_op jit(solution)/shard_map/ppermute | solution.py:316
  95.5 3.4 %copy-start.2 = (f32[2,2048,512]{2,1,0:T(8,128)S(1)}, f32[2,2048,512]{2,1,0:T(8,128)}, u32[]{:S(2)}) copy-start(f32[2,2048,512]{2,1,0:T(8,128)} %get-tuple-element.15.sl) | copy-start | bytes 25165828
  109.4 1.3 collective-permute-start.13
  110.7 3.9 %collective-permute-start.14 = (f32[16,512]{1,0:T(8,128)S(1)}, f32[16,512]{1,0:T(8,128)S(1)}, u32[]{:S(2)}, u32[]{:S(2)}) collective-permute-start(f32[16,512]{1,0:T(8,128)S(1)} %add.134), channel_id=1, source_target_pairs={{0,2},{1,3},{2,0},{3,1},{4,6},{5,7},{6,4},{7,5},{8,10},{9,11},{10,... | collective-permute-start | bytes 98312 | tf_op jit(solution)/shard_map/ppermute | solution.py:316
  114.6 5.4 %collective-permute-start.15 = (f32[16,512]{1,0:T(8,128)S(1)}, f32[16,512]{1,0:T(8,128)S(1)}, u32[]{:S(2)}, u32[]{:S(2)}) collective-permute-start(f32[16,512]{1,0:T(8,128)S(1)} %add.135), channel_id=1, source_target_pairs={{0,4},{1,5},{2,6},{3,7},{4,0},{5,1},{6,2},{7,3},{8,12},{9,13},{10,... | collective-permute-start | bytes 98312 | tf_op jit(solution)/shard_map/ppermute | solution.py:316
  115.3 19.3 %collective-permute-start.9 = (f32[64,384]{1,0:T(8,128)S(1)}, f32[64,384]{1,0:T(8,128)S(1)}, u32[]{:S(2)}, u32[]{:S(2)}) collective-permute-start(f32[64,384]{1,0:T(8,128)S(1)} %select_bitcast_fusion), channel_id=1, source_target_pairs={{0,128},{8,136},{16,144},{24,152},{32,160},{40,168},{48,176},{56,1... | collective-permute-start | bytes 294920 | tf_op jit(solution)/shard_map/ppermute | solution.py:316
  120.1 4.8 %collective-permute-start.16 = (f32[16,512]{1,0:T(8,128)S(1)}, f32[16,512]{1,0:T(8,128)S(1)}, u32[]{:S(2)}, u32[]{:S(2)}) collective-permute-start(f32[16,512]{1,0:T(8,128)S(1)} %add.136), channel_id=1, source_target_pairs={{0,8},{8,0},{16,24},{24,16},{32,40},{40,32},{48,56},{56,48},{64,72... | collective-permute-start | bytes 98312 | tf_op jit(solution)/shard_map/ppermute | solution.py:316
  124.9 4.8 %collective-permute-start.17 = (f32[16,512]{1,0:T(8,128)S(1)}, f32[16,512]{1,0:T(8,128)S(1)}, u32[]{:S(2)}, u32[]{:S(2)}) collective-permute-start(f32[16,512]{1,0:T(8,128)S(1)} %add.137), channel_id=1, source_target_pairs={{0,16},{8,24},{16,0},{24,8},{32,48},{40,56},{48,32},{56,40},{64,80... | collective-permute-start | bytes 98312 | tf_op jit(solution)/shard_map/ppermute | solution.py:316
  129.7 7.8 %collective-permute-start.18 = (f32[16,512]{1,0:T(8,128)S(1)}, f32[16,512]{1,0:T(8,128)S(1)}, u32[]{:S(2)}, u32[]{:S(2)}) collective-permute-start(f32[16,512]{1,0:T(8,128)S(1)} %add.138), channel_id=1, source_target_pairs={{0,32},{8,40},{16,48},{24,56},{32,0},{40,8},{48,16},{56,24},{64,96... | collective-permute-start | bytes 98312 | tf_op jit(solution)/shard_map/ppermute | solution.py:316
  135.2 9.8 %collective-permute-start.10 = (f32[4,48,64]{1,0,2:T(4,128)S(1)}, f32[4,48,64]{1,0,2:T(4,128)S(1)}, u32[]{:S(2)}, u32[]{:S(2)}) collective-permute-start(f32[4,48,64]{1,0,2:T(4,128)S(1)} %bitcast.120), channel_id=1, source_target_pairs={{0,8},{8,0},{16,24},{24,16},{32,40},{40,32},{48,56},{56,48},{64,72... | collective-permute-start | bytes 147464 | tf_op jit(solution)/shard_map/ppermute | solution.py:316
  137.5 3.9 %collective-permute-start.19 = (f32[16,512]{1,0:T(8,128)S(1)}, f32[16,512]{1,0:T(8,128)S(1)}, u32[]{:S(2)}, u32[]{:S(2)}) collective-permute-start(f32[16,512]{1,0:T(8,128)S(1)} %add.139), channel_id=1, source_target_pairs={{0,64},{8,72},{16,80},{24,88},{32,96},{40,104},{48,112},{56,120},{... | collective-permute-start | bytes 98312 | tf_op jit(solution)/shard_map/ppermute | solution.py:316
  141.5 6.0 %collective-permute-start.20 = (f32[16,512]{1,0:T(8,128)S(1)}, f32[16,512]{1,0:T(8,128)S(1)}, u32[]{:S(2)}, u32[]{:S(2)}) collective-permute-start(f32[16,512]{1,0:T(8,128)S(1)} %add.140), channel_id=1, source_target_pairs={{0,128},{8,136},{16,144},{24,152},{32,160},{40,168},{48,176},{56,1... | collective-permute-start | bytes 98312 | tf_op jit(solution)/shard_map/ppermute | solution.py:316
  145.2 5.4 %collective-permute-start.11 = (f32[2,48,64]{2,1,0:T(8,128)S(1)}, f32[2,48,64]{2,1,0:T(8,128)S(1)}, u32[]{:S(2)}, u32[]{:S(2)}) collective-permute-start(f32[2,48,64]{2,1,0:T(8,128)S(1)} %select_bitcast_fusion.1), channel_id=1, source_target_pairs={{0,16},{8,24},{16,0},{24,8},{32,48},{40,56},{48,32},{56,40},{64,80... | collective-permute-start | bytes 73736 | tf_op jit(solution)/shard_map/ppermute | solution.py:316
  147.4 11.6 %copy-start.7 = (f32[16,512]{1,0:T(8,128)}, f32[16,512]{1,0:T(8,128)S(1)}, u32[]{:S(2)}) copy-start(f32[16,512]{1,0:T(8,128)S(1)} %add.141) | copy-start | bytes 98308
  150.6 7.8 %collective-permute-start.12 = (f32[48,64]{1,0:T(8,128)S(1)}, f32[48,64]{1,0:T(8,128)S(1)}, u32[]{:S(2)}, u32[]{:S(2)}) collective-permute-start(f32[48,64]{1,0:T(8,128)S(1)} %select_bitcast_fusion.2), channel_id=1, source_target_pairs={{0,32},{8,40},{16,48},{24,56},{32,0},{40,8},{48,16},{56,24},{64,96... | collective-permute-start | bytes 36872 | tf_op jit(solution)/shard_map/ppermute | solution.py:316
  (5 other events, 6.8 us)

commit v2 on v1

--- a/solution.py
+++ b/solution.py
@@ -16,6 +16,7 @@
 ROWS = 2048
 CH = 512
 BLK = 256
+BLOCKS = [(2 * xh + xl, 2 * yh + yl) for xl in range(2) for yl in range(2) for xh in range(2) for yh in range(2)]
 
 
 def dot(a, b, precision=None):
@@ -70,19 +71,20 @@
     return out
 
 
-def forward_kernel(
-    sc, u, cot, wst, gain, bias, w2,
-    lg, sl, keep, send, xs, nst, tc, im,
-    buf, xd, xbig, wbig, acc,
+def window_kernel(
+    sc, u, cot, wst, gain, bias, w2, wt,
+    keep, send, small,
+    buf, xd, xbig, xs, wbig, acc, nst, tc, im, grads, carry,
 ):
     step = pl.program_id(0)
     segs = plan(sc)
 
     @pl.when(step == 0)
     def _():
-        buf[pl.ds(ROWS, 8), :] = jnp.zeros((8, 128), F32)
+        buf[...] = jnp.zeros_like(buf)
         for slot, off, _n in segs:
-            buf[pl.ds(off, GRAN), :] = u[pl.ds(pl.multiple_of(slot * GRAN, GRAN), GRAN), :]
+            piece = u[pl.ds(pl.multiple_of(slot * GRAN, GRAN), GRAN), :].astype(F32)
+            buf[pl.ds(off, GRAN), 0:TAPS] = piece
         src = lax.broadcasted_iota(jnp.int32, (128, 256), 0)
         tap = lax.broadcasted_iota(jnp.int32, (128, 256), 1) % 16
         r0 = ((tap == src) & (src < TAPS)).astype(F32).astype(BF16)
@@ -166,6 +168,8 @@
                 wbig[64 * s + 32 : 64 * s + 48, cols] = f.astype(BF16)
                 wbig[64 * s + 48 : 64 * s + 64, cols] = jnp.zeros((16, CH), BF16)
         acc[...] = jnp.zeros_like(acc)
+        grads[...] = jnp.zeros_like(grads)
+        carry[...] = jnp.zeros_like(carry)
 
     base = pl.multiple_of(step * BLK, BLK)
     pre_e = dot(xbig[pl.ds(base, BLK + 16), :], wbig[:, :CH])
@@ -173,8 +177,6 @@
     c_e, s_e = cdf_slope(pre_e)
     act_e = pre_e * c_e
     c_o, s_o = cdf_slope(pre_o)
-    sl[0] = s_e[:BLK]
-    sl[1] = s_o
     taps = jnp.concatenate(
         [act_e[:BLK].astype(BF16), (pre_o * c_o).astype(BF16), act_e[1 : BLK + 1].astype(BF16)], axis=1
     )
@@ -185,51 +187,31 @@
     for _s, off, n in segs[1:]:
         drop = drop | (row == off + n - 1)
     grad = jnp.where(drop, 0.0, cot[...].astype(F32) * slope).astype(BF16)
-    lg[...] = grad
     acc[...] += dot_t(grad, taps)
 
-    @pl.when(step == pl.num_programs(0) - 1)
-    def _():
-        core = sc[8]
-        for x in range(4):
-            mine = pl.ds(pl.multiple_of(x * 128 + core * 64, 64), 64)
-            other = pl.ds(pl.multiple_of(x * 128 + (1 - core) * 64, 64), 64)
-            keep[x] = acc[mine, :]
-            send[x] = acc[other, :].astype(BF16)
-
-
-def backward_kernel(sc, lg, sl, xs, wt, wst, gain, nst, tc, im, out, acc, carry):
-    step = pl.program_id(0)
-
-    @pl.when(step == 0)
-    def _():
-        acc[...] = jnp.zeros_like(acc)
-        carry[...] = jnp.zeros_like(carry)
-
-    grad = lg[...]
     third = dot(grad, wt[:, 2 * CH :])
     row = lax.broadcasted_iota(jnp.int32, (BLK, 1), 0)
     shifted = jnp.where(row == 0, carry[0:1, :], pltpu.roll(third, 1, 0))
     carry[0:1, :] = third[BLK - 1 : BLK]
-    ag_e = (dot(grad, wt[:, :CH]) + shifted) * sl[0]
-    ag_o = dot(grad, wt[:, CH : 2 * CH]) * sl[1]
-    total = acc[...]
-    for part, ag in ((xs[0], ag_e), (xs[1], ag_o)):
+    ag_e = (dot(grad, wt[:, :CH]) + shifted) * s_e[:BLK]
+    ag_o = dot(grad, wt[:, CH : 2 * CH]) * s_o
+    total = grads[...]
+    for g, ag in enumerate((ag_e, ag_o)):
+        part = xs[g, pl.ds(base, BLK), :]
         high = ag.astype(BF16)
         low = (ag - high.astype(F32)).astype(BF16)
         total = total + dot_t(part, high) + dot_t(part, low)
-    acc[...] = total
+    grads[...] = total
 
     @pl.when(step == pl.num_programs(0) - 1)
     def _():
-        segs = plan(sc)
         z = jnp.zeros((32, CH), F32)
         g_bias = jnp.zeros((1, CH), F32)
         g_gain = jnp.zeros((1, CH), F32)
         g = gain[...]
         for s, (_slot, _off, n) in enumerate(segs):
             at = 32 * s
-            a = acc[at : at + 32, :]
+            a = grads[at : at + 32, :]
             inv, mean = im[s : s + 1, :], im[4 + s : 5 + s, :]
             count = 2.0 * n.astype(F32) - 1.0
             s1 = a[15:16] + a[31:32]
@@ -241,74 +223,148 @@
             )
             g_bias = g_bias + s1
             g_gain = g_gain + s2
-        out[0:10, :] = z[0:10] + z[21:31]
-        out[10:11, :] = g_gain
-        out[11:12, :] = g_bias
-        out[12:16, :] = jnp.zeros((4, CH), F32)
+        grads[0:10, :] = z[0:10] + z[21:31]
+        grads[10:11, :] = g_gain
+        grads[11:12, :] = g_bias
+        small[0:12, :] = grads[0:12, 0:384]
+        for j in range(3):
+            small[12:16, 128 * j : 128 * (j + 1)] = grads[4 * j : 4 * j + 4, 384:512]
+        core = sc[8]
+        for k, (x, y) in enumerate(BLOCKS):
+            lanes = pl.ds(384 * y, 384)
+            rows = pl.ds(64 * k, 64)
+            keep[rows, :] = acc[pl.ds(pl.multiple_of(x * 128 + core * 64, 64), 64), lanes]
+            send[rows, :] = acc[
+                pl.ds(pl.multiple_of(x * 128 + (1 - core) * 64, 64), 64), lanes
+            ].astype(BF16)
+        pack_small(small, send, 1024, True)
+
+
+def pack_small(small, send, at, coarse):
+    value = small[...]
+    if not coarse:
+        send[at : at + value.shape[0], :] = value
+        return
+    high = value.astype(BF16)
+    low = (value - high.astype(F32)).astype(BF16)
+    send[at : at + 16, :] = high
+    send[at + 16 : at + 32, :] = low
+    small[...] = high.astype(F32) + low.astype(F32)
+
+
+def received_small(recv, at):
+    if recv.dtype == F32:
+        return recv[at:, :]
+    return recv[at : at + 16, :].astype(F32) + recv[at + 16 : at + 32, :].astype(F32)
+
+
+def combine_kernel(n, flag, coarse, sc, keep, small, recv, keep_out, small_out, send):
+    half = n // 2
+    mine = pl.ds(pl.multiple_of(sc[flag] * half, half), half)
+    other = pl.ds(pl.multiple_of((1 - sc[flag]) * half, half), half)
+    keep_out[...] = keep[mine, :] + recv[mine, :].astype(F32)
+    send[0:half, :] = (keep[other, :] + recv[other, :].astype(F32)).astype(send.dtype)
+    small_out[...] = small[...] + received_small(recv, n)
+    pack_small(small_out, send, half, coarse)
+
+
+def turn_kernel(sc, keep, small, recv, keep_out, small_out, send):
+    total = (keep[...] + recv[0:64, :]).T
+    total = jnp.concatenate([total[0:192], total[192:384]], axis=1)
+    low = sc[13]
+    for mid in range(2):
+        even = total[96 * mid : 96 * mid + 48]
+        odd = total[96 * mid + 48 : 96 * mid + 96]
+        at = pl.ds(48 * mid, 48)
+        keep_out[at, :] = jnp.where(low == 1, odd, even)
+        send[at, :] = jnp.where(low == 1, even, odd)
+    sums = small[...] + recv[64:80, :]
+    for j in range(3):
+        small_out[16 * j : 16 * j + 16, :] = sums[:, 128 * j : 128 * (j + 1)]
+    send[96:144, :] = small_out[...]
+
+
+def middle_kernel(sc, keep, small, recv, keep_out, small_out, send):
+    mine = pl.ds(pl.multiple_of(sc[14] * 48, 8), 48)
+    other = pl.ds(pl.multiple_of((1 - sc[14]) * 48, 8), 48)
+    kept = keep[mine, :] + recv[mine, :]
+    keep_out[...] = kept
+    send[0:48, :] = keep[other, :] + recv[other, :]
+    sums = small[...] + recv[96:144, :]
+    small_out[...] = sums
+    send[48:96, :] = sums
+
+
+def last_kernel(sc, keep, small, recv, keep_out, small_out, send):
+    del sc
+    kept = keep[...] + recv[0:48, :]
+    sums = small[...] + recv[48:96, :]
+    keep_out[...] = kept
+    small_out[...] = sums
+    send[0:48, :] = kept
+    send[48:96, :] = sums
+
+
+def final_kernel(sc, keep, small, recv, second, first, g_gain, g_bias, flat):
+    total = keep[...] + recv[0:48, :]
+    second[...] = jnp.where(sc[15] == 1, total[:, 64:128], total[:, 0:64])
+    sums = small[...] + recv[48:96, :]
+    for j in range(3):
+        part = sums[16 * j : 16 * j + 16]
+        flat[0:12, 128 * j : 128 * (j + 1)] = part[0:12]
+        flat[4 * j : 4 * j + 4, 384:512] = part[12:16]
+    first[...] = flat[0:10, :]
+    g_gain[...] = flat[10:11, :]
+    g_bias[...] = flat[11:12, :]
 
 
 def full(shape):
     return pl.BlockSpec(shape, lambda i, sc: (0,) * len(shape))
 
 
-def forward(sc, u, cot, wst, gain, bias, w2):
-    shapes = [
-        ((ROWS, CH), BF16, pl.BlockSpec((BLK, CH), lambda i, sc: (i, 0))),
-        ((2, ROWS, CH), F32, pl.BlockSpec((2, BLK, CH), lambda i, sc: (0, i, 0))),
-        ((4, 64, 3 * CH), F32, None),
-        ((4, 64, 3 * CH), BF16, None),
-        ((2, ROWS, 128), BF16, None),
-        ((128, CH), F32, None),
-        ((128, 128), F32, None),
-        ((8, CH), F32, None),
-    ]
+def window(sc, u, cot, wst, gain, bias, w2, wt):
+    shapes = [((1024, 384), F32), ((1056, 384), BF16), ((16, 384), F32)]
     return pl.pallas_call(
-        forward_kernel,
+        window_kernel,
         grid_spec=pltpu.PrefetchScalarGridSpec(
             num_scalar_prefetch=1,
             grid=(ROWS // BLK,),
             in_specs=[
-                full((SLOTS * GRAN, 128)),
+                full((SLOTS * GRAN, TAPS)),
                 pl.BlockSpec((BLK, CH), lambda i, sc: (i, 0)),
-                full((128, CH)), full((1, CH)), full((1, CH)), full((3 * CH, CH)),
+                full((128, CH)), full((1, CH)), full((1, CH)), full((3 * CH, CH)), full((CH, 3 * CH)),
             ],
-            out_specs=[full(s) if b is None else b for s, _d, b in shapes],
+            out_specs=[full(s) for s, _d in shapes],
             scratch_shapes=[
                 pltpu.VMEM((ROWS + GRAN, 128), F32),
                 pltpu.VMEM((ROWS, 128), F32),
                 pltpu.VMEM((ROWS + 16, 256), BF16),
+                pltpu.VMEM((2, ROWS, 128), BF16),
                 pltpu.VMEM((256, 2 * CH), BF16),
                 pltpu.VMEM((CH, 3 * CH), F32),
+                pltpu.VMEM((128, CH), F32),
+                pltpu.VMEM((128, 128), F32),
+                pltpu.VMEM((8, CH), F32),
+                pltpu.VMEM((128, CH), F32),
+                pltpu.VMEM((8, CH), F32),
             ],
         ),
-        out_shape=[jax.ShapeDtypeStruct(s, d) for s, d, _b in shapes],
-        compiler_params=pltpu.CompilerParams(vmem_limit_bytes=50 * 2**20),
-        cost_estimate=pl.CostEstimate(flops=8 * 10**9, bytes_accessed=20 * 10**6, transcendentals=0),
-        name="forward_window",
-    )(sc, u, cot, wst, gain, bias, w2)
-
-
-def backward(sc, lg, sl, xs, wt, wst, gain, nst, tc, im):
+        out_shape=[jax.ShapeDtypeStruct(s, d) for s, d in shapes],
+        compiler_params=pltpu.CompilerParams(vmem_limit_bytes=56 * 2**20),
+        cost_estimate=pl.CostEstimate(flops=14 * 10**9, bytes_accessed=10 * 10**6, transcendentals=0),
+        name="window",
+    )(sc, u, cot, wst, gain, bias, w2, wt)
+
+
+def small_call(kernel, name, sc, args, shapes, scratch=()):
     return pl.pallas_call(
-        backward_kernel,
-        grid_spec=pltpu.PrefetchScalarGridSpec(
-            num_scalar_prefetch=1,
-            grid=(ROWS // BLK,),
-            in_specs=[
-                pl.BlockSpec((BLK, CH), lambda i, sc: (i, 0)),
-                pl.BlockSpec((2, BLK, CH), lambda i, sc: (0, i, 0)),
-                pl.BlockSpec((2, BLK, 128), lambda i, sc: (0, i, 0)),
-                full((CH, 3 * CH)), full((128, CH)), full((1, CH)),
-                full((128, CH)), full((128, 128)), full((8, CH)),
-            ],
-            out_specs=full((16, CH)),
-            scratch_shapes=[pltpu.VMEM((128, CH), F32), pltpu.VMEM((8, CH), F32)],
-        ),
-        out_shape=jax.ShapeDtypeStruct((16, CH), F32),
-        compiler_params=pltpu.CompilerParams(vmem_limit_bytes=40 * 2**20),
-        cost_estimate=pl.CostEstimate(flops=5 * 10**9, bytes_accessed=14 * 10**6, transcendentals=0),
-        name="backward_window",
-    )(sc, lg, sl, xs, wt, wst, gain, nst, tc, im)
+        kernel,
+        in_specs=[pl.BlockSpec(memory_space=pltpu.SMEM)] + [pl.BlockSpec(memory_space=pltpu.VMEM)] * len(args),
+        out_specs=[pl.BlockSpec(memory_space=pltpu.VMEM)] * len(shapes),
+        out_shape=[jax.ShapeDtypeStruct(s, d) for s, d in shapes],
+        scratch_shapes=list(scratch),
+        name=name,
+    )(sc, *args)
 
 
 def swap(value, axis, bit):
@@ -334,22 +390,12 @@
     return jnp.tile(jnp.concatenate([even, odd], axis=0), (SLOTS, 1))
 
 
-def halve(pair, bit, axis, dtype, mask):
-    low, high = pair
-    flag = bit == 1
-    mine = jnp.where(flag, high, low)
-    other = jnp.where(flag, low, high).astype(dtype)
-    return mine + swap(other, axis, mask).astype(F32)
-
-
-def local(rows, units, sources, core, cot, conv_first, norm_gain, norm_bias, conv_second):
-    u = jnp.pad(rows.reshape(SLOTS * GRAN, TAPS).astype(F32), ((0, 0), (0, 128 - TAPS)))
-    sc = jnp.concatenate([units, sources, jnp.full((8,), core, jnp.int32)])
+def local(rows, units, sources, places, cot, conv_first, norm_gain, norm_bias, conv_second):
+    u = rows.reshape(SLOTS * GRAN, TAPS)
+    sc = jnp.concatenate([units, sources, places])
     wst = window_inputs(conv_first)
     gain, bias = norm_gain[None, :], norm_bias[None, :]
-    lg, sl, keep, send, xs, nst, tc, im = forward(sc, u, cot, wst, gain, bias, conv_second)
-    small = backward(sc, lg, sl, xs, conv_second.T, wst, gain, nst, tc, im)
-    return keep, send, small
+    return sc, window(sc, u, cot, wst, gain, bias, conv_second, conv_second.T)
 
 
 def per_device(waveforms, owner_of, lengths, cotangent, conv_first, norm_gain, norm_bias, conv_second):
@@ -357,31 +403,38 @@
     place = lax.axis_index("bulk")
     masks = jnp.bitwise_xor(owner_of[0], me)
     rows, units = route(waveforms[0], lengths[0], masks)
-    keep, send, small = local(
-        rows, units, jnp.bitwise_xor(masks, me), place % 2, cotangent[0, 0],
+    places = jnp.stack(
+        [place % 2, (place // 2) % 2, (me // 8) % 2, place // 4, me // 16, me % 2, (me // 2) % 2, (me // 4) % 2]
+    ).astype(jnp.int32)
+    sc, (keep, send, small) = local(
+        rows, units, jnp.bitwise_xor(masks, me), places, cotangent[0, 0],
         conv_first, norm_gain, norm_bias, conv_second,
     )
-    total = keep + swap(send, "bulk", 1).astype(F32)
-
-    x, y, z = place // 2, me // 8, me % 8
-    t = total.reshape(2, 2, 64, 3 * CH)
-    t = halve((t[:, 0], t[:, 1]), x % 2, "bulk", BF16, 2)
-    q = [t[:, :, 384 * k : 384 * (k + 1)] for k in range(4)]
-    t = halve(
-        (jnp.stack([q[0], q[2]]), jnp.stack([q[1], q[3]])), y % 2, "wide", BF16, 8
-    )
-    t = halve((t[:, 0], t[:, 1]), x // 2, "bulk", BF16, 4)
-    t = halve((t[0], t[1]), y // 2, "wide", F32, 16)
-    t = t.T.reshape(8, 48, 64)
-    t = t.reshape(4, 2, 48, 64)
-    t = halve((t[:, 0], t[:, 1]), z % 2, "wide", F32, 1)
-    t = t.reshape(2, 2, 48, 64)
-    t = halve((t[:, 0], t[:, 1]), (z // 2) % 2, "wide", F32, 2)
-    grad_second = halve((t[0], t[1]), z // 4, "wide", F32, 4)
-
-    for axis, mask in (("bulk", 1), ("bulk", 2), ("bulk", 4), ("wide", 1), ("wide", 2), ("wide", 4), ("wide", 8), ("wide", 16)):
-        small = small + swap(small, axis, mask)
-    return (grad_second, small[:10], small[10], small[11])
+    n = 1024
+    recv = swap(send, "bulk", 1)
+    for flag, axis, bit, coarse in ((9, "bulk", 2, True), (10, "wide", 8, True), (11, "bulk", 4, True), (12, "wide", 16, False)):
+        half = n // 2
+        out = [
+            ((half, 384), F32), ((16, 384), F32),
+            ((half + 32, 384), BF16) if coarse else ((half + 16, 384), F32),
+        ]
+        kernel = functools.partial(combine_kernel, n, flag, coarse)
+        keep, small, send = small_call(kernel, "combine%d" % n, sc, (keep, small, recv), out)
+        recv = swap(send, axis, bit)
+        n = half
+    out = [((96, 128), F32), ((48, 128), F32), ((144, 128), F32)]
+    keep, small, send = small_call(turn_kernel, "turn", sc, (keep, small, recv), out)
+    recv = swap(send, "wide", 1)
+    out = [((48, 128), F32), ((48, 128), F32), ((96, 128), F32)]
+    keep, small, send = small_call(middle_kernel, "middle", sc, (keep, small, recv), out)
+    recv = swap(send, "wide", 2)
+    keep, small, send = small_call(last_kernel, "last", sc, (keep, small, recv), out)
+    recv = swap(send, "wide", 4)
+    out = [((48, 64), F32), ((10, CH), F32), ((1, CH), F32), ((1, CH), F32)]
+    second, first, g_gain, g_bias = small_call(
+        final_kernel, "final", sc, (keep, small, recv), out, [pltpu.VMEM((16, CH), F32)]
+    )
+    return (second, first, g_gain[0], g_bias[0])
 
 
 def solution(mesh):

time: 160 us -> 149 us (0.931); the launches traced: 159 us -> 146 us
  starting transfers between devices: 52.4 us -> 36 us
  Pallas kernels: 35.6 us -> 48.8 us
  other arithmetic: 11.3 us -> 4.64 us
  waiting for transfers between devices: 45 us -> 43.2 us
    ppermute x21 -> x13, starting transfers between devices: 52.4 us -> 36 us  [swap(): return lax.ppermute(value, axis, [(i, i ^ bit) for i in range(count)])]
    pallas_call x2 -> x9, Pallas kernels: 35.6 us -> 48.8 us  [the longest x1 33.8 us: window(): pl.pallas_call(window_kernel, grid_spec=pltpu.PrefetchScalarGridSpec(num_...]
    add x15 -> x0, other arithmetic: 4.63 us -> none  [the longest x6 3.22 us: halve(): return mine + swap(other, axis, mask).astype(F32)]
    reshape x0 -> x1, local copies, waits for them, and re-layouts: none -> 3.34 us  [local(): u = rows.reshape(SLOTS * GRAN, TAPS)]
    convert_element_type x1 -> x0, local copies, waits for them, and re-layouts: 2.36 us -> none  [local(): rows.reshape(SLOTS * GRAN, TAPS).astype(F32)]
    unnamed x18, local copies, waits for them, and re-layouts: 10.2 us -> 8.24 us
    ppermute x21 -> x13, waiting for transfers between devices: 45 us -> 43.2 us  [swap(): return lax.ppermute(value, axis, [(i, i ^ bit) for i in range(count)])]
  transfers between devices with their start and end apart: 21 -> 13, of which waited for: 17 -> 12; matrix products, arithmetic and copies ran while one was open for 3% -> 3% of each run, Pallas kernels for 5% -> 0%
where the time goes in v2:
time: 149 us; the launch traced here: 146 us
  Pallas kernels  48.8 us (33%)
  waiting for transfers between devices  43.2 us (29%)
  starting transfers between devices  36 us (24%)
  local copies, waits for them, and re-layouts  13 us (9%)
  other arithmetic  4.64 us (3%)
    ppermute x13, waiting for transfers between devices, swap(): return lax.ppermute(value, axis, [(i, i ^ bit) for i in range(count)])  43.2 us
    ppermute x13, starting transfers between devices, swap(): return lax.ppermute(value, axis, [(i, i ^ bit) for i in range(count)])  36 us
    pallas_call x1, Pallas kernels, window(): pl.pallas_call(window_kernel, grid_spec=pltpu.PrefetchScalarGridSpec(num_...  33.8 us
    pallas_call x8, Pallas kernels, small_call(): pl.pallas_call(kernel, in_specs=[pl.BlockSpec(memory_space=pltpu.SMEM)] +...  15 us
    unnamed x18, local copies, waits for them, and re-layouts  8.24 us
    reshape x1, local copies, waits for them, and re-layouts, local(): u = rows.reshape(SLOTS * GRAN, TAPS)  3.34 us
  transfers between devices with their start and end apart: 13, of which 12 were waited for; matrix products, arithmetic and copies ran while one was open for 3% of the time, Pallas kernels for 0%

profile of v2, /device:TPU:32, one launch (start us, length us, event | category | flops | bytes accessed | tf_op | source)
XLA Modules:
  0.0 146.4 jit_solution(13154426267353401252)
XLA Ops:
  7.9 3.4 %collective-permute-start.1 = (bf16[4,10368]{1,0:T(4,128)(2,1)S(1)}, bf16[4,10368]{1,0:T(4,128)(2,1)S(1)}, u32[]{:S(2)}, u32[]{:S(2)}) collective-permute-start(bf16[4,10368]{1,0:T(4,128)(2,1)S(1)} %broadcast_select_fusion), channel_id=1, source_target_pairs={{0,16},{8,24},{16,0},{24,8},{32,48},{40,56},{48,32},{56,40},{64,80... | collective-permute-start | bytes 248840 | tf_op jit(solution)/shard_map/ppermute | solution.py:372
  11.3 2.5 %collective-permute-done.1 = bf16[4,10368]{1,0:T(4,128)(2,1)S(1)} collective-permute-done((bf16[4,10368]{1,0:T(4,128)(2,1)S(1)}, bf16[4,10368]{1,0:T(4,128)(2,1)S(1)}, u32[]{:S(2)}, u32[]{:S(2)}) %collective-permute-start.1) | collective-permute-done | bytes 82976 | tf_op jit(solution)/shard_map/ppermute | solution.py:372
  13.9 6.0 %collective-permute-start.2 = (bf16[4,10368]{1,0:T(4,128)(2,1)S(1)}, bf16[4,10368]{1,0:T(4,128)(2,1)S(1)}, u32[]{:S(2)}, u32[]{:S(2)}) collective-permute-start(bf16[4,10368]{1,0:T(4,128)(2,1)S(1)} %broadcast_select_fusion.1), channel_id=1, source_target_pairs={{0,32},{8,40},{16,48},{24,56},{32,0},{40,8},{48,16},{56,24},{64,96... | collective-permute-start | bytes 248840 | tf_op jit(solution)/shard_map/ppermute | solution.py:372
  19.9 2.7 %collective-permute-done.2 = bf16[4,10368]{1,0:T(4,128)(2,1)S(1)} collective-permute-done((bf16[4,10368]{1,0:T(4,128)(2,1)S(1)}, bf16[4,10368]{1,0:T(4,128)(2,1)S(1)}, u32[]{:S(2)}, u32[]{:S(2)}) %collective-permute-start.2) | collective-permute-done | bytes 82976 | tf_op jit(solution)/shard_map/ppermute | solution.py:372
  25.2 2.6 %copy.15 = bf16[1536,512]{0,1:T(8,128)(2,1)} copy(bf16[1536,512]{1,0:T(8,128)(2,1)} %w2.1) | data formatting | bytes 3145728 | tf_op args[7]
  27.9 3.7 %collective-permute-start.4 = (bf16[4,10368]{1,0:T(4,128)(2,1)S(1)}, bf16[4,10368]{1,0:T(4,128)(2,1)S(1)}, u32[]{:S(2)}, u32[]{:S(2)}) collective-permute-start(bf16[4,10368]{1,0:T(4,128)(2,1)S(1)} %broadcast_select_fusion.3), channel_id=1, source_target_pairs={{0,128},{8,136},{16,144},{24,152},{32,160},{40,168},{48,176},{56,1... | collective-permute-start | bytes 248840 | tf_op jit(solution)/shard_map/ppermute | solution.py:372
  31.7 2.5 %collective-permute-done.4 = bf16[4,10368]{1,0:T(4,128)(2,1)S(1)} collective-permute-done((bf16[4,10368]{1,0:T(4,128)(2,1)S(1)}, bf16[4,10368]{1,0:T(4,128)(2,1)S(1)}, u32[]{:S(2)}, u32[]{:S(2)}) %collective-permute-start.4) | collective-permute-done | bytes 82976 | tf_op jit(solution)/shard_map/ppermute | solution.py:372
  34.5 3.3 %reshape.203.u = bf16[4096,10]{1,0:T(8,128)(2,1)} reshape(bf16[4,10240]{1,0:T(4,128)(2,1)S(1)} %slice.17) | data formatting | bytes 163840 | tf_op jit(solution)/shard_map/reshape | solution.py:394
  39.2 33.8 %window.1 = (f32[1024,384]{1,0:T(8,128)}, bf16[1056,384]{1,0:T(8,128)(2,1)}, f32[16,384]{1,0:T(8,128)}) custom-call(s32[16]{0:T(128)} %concatenate.10.sc, bf16[4096,10]{1,0:T(8,128)(2,1)} %reshape.203.u, bf16[2048,512]{1,0:T(8,128)(2,1)} %bitcast.38, f32[128,512]{1,0:T(8,128)} %bitcast.37, f32[1,512]{1,0:T(1,128)} %bitcast.39, f32[1,512]{1,0:T(1,128)} %bitcast.40, ...), custom_call_target="tpu_custom_call" | custom-call | flops 14000000000 | bytes 10000000 | tf_op jit(solution)/shard_map/window/pallas_call | solution.py:327
  73.0 2.5 %collective-permute-done.5.recv = bf16[1056,384]{1,0:T(8,128)(2,1)S(1)} collective-permute-done((bf16[1056,384]{1,0:T(8,128)(2,1)}, bf16[1056,384]{1,0:T(8,128)(2,1)S(1)}, u32[]{:S(2)}, u32[]{:S(2)}) %collective-permute-start.5) | collective-permute-done | bytes 811040 | tf_op jit(solution)/shard_map/ppermute | solution.py:372
  76.4 2.8 %combine1024.1 = (f32[512,384]{1,0:T(8,128)}, f32[16,384]{1,0:T(8,128)}, bf16[544,384]{1,0:T(8,128)(2,1)}) custom-call(s32[16]{0:T(128)} %concatenate.10.sc, f32[1024,384]{1,0:T(8,128)} %get-tuple-element.32.keep, f32[16,384]{1,0:T(8,128)} %get-tuple-element.33.small, bf16[1056,384]{1,0:T(8,128)(2,1)} %copy-done), custom_call_target="tpu_custom_call" | custom-call | tf_op jit(solution)/shard_map/combine1024/pallas_call | solution.py:360
  80.7 10.4 %collective-permute-done.6.recv = bf16[544,384]{1,0:T(8,128)(2,1)S(1)} collective-permute-done((bf16[544,384]{1,0:T(8,128)(2,1)}, bf16[544,384]{1,0:T(8,128)(2,1)S(1)}, u32[]{:S(2)}, u32[]{:S(2)}) %collective-permute-start.6) | collective-permute-done | bytes 417824 | tf_op jit(solution)/shard_map/ppermute | solution.py:372
  91.9 2.2 %combine512.1 = (f32[256,384]{1,0:T(8,128)}, f32[16,384]{1,0:T(8,128)}, bf16[288,384]{1,0:T(8,128)(2,1)}) custom-call(s32[16]{0:T(128)} %concatenate.10.sc, f32[512,384]{1,0:T(8,128)} %get-tuple-element.35.keep, f32[16,384]{1,0:T(8,128)} %get-tuple-element.36.small, bf16[544,384]{1,0:T(8,128)(2,1)} %copy-done.1), custom_call_target="tpu_custom_call" | custom-call | tf_op jit(solution)/shard_map/combine512/pallas_call | solution.py:360
  95.1 5.8 %collective-permute-done.7.recv = bf16[288,384]{1,0:T(8,128)(2,1)S(1)} collective-permute-done((bf16[288,384]{1,0:T(8,128)(2,1)}, bf16[288,384]{1,0:T(8,128)(2,1)S(1)}, u32[]{:S(2)}, u32[]{:S(2)}) %collective-permute-start.7) | collective-permute-done | bytes 221216 | tf_op jit(solution)/shard_map/ppermute | solution.py:372
  103.4 3.0 %collective-permute-start.8 = (bf16[160,384]{1,0:T(8,128)(2,1)}, bf16[160,384]{1,0:T(8,128)(2,1)S(1)}, u32[]{:S(2)}, u32[]{:S(2)}) collective-permute-start(bf16[160,384]{1,0:T(8,128)(2,1)} %get-tuple-element.43), channel_id=1, source_target_pairs={{0,4},{1,5},{2,6},{3,7},{4,0},{5,1},{6,2},{7,3},{8,12},{9,13},{10,... | collective-permute-start | bytes 368648 | tf_op jit(solution)/shard_map/ppermute | solution.py:372
  106.4 3.6 %collective-permute-done.8.recv = bf16[160,384]{1,0:T(8,128)(2,1)S(1)} collective-permute-done((bf16[160,384]{1,0:T(8,128)(2,1)}, bf16[160,384]{1,0:T(8,128)(2,1)S(1)}, u32[]{:S(2)}, u32[]{:S(2)}) %collective-permute-start.8) | collective-permute-done | bytes 122912 | tf_op jit(solution)/shard_map/ppermute | solution.py:372
  112.4 3.5 %collective-permute-start.9 = (f32[80,384]{1,0:T(8,128)}, f32[80,384]{1,0:T(8,128)S(1)}, u32[]{:S(2)}, u32[]{:S(2)}) collective-permute-start(f32[80,384]{1,0:T(8,128)} %get-tuple-element.46), channel_id=1, source_target_pairs={{0,128},{8,136},{16,144},{24,152},{32,160},{40,168},{48,176},{56,1... | collective-permute-start | bytes 368648 | tf_op jit(solution)/shard_map/ppermute | solution.py:372
  115.8 3.1 %collective-permute-done.9.recv = f32[80,384]{1,0:T(8,128)S(1)} collective-permute-done((f32[80,384]{1,0:T(8,128)}, f32[80,384]{1,0:T(8,128)S(1)}, u32[]{:S(2)}, u32[]{:S(2)}) %collective-permute-start.9) | collective-permute-done | bytes 122912 | tf_op jit(solution)/shard_map/ppermute | solution.py:372
  121.4 2.5 %collective-permute-start.10 = (f32[144,128]{1,0:T(8,128)}, f32[144,128]{1,0:T(8,128)S(1)}, u32[]{:S(2)}, u32[]{:S(2)}) collective-permute-start(f32[144,128]{1,0:T(8,128)} %get-tuple-element.49), channel_id=1, source_target_pairs={{0,8},{8,0},{16,24},{24,16},{32,40},{40,32},{48,56},{56,48},{64,72... | collective-permute-start | bytes 221192 | tf_op jit(solution)/shard_map/ppermute | solution.py:372
  123.9 2.5 %collective-permute-done.10.recv = f32[144,128]{1,0:T(8,128)S(1)} collective-permute-done((f32[144,128]{1,0:T(8,128)}, f32[144,128]{1,0:T(8,128)S(1)}, u32[]{:S(2)}, u32[]{:S(2)}) %collective-permute-start.10) | collective-permute-done | bytes 73760 | tf_op jit(solution)/shard_map/ppermute | solution.py:372
  128.7 2.6 %collective-permute-start.11 = (f32[96,128]{1,0:T(8,128)}, f32[96,128]{1,0:T(8,128)S(1)}, u32[]{:S(2)}, u32[]{:S(2)}) collective-permute-start(f32[96,128]{1,0:T(8,128)} %get-tuple-element.52), channel_id=1, source_target_pairs={{0,16},{8,24},{16,0},{24,8},{32,48},{40,56},{48,32},{56,40},{64,80... | collective-permute-start | bytes 147464 | tf_op jit(solution)/shard_map/ppermute | solution.py:372
  131.3 2.6 %collective-permute-done.11.recv = f32[96,128]{1,0:T(8,128)S(1)} collective-permute-done((f32[96,128]{1,0:T(8,128)}, f32[96,128]{1,0:T(8,128)S(1)}, u32[]{:S(2)}, u32[]{:S(2)}) %collective-permute-start.11) | collective-permute-done | bytes 49184 | tf_op jit(solution)/shard_map/ppermute | solution.py:372
  136.0 5.2 %collective-permute-start.12 = (f32[96,128]{1,0:T(8,128)}, f32[96,128]{1,0:T(8,128)S(1)}, u32[]{:S(2)}, u32[]{:S(2)}) collective-permute-start(f32[96,128]{1,0:T(8,128)} %get-tuple-element.55), channel_id=1, source_target_pairs={{0,32},{8,40},{16,48},{24,56},{32,0},{40,8},{48,16},{56,24},{64,96... | collective-permute-start | bytes 147464 | tf_op jit(solution)/shard_map/ppermute | solution.py:372
  141.1 3.0 %collective-permute-done.12.recv = f32[96,128]{1,0:T(8,128)S(1)} collective-permute-done((f32[96,128]{1,0:T(8,128)}, f32[96,128]{1,0:T(8,128)S(1)}, u32[]{:S(2)}, u32[]{:S(2)}) %collective-permute-start.12) | collective-permute-done | bytes 49184 | tf_op jit(solution)/shard_map/ppermute | solution.py:372
  (48 shorter events, 29.8 us)
Async XLA Ops:
  2.4 4.5 %collective-permute-start = (bf16[4,10368]{1,0:T(4,128)(2,1)S(1)}, bf16[4,10368]{1,0:T(4,128)(2,1)S(1)}, u32[]{:S(2)}, u32[]{:S(2)}) collective-permute-start(bf16[4,10368]{1,0:T(4,128)(2,1)S(1)} %fusion.1), channel_id=1, source_target_pairs={{0,8},{8,0},{16,24},{24,16},{32,40},{40,32},{48,56},{56,48},{64,72... | collective-permute-start | bytes 248840 | tf_op jit(solution)/shard_map/ppermute | solution.py:372
  7.9 5.9 %collective-permute-start.1 = (bf16[4,10368]{1,0:T(4,128)(2,1)S(1)}, bf16[4,10368]{1,0:T(4,128)(2,1)S(1)}, u32[]{:S(2)}, u32[]{:S(2)}) collective-permute-start(bf16[4,10368]{1,0:T(4,128)(2,1)S(1)} %broadcast_select_fusion), channel_id=1, source_target_pairs={{0,16},{8,24},{16,0},{24,8},{32,48},{40,56},{48,32},{56,40},{64,80... | collective-permute-start | bytes 248840 | tf_op jit(solution)/shard_map/ppermute | solution.py:372
  13.9 8.8 %collective-permute-start.2 = (bf16[4,10368]{1,0:T(4,128)(2,1)S(1)}, bf16[4,10368]{1,0:T(4,128)(2,1)S(1)}, u32[]{:S(2)}, u32[]{:S(2)}) collective-permute-start(bf16[4,10368]{1,0:T(4,128)(2,1)S(1)} %broadcast_select_fusion.1), channel_id=1, source_target_pairs={{0,32},{8,40},{16,48},{24,56},{32,0},{40,8},{48,16},{56,24},{64,96... | collective-permute-start | bytes 248840 | tf_op jit(solution)/shard_map/ppermute | solution.py:372
  22.8 5.0 %collective-permute-start.3 = (bf16[4,10368]{1,0:T(4,128)(2,1)S(1)}, bf16[4,10368]{1,0:T(4,128)(2,1)S(1)}, u32[]{:S(2)}, u32[]{:S(2)}) collective-permute-start(bf16[4,10368]{1,0:T(4,128)(2,1)S(1)} %broadcast_select_fusion.2), channel_id=1, source_target_pairs={{0,64},{8,72},{16,80},{24,88},{32,96},{40,104},{48,112},{56,120},{... | collective-permute-start | bytes 248840 | tf_op jit(solution)/shard_map/ppermute | solution.py:372
  27.9 6.2 %collective-permute-start.4 = (bf16[4,10368]{1,0:T(4,128)(2,1)S(1)}, bf16[4,10368]{1,0:T(4,128)(2,1)S(1)}, u32[]{:S(2)}, u32[]{:S(2)}) collective-permute-start(bf16[4,10368]{1,0:T(4,128)(2,1)S(1)} %broadcast_select_fusion.3), channel_id=1, source_target_pairs={{0,128},{8,136},{16,144},{24,152},{32,160},{40,168},{48,176},{56,1... | collective-permute-start | bytes 248840 | tf_op jit(solution)/shard_map/ppermute | solution.py:372
  73.0 2.5 %collective-permute-start.5 = (bf16[1056,384]{1,0:T(8,128)(2,1)}, bf16[1056,384]{1,0:T(8,128)(2,1)S(1)}, u32[]{:S(2)}, u32[]{:S(2)}) collective-permute-start(bf16[1056,384]{1,0:T(8,128)(2,1)} %get-tuple-element.34), channel_id=1, source_target_pairs={{0,1},{1,0},{2,3},{3,2},{4,5},{5,4},{6,7},{7,6},{8,9},{9,8},{10,11... | collective-permute-start | bytes 2433032 | tf_op jit(solution)/shard_map/ppermute | solution.py:372
  75.5 0.9 copy-start
  79.2 11.9 %collective-permute-start.6 = (bf16[544,384]{1,0:T(8,128)(2,1)}, bf16[544,384]{1,0:T(8,128)(2,1)S(1)}, u32[]{:S(2)}, u32[]{:S(2)}) collective-permute-start(bf16[544,384]{1,0:T(8,128)(2,1)} %get-tuple-element.37), channel_id=1, source_target_pairs={{0,2},{1,3},{2,0},{3,1},{4,6},{5,7},{6,4},{7,5},{8,10},{9,11},{10,... | collective-permute-start | bytes 1253384 | tf_op jit(solution)/shard_map/ppermute | solution.py:372
  91.1 0.8 copy-start.1
  94.0 6.9 %collective-permute-start.7 = (bf16[288,384]{1,0:T(8,128)(2,1)}, bf16[288,384]{1,0:T(8,128)(2,1)S(1)}, u32[]{:S(2)}, u32[]{:S(2)}) collective-permute-start(bf16[288,384]{1,0:T(8,128)(2,1)} %get-tuple-element.40), channel_id=1, source_target_pairs={{0,64},{8,72},{16,80},{24,88},{32,96},{40,104},{48,112},{56,120},{... | collective-permute-start | bytes 663560 | tf_op jit(solution)/shard_map/ppermute | solution.py:372
  100.9 0.7 copy-start.2
  103.4 6.6 %collective-permute-start.8 = (bf16[160,384]{1,0:T(8,128)(2,1)}, bf16[160,384]{1,0:T(8,128)(2,1)S(1)}, u32[]{:S(2)}, u32[]{:S(2)}) collective-permute-start(bf16[160,384]{1,0:T(8,128)(2,1)} %get-tuple-element.43), channel_id=1, source_target_pairs={{0,4},{1,5},{2,6},{3,7},{4,0},{5,1},{6,2},{7,3},{8,12},{9,13},{10,... | collective-permute-start | bytes 368648 | tf_op jit(solution)/shard_map/ppermute | solution.py:372
  110.0 0.6 copy-start.4
  112.4 6.6 %collective-permute-start.9 = (f32[80,384]{1,0:T(8,128)}, f32[80,384]{1,0:T(8,128)S(1)}, u32[]{:S(2)}, u32[]{:S(2)}) collective-permute-start(f32[80,384]{1,0:T(8,128)} %get-tuple-element.46), channel_id=1, source_target_pairs={{0,128},{8,136},{16,144},{24,152},{32,160},{40,168},{48,176},{56,1... | collective-permute-start | bytes 368648 | tf_op jit(solution)/shard_map/ppermute | solution.py:372
  119.0 0.6 copy-start.3
  121.4 5.0 %collective-permute-start.10 = (f32[144,128]{1,0:T(8,128)}, f32[144,128]{1,0:T(8,128)S(1)}, u32[]{:S(2)}, u32[]{:S(2)}) collective-permute-start(f32[144,128]{1,0:T(8,128)} %get-tuple-element.49), channel_id=1, source_target_pairs={{0,8},{8,0},{16,24},{24,16},{32,40},{40,32},{48,56},{56,48},{64,72... | collective-permute-start | bytes 221192 | tf_op jit(solution)/shard_map/ppermute | solution.py:372
  126.5 0.6 copy-start.5
  128.7 5.2 %collective-permute-start.11 = (f32[96,128]{1,0:T(8,128)}, f32[96,128]{1,0:T(8,128)S(1)}, u32[]{:S(2)}, u32[]{:S(2)}) collective-permute-start(f32[96,128]{1,0:T(8,128)} %get-tuple-element.52), channel_id=1, source_target_pairs={{0,16},{8,24},{16,0},{24,8},{32,48},{40,56},{48,32},{56,40},{64,80... | collective-permute-start | bytes 147464 | tf_op jit(solution)/shard_map/ppermute | solution.py:372
  133.9 0.6 copy-start.7
  136.0 8.2 %collective-permute-start.12 = (f32[96,128]{1,0:T(8,128)}, f32[96,128]{1,0:T(8,128)S(1)}, u32[]{:S(2)}, u32[]{:S(2)}) collective-permute-start(f32[96,128]{1,0:T(8,128)} %get-tuple-element.55), channel_id=1, source_target_pairs={{0,32},{8,40},{16,48},{24,56},{32,0},{40,8},{48,16},{56,24},{64,96... | collective-permute-start | bytes 147464 | tf_op jit(solution)/shard_map/ppermute | solution.py:372
  144.2 0.6 copy-start.6

commit v3 on v2

--- a/solution.py
+++ b/solution.py
@@ -16,7 +16,9 @@
 ROWS = 2048
 CH = 512
 BLK = 256
-BLOCKS = [(2 * xh + xl, 2 * yh + yl) for xl in range(2) for yl in range(2) for xh in range(2) for yh in range(2)]
+BLOCKS = [
+    (2 * xh + (xl ^ xh), 2 * yh + (yl ^ yh)) for xl in range(2) for yl in range(2) for xh in range(2) for yh in range(2)
+]
 
 
 def dot(a, b, precision=None):
@@ -127,7 +129,7 @@
         ri = lax.broadcasted_iota(jnp.int32, (128, 128), 0)
         ci = lax.broadcasted_iota(jnp.int32, (128, 128), 1)
         moment = jnp.where(ri // 16 == ci // 16, moment, 0.0)
-        wrow = wst[...]
+        wrow = jnp.concatenate([wst[...]] * SLOTS, axis=0)
         v = dot(moment, wrow, HIGHEST)
         block8 = (
             lax.broadcasted_iota(jnp.int32, (8, 128), 0)
@@ -215,7 +217,7 @@
             inv, mean = im[s : s + 1, :], im[4 + s : 5 + s, :]
             count = 2.0 * n.astype(F32) - 1.0
             s1 = a[15:16] + a[31:32]
-            s2 = inv * (jnp.sum(a * wst[at : at + 32, :], axis=0, keepdims=True) - mean * s1)
+            s2 = inv * (jnp.sum(a * wst[...], axis=0, keepdims=True) - mean * s1)
             first = g * s1 / count
             cross = g * s2 / count
             z = z + inv * (
@@ -270,14 +272,15 @@
 
 def turn_kernel(sc, keep, small, recv, keep_out, small_out, send):
     total = (keep[...] + recv[0:64, :]).T
-    total = jnp.concatenate([total[0:192], total[192:384]], axis=1)
     low = sc[13]
     for mid in range(2):
-        even = total[96 * mid : 96 * mid + 48]
-        odd = total[96 * mid + 48 : 96 * mid + 96]
-        at = pl.ds(48 * mid, 48)
-        keep_out[at, :] = jnp.where(low == 1, odd, even)
-        send[at, :] = jnp.where(low == 1, even, odd)
+        halves = []
+        for bit in range(2):
+            at = [192 * high + 96 * (mid ^ high) + 48 * (bit ^ high) for high in range(2)]
+            halves.append(jnp.concatenate([total[at[0] : at[0] + 48], total[at[1] : at[1] + 48]], axis=1))
+        rows = pl.ds(48 * mid, 48)
+        keep_out[rows, :] = jnp.where(low == 1, halves[1], halves[0])
+        send[rows, :] = jnp.where(low == 1, halves[0], halves[1])
     sums = small[...] + recv[64:80, :]
     for j in range(3):
         small_out[16 * j : 16 * j + 16, :] = sums[:, 128 * j : 128 * (j + 1)]
@@ -318,11 +321,12 @@
     g_bias[...] = flat[11:12, :]
 
 
-def full(shape):
-    return pl.BlockSpec(shape, lambda i, sc: (0,) * len(shape))
+def in_vmem(value):
+    return pltpu.with_memory_space_constraint(value, pltpu.VMEM)
 
 
 def window(sc, u, cot, wst, gain, bias, w2, wt):
+    whole = pl.BlockSpec(memory_space=pltpu.VMEM)
     shapes = [((1024, 384), F32), ((1056, 384), BF16), ((16, 384), F32)]
     return pl.pallas_call(
         window_kernel,
@@ -330,11 +334,11 @@
             num_scalar_prefetch=1,
             grid=(ROWS // BLK,),
             in_specs=[
-                full((SLOTS * GRAN, TAPS)),
+                whole,
                 pl.BlockSpec((BLK, CH), lambda i, sc: (i, 0)),
-                full((128, CH)), full((1, CH)), full((1, CH)), full((3 * CH, CH)), full((CH, 3 * CH)),
+                whole, whole, whole, whole, whole,
             ],
-            out_specs=[full(s) for s, _d in shapes],
+            out_specs=[pl.BlockSpec(memory_space=pltpu.VMEM)] * len(shapes),
             scratch_shapes=[
                 pltpu.VMEM((ROWS + GRAN, 128), F32),
                 pltpu.VMEM((ROWS, 128), F32),
@@ -349,20 +353,25 @@
                 pltpu.VMEM((8, CH), F32),
             ],
         ),
-        out_shape=[jax.ShapeDtypeStruct(s, d) for s, d in shapes],
-        compiler_params=pltpu.CompilerParams(vmem_limit_bytes=56 * 2**20),
+        out_shape=[pltpu.VMEM(s, d) for s, d in shapes],
+        compiler_params=pltpu.CompilerParams(vmem_limit_bytes=40 * 2**20),
         cost_estimate=pl.CostEstimate(flops=14 * 10**9, bytes_accessed=10 * 10**6, transcendentals=0),
         name="window",
-    )(sc, u, cot, wst, gain, bias, w2, wt)
-
-
-def small_call(kernel, name, sc, args, shapes, scratch=()):
+    )(
+        sc, in_vmem(u), pltpu.with_memory_space_constraint(cot, pltpu.HBM),
+        in_vmem(wst), in_vmem(gain), in_vmem(bias), in_vmem(w2), in_vmem(wt),
+    )
+
+
+def small_call(kernel, name, sc, args, shapes, scratch=(), place=pltpu.VMEM):
+    args = [in_vmem(a) for a in args]
     return pl.pallas_call(
         kernel,
         in_specs=[pl.BlockSpec(memory_space=pltpu.SMEM)] + [pl.BlockSpec(memory_space=pltpu.VMEM)] * len(args),
         out_specs=[pl.BlockSpec(memory_space=pltpu.VMEM)] * len(shapes),
-        out_shape=[jax.ShapeDtypeStruct(s, d) for s, d in shapes],
+        out_shape=[place(s, d) for s, d in shapes],
         scratch_shapes=list(scratch),
+        compiler_params=pltpu.CompilerParams(vmem_limit_bytes=8 * 2**20),
         name=name,
     )(sc, *args)
 
@@ -373,12 +382,20 @@
 
 
 def route(rows, sizes, masks):
+    high_z, high_y = masks & 4, masks & 16
+    steps = (
+        (1, (masks & 1) ^ (high_z // 4)),
+        (2, (masks & 2) ^ (high_z // 2)),
+        (7, high_z),
+        (8, (masks & 8) ^ (high_y // 2)),
+        (24, high_y),
+    )
     units = sizes // TAPS
     extra = jnp.stack([(units // 32).astype(BF16), (units % 32).astype(BF16)], axis=1)
     value = jnp.concatenate([rows, jnp.pad(extra, ((0, 0), (0, 126)))], axis=1)
-    for bit in (1, 2, 4, 8, 16):
+    for bit, used in steps:
         moved = swap(value, "wide", bit)
-        value = jnp.where(((masks & bit) != 0)[:, None], moved, value)
+        value = jnp.where((used != 0)[:, None], moved, value)
     tail = value[:, -128:-126].astype(F32)
     return value[:, :-128], (tail[:, 0] * 32.0 + tail[:, 1]).astype(jnp.int32)
 
@@ -387,7 +404,7 @@
     w = conv_first.astype(F32)
     even = jnp.pad(w, ((0, 6), (0, 0)))
     odd = jnp.pad(w, ((5, 1), (0, 0)))
-    return jnp.tile(jnp.concatenate([even, odd], axis=0), (SLOTS, 1))
+    return jnp.concatenate([even, odd], axis=0)
 
 
 def local(rows, units, sources, places, cot, conv_first, norm_gain, norm_bias, conv_second):
@@ -403,8 +420,10 @@
     place = lax.axis_index("bulk")
     masks = jnp.bitwise_xor(owner_of[0], me)
     rows, units = route(waveforms[0], lengths[0], masks)
+    x_low, x_high, y_low, y_high = (place // 2) % 2, place // 4, (me // 8) % 2, me // 16
+    z_low, z_mid, z_high = me % 2, (me // 2) % 2, (me // 4) % 2
     places = jnp.stack(
-        [place % 2, (place // 2) % 2, (me // 8) % 2, place // 4, me // 16, me % 2, (me // 2) % 2, (me // 4) % 2]
+        [place % 2, x_low ^ x_high, y_low ^ y_high, x_high, y_high, z_low ^ z_high, z_mid ^ z_high, z_high]
     ).astype(jnp.int32)
     sc, (keep, send, small) = local(
         rows, units, jnp.bitwise_xor(masks, me), places, cotangent[0, 0],
@@ -412,7 +431,7 @@
     )
     n = 1024
     recv = swap(send, "bulk", 1)
-    for flag, axis, bit, coarse in ((9, "bulk", 2, True), (10, "wide", 8, True), (11, "bulk", 4, True), (12, "wide", 16, False)):
+    for flag, axis, bit, coarse in ((9, "bulk", 2, True), (10, "wide", 8, True), (11, "bulk", 6, True), (12, "wide", 24, False)):
         half = n // 2
         out = [
             ((half, 384), F32), ((16, 384), F32),
@@ -429,10 +448,10 @@
     keep, small, send = small_call(middle_kernel, "middle", sc, (keep, small, recv), out)
     recv = swap(send, "wide", 2)
     keep, small, send = small_call(last_kernel, "last", sc, (keep, small, recv), out)
-    recv = swap(send, "wide", 4)
+    recv = swap(send, "wide", 7)
     out = [((48, 64), F32), ((10, CH), F32), ((1, CH), F32), ((1, CH), F32)]
     second, first, g_gain, g_bias = small_call(
-        final_kernel, "final", sc, (keep, small, recv), out, [pltpu.VMEM((16, CH), F32)]
+        final_kernel, "final", sc, (keep, small, recv), out, [pltpu.VMEM((16, CH), F32)], jax.ShapeDtypeStruct
     )
     return (second, first, g_gain[0], g_bias[0])
 

time: 149 us -> 126 us (0.85)
  Pallas kernels: 48.8 us -> 36.4 us
  local copies, waits for them, and re-layouts: 13 us -> 6.56 us
  starting transfers between devices: 36 us -> 33 us
    pallas_call x8, Pallas kernels: 15 us -> 5.76 us  [small_call(): pl.pallas_call(kernel, in_specs=[pl.BlockSpec(memory_space=pltpu.SMEM)] +...]
    unnamed x18 -> x10, local copies, waits for them, and re-layouts: 8.24 us -> 3.05 us
    pallas_call x1, Pallas kernels: 33.8 us -> 30.7 us  [window(): pl.pallas_call(window_kernel, grid_spec=pltpu.PrefetchScalarGridSpec(num_...]
    ppermute x13, starting transfers between devices: 36 us -> 33 us  [swap(): return lax.ppermute(value, axis, [(i, i ^ bit) for i in range(count)])]
  transfers between devices with their start and end apart: 13 -> 13, of which waited for: 12 -> 13; matrix products, arithmetic and copies ran while one was open for 3% -> 3% of each run, Pallas kernels for 0% -> 0%
where the time goes in v3:
time: 126 us; the launch traced here: 124 us
  waiting for transfers between devices  42.9 us (34%)
  Pallas kernels  36.4 us (29%)
  starting transfers between devices  33 us (26%)
  local copies, waits for them, and re-layouts  6.56 us (5%)
  other arithmetic  4.65 us (4%)
    ppermute x13, waiting for transfers between devices, swap(): return lax.ppermute(value, axis, [(i, i ^ bit) for i in range(count)])  42.9 us
    ppermute x13, starting transfers between devices, swap(): return lax.ppermute(value, axis, [(i, i ^ bit) for i in range(count)])  33 us
    pallas_call x1, Pallas kernels, window(): pl.pallas_call(window_kernel, grid_spec=pltpu.PrefetchScalarGridSpec(num_...  30.7 us
    pallas_call x8, Pallas kernels, small_call(): pl.pallas_call(kernel, in_specs=[pl.BlockSpec(memory_space=pltpu.SMEM)] +...  5.76 us
    reshape x1, local copies, waits for them, and re-layouts, local(): u = rows.reshape(SLOTS * GRAN, TAPS)  3.39 us
    unnamed x10, local copies, waits for them, and re-layouts  3.05 us
  transfers between devices with their start and end apart: 13, of which 13 were waited for; matrix products, arithmetic and copies ran while one was open for 3% of the time, Pallas kernels for 0%

profile of v3, /device:TPU:32, one launch (start us, length us, event | category | flops | bytes accessed | tf_op | source)
XLA Modules:
  0.0 124.4 jit_solution(9942438301025277589)
XLA Ops:
  2.4 1.9 %collective-permute-start = (bf16[4,10368]{1,0:T(4,128)(2,1)S(1)}, bf16[4,10368]{1,0:T(4,128)(2,1)S(1)}, u32[]{:S(2)}, u32[]{:S(2)}) collective-permute-start(bf16[4,10368]{1,0:T(4,128)(2,1)S(1)} %fusion.1), channel_id=1, source_target_pairs={{0,8},{8,0},{16,24},{24,16},{32,40},{40,32},{48,56},{56,48},{64,72... | collective-permute-start | bytes 248840 | tf_op jit(solution)/shard_map/ppermute | solution.py:381
  5.0 1.9 %collective-permute-done = bf16[4,10368]{1,0:T(4,128)(2,1)S(1)} collective-permute-done((bf16[4,10368]{1,0:T(4,128)(2,1)S(1)}, bf16[4,10368]{1,0:T(4,128)(2,1)S(1)}, u32[]{:S(2)}, u32[]{:S(2)}) %collective-permute-start) | collective-permute-done | bytes 82976 | tf_op jit(solution)/shard_map/ppermute | solution.py:381
  7.9 3.4 %collective-permute-start.1 = (bf16[4,10368]{1,0:T(4,128)(2,1)S(1)}, bf16[4,10368]{1,0:T(4,128)(2,1)S(1)}, u32[]{:S(2)}, u32[]{:S(2)}) collective-permute-start(bf16[4,10368]{1,0:T(4,128)(2,1)S(1)} %broadcast_select_fusion), channel_id=1, source_target_pairs={{0,16},{8,24},{16,0},{24,8},{32,48},{40,56},{48,32},{56,40},{64,80... | collective-permute-start | bytes 248840 | tf_op jit(solution)/shard_map/ppermute | solution.py:381
  11.3 2.5 %collective-permute-done.1 = bf16[4,10368]{1,0:T(4,128)(2,1)S(1)} collective-permute-done((bf16[4,10368]{1,0:T(4,128)(2,1)S(1)}, bf16[4,10368]{1,0:T(4,128)(2,1)S(1)}, u32[]{:S(2)}, u32[]{:S(2)}) %collective-permute-start.1) | collective-permute-done | bytes 82976 | tf_op jit(solution)/shard_map/ppermute | solution.py:381
  13.9 5.6 %collective-permute-start.2 = (bf16[4,10368]{1,0:T(4,128)(2,1)S(1)}, bf16[4,10368]{1,0:T(4,128)(2,1)S(1)}, u32[]{:S(2)}, u32[]{:S(2)}) collective-permute-start(bf16[4,10368]{1,0:T(4,128)(2,1)S(1)} %broadcast_select_fusion.1), channel_id=1, source_target_pairs={{0,56},{8,48},{16,40},{24,32},{32,24},{40,16},{48,8},{56,0},{64,12... | collective-permute-start | bytes 248840 | tf_op jit(solution)/shard_map/ppermute | solution.py:381
  19.5 2.5 %collective-permute-done.2 = bf16[4,10368]{1,0:T(4,128)(2,1)S(1)} collective-permute-done((bf16[4,10368]{1,0:T(4,128)(2,1)S(1)}, bf16[4,10368]{1,0:T(4,128)(2,1)S(1)}, u32[]{:S(2)}, u32[]{:S(2)}) %collective-permute-start.2) | collective-permute-done | bytes 82976 | tf_op jit(solution)/shard_map/ppermute | solution.py:381
  22.1 1.7 %collective-permute-start.3 = (bf16[4,10368]{1,0:T(4,128)(2,1)S(1)}, bf16[4,10368]{1,0:T(4,128)(2,1)S(1)}, u32[]{:S(2)}, u32[]{:S(2)}) collective-permute-start(bf16[4,10368]{1,0:T(4,128)(2,1)S(1)} %broadcast_select_fusion.2), channel_id=1, source_target_pairs={{0,64},{8,72},{16,80},{24,88},{32,96},{40,104},{48,112},{56,120},{... | collective-permute-start | bytes 248840 | tf_op jit(solution)/shard_map/ppermute | solution.py:381
  24.5 1.7 %copy.15 = bf16[1536,512]{0,1:T(8,128)(2,1)S(1)} copy(bf16[1536,512]{1,0:T(8,128)(2,1)} %w2.1) | data formatting | bytes 3145728 | tf_op args[7]
  26.7 3.3 %collective-permute-start.4 = (bf16[4,10368]{1,0:T(4,128)(2,1)S(1)}, bf16[4,10368]{1,0:T(4,128)(2,1)S(1)}, u32[]{:S(2)}, u32[]{:S(2)}) collective-permute-start(bf16[4,10368]{1,0:T(4,128)(2,1)S(1)} %broadcast_select_fusion.3), channel_id=1, source_target_pairs={{0,192},{8,200},{16,208},{24,216},{32,224},{40,232},{48,240},{56,2... | collective-permute-start | bytes 248840 | tf_op jit(solution)/shard_map/ppermute | solution.py:381
  30.0 2.6 %collective-permute-done.4 = bf16[4,10368]{1,0:T(4,128)(2,1)S(1)} collective-permute-done((bf16[4,10368]{1,0:T(4,128)(2,1)S(1)}, bf16[4,10368]{1,0:T(4,128)(2,1)S(1)}, u32[]{:S(2)}, u32[]{:S(2)}) %collective-permute-start.4) | collective-permute-done | bytes 82976 | tf_op jit(solution)/shard_map/ppermute | solution.py:381
  33.0 3.4 %reshape.232.u = bf16[4096,10]{1,0:T(8,128)(2,1)} reshape(bf16[4,10240]{1,0:T(4,128)(2,1)S(1)} %slice.17) | data formatting | bytes 163840 | tf_op jit(solution)/shard_map/reshape | solution.py:411
  37.8 30.7 %window.1 = (f32[1024,384]{1,0:T(8,128)S(1)}, bf16[1056,384]{1,0:T(8,128)(2,1)S(1)}, f32[16,384]{1,0:T(8,128)S(1)}) custom-call(s32[16]{0:T(128)S(1)} %concatenate.10.sc, bf16[4096,10]{1,0:T(8,128)(2,1)S(1)} %copy-done.1, bf16[2048,512]{1,0:T(8,128)(2,1)} %bitcast.69, f32[32,512]{1,0:T(8,128)S(1)} %select_maximum_fusion.wst, f32[1,512]{1,0:T(1,128)S(1)} %bitcast.65, ...), custom_call_target="tpu_custom_call" | custom-call | flops 14000000000 | bytes 10000000 | tf_op jit(solution)/shard_map/window/pallas_call | solution.py:331
  68.5 2.3 %collective-permute-done.5.recv = bf16[1056,384]{1,0:T(8,128)(2,1)S(1)} collective-permute-done((bf16[1056,384]{1,0:T(8,128)(2,1)S(1)}, bf16[1056,384]{1,0:T(8,128)(2,1)S(1)}, u32[]{:S(2)}, u32[]{:S(2)}) %collective-permute-start.5) | collective-permute-done | bytes 811040 | tf_op jit(solution)/shard_map/ppermute | solution.py:381
  73.2 10.2 %collective-permute-done.6.recv = bf16[544,384]{1,0:T(8,128)(2,1)S(1)} collective-permute-done((bf16[544,384]{1,0:T(8,128)(2,1)S(1)}, bf16[544,384]{1,0:T(8,128)(2,1)S(1)}, u32[]{:S(2)}, u32[]{:S(2)}) %collective-permute-start.6) | collective-permute-done | bytes 417824 | tf_op jit(solution)/shard_map/ppermute | solution.py:381
  84.5 6.3 %collective-permute-done.7.recv = bf16[288,384]{1,0:T(8,128)(2,1)S(1)} collective-permute-done((bf16[288,384]{1,0:T(8,128)(2,1)S(1)}, bf16[288,384]{1,0:T(8,128)(2,1)S(1)}, u32[]{:S(2)}, u32[]{:S(2)}) %collective-permute-start.7) | collective-permute-done | bytes 221216 | tf_op jit(solution)/shard_map/ppermute | solution.py:381
  91.4 2.8 %collective-permute-start.8 = (bf16[160,384]{1,0:T(8,128)(2,1)S(1)}, bf16[160,384]{1,0:T(8,128)(2,1)S(1)}, u32[]{:S(2)}, u32[]{:S(2)}) collective-permute-start(bf16[160,384]{1,0:T(8,128)(2,1)S(1)} %get-tuple-element.43), channel_id=1, source_target_pairs={{0,6},{1,7},{2,4},{3,5},{4,2},{5,3},{6,0},{7,1},{8,14},{9,15},{10,... | collective-permute-start | bytes 368648 | tf_op jit(solution)/shard_map/ppermute | solution.py:381
  94.2 3.3 %collective-permute-done.8.recv = bf16[160,384]{1,0:T(8,128)(2,1)S(1)} collective-permute-done((bf16[160,384]{1,0:T(8,128)(2,1)S(1)}, bf16[160,384]{1,0:T(8,128)(2,1)S(1)}, u32[]{:S(2)}, u32[]{:S(2)}) %collective-permute-start.8) | collective-permute-done | bytes 122912 | tf_op jit(solution)/shard_map/ppermute | solution.py:381
  98.1 3.1 %collective-permute-start.9 = (f32[80,384]{1,0:T(8,128)S(1)}, f32[80,384]{1,0:T(8,128)S(1)}, u32[]{:S(2)}, u32[]{:S(2)}) collective-permute-start(f32[80,384]{1,0:T(8,128)S(1)} %get-tuple-element.46), channel_id=1, source_target_pairs={{0,192},{8,200},{16,208},{24,216},{32,224},{40,232},{48,240},{56,2... | collective-permute-start | bytes 368648 | tf_op jit(solution)/shard_map/ppermute | solution.py:381
  101.2 3.1 %collective-permute-done.9.recv = f32[80,384]{1,0:T(8,128)S(1)} collective-permute-done((f32[80,384]{1,0:T(8,128)S(1)}, f32[80,384]{1,0:T(8,128)S(1)}, u32[]{:S(2)}, u32[]{:S(2)}) %collective-permute-start.9) | collective-permute-done | bytes 122912 | tf_op jit(solution)/shard_map/ppermute | solution.py:381
  106.6 3.0 %collective-permute-done.10.recv = f32[144,128]{1,0:T(8,128)S(1)} collective-permute-done((f32[144,128]{1,0:T(8,128)S(1)}, f32[144,128]{1,0:T(8,128)S(1)}, u32[]{:S(2)}, u32[]{:S(2)}) %collective-permute-start.10) | collective-permute-done | bytes 73760 | tf_op jit(solution)/shard_map/ppermute | solution.py:381
  110.1 2.4 %collective-permute-start.11 = (f32[96,128]{1,0:T(8,128)S(1)}, f32[96,128]{1,0:T(8,128)S(1)}, u32[]{:S(2)}, u32[]{:S(2)}) collective-permute-start(f32[96,128]{1,0:T(8,128)S(1)} %get-tuple-element.52), channel_id=1, source_target_pairs={{0,16},{8,24},{16,0},{24,8},{32,48},{40,56},{48,32},{56,40},{64,80... | collective-permute-start | bytes 147464 | tf_op jit(solution)/shard_map/ppermute | solution.py:381
  112.5 2.7 %collective-permute-done.11.recv = f32[96,128]{1,0:T(8,128)S(1)} collective-permute-done((f32[96,128]{1,0:T(8,128)S(1)}, f32[96,128]{1,0:T(8,128)S(1)}, u32[]{:S(2)}, u32[]{:S(2)}) %collective-permute-start.11) | collective-permute-done | bytes 49184 | tf_op jit(solution)/shard_map/ppermute | solution.py:381
  115.8 5.2 %collective-permute-start.12 = (f32[96,128]{1,0:T(8,128)S(1)}, f32[96,128]{1,0:T(8,128)S(1)}, u32[]{:S(2)}, u32[]{:S(2)}) collective-permute-start(f32[96,128]{1,0:T(8,128)S(1)} %get-tuple-element.55), channel_id=1, source_target_pairs={{0,56},{8,48},{16,40},{24,32},{32,24},{40,16},{48,8},{56,0},{64,12... | collective-permute-start | bytes 147464 | tf_op jit(solution)/shard_map/ppermute | solution.py:381
  121.0 2.1 %collective-permute-done.12.recv = f32[96,128]{1,0:T(8,128)S(1)} collective-permute-done((f32[96,128]{1,0:T(8,128)S(1)}, f32[96,128]{1,0:T(8,128)S(1)}, u32[]{:S(2)}, u32[]{:S(2)}) %collective-permute-start.12) | collective-permute-done | bytes 49184 | tf_op jit(solution)/shard_map/ppermute | solution.py:381
  (39 shorter events, 15.8 us)
Async XLA Ops:
  2.4 4.5 %collective-permute-start = (bf16[4,10368]{1,0:T(4,128)(2,1)S(1)}, bf16[4,10368]{1,0:T(4,128)(2,1)S(1)}, u32[]{:S(2)}, u32[]{:S(2)}) collective-permute-start(bf16[4,10368]{1,0:T(4,128)(2,1)S(1)} %fusion.1), channel_id=1, source_target_pairs={{0,8},{8,0},{16,24},{24,16},{32,40},{40,32},{48,56},{56,48},{64,72... | collective-permute-start | bytes 248840 | tf_op jit(solution)/shard_map/ppermute | solution.py:381
  7.9 5.9 %collective-permute-start.1 = (bf16[4,10368]{1,0:T(4,128)(2,1)S(1)}, bf16[4,10368]{1,0:T(4,128)(2,1)S(1)}, u32[]{:S(2)}, u32[]{:S(2)}) collective-permute-start(bf16[4,10368]{1,0:T(4,128)(2,1)S(1)} %broadcast_select_fusion), channel_id=1, source_target_pairs={{0,16},{8,24},{16,0},{24,8},{32,48},{40,56},{48,32},{56,40},{64,80... | collective-permute-start | bytes 248840 | tf_op jit(solution)/shard_map/ppermute | solution.py:381
  13.9 8.1 %collective-permute-start.2 = (bf16[4,10368]{1,0:T(4,128)(2,1)S(1)}, bf16[4,10368]{1,0:T(4,128)(2,1)S(1)}, u32[]{:S(2)}, u32[]{:S(2)}) collective-permute-start(bf16[4,10368]{1,0:T(4,128)(2,1)S(1)} %broadcast_select_fusion.1), channel_id=1, source_target_pairs={{0,56},{8,48},{16,40},{24,32},{32,24},{40,16},{48,8},{56,0},{64,12... | collective-permute-start | bytes 248840 | tf_op jit(solution)/shard_map/ppermute | solution.py:381
  22.1 4.5 %collective-permute-start.3 = (bf16[4,10368]{1,0:T(4,128)(2,1)S(1)}, bf16[4,10368]{1,0:T(4,128)(2,1)S(1)}, u32[]{:S(2)}, u32[]{:S(2)}) collective-permute-start(bf16[4,10368]{1,0:T(4,128)(2,1)S(1)} %broadcast_select_fusion.2), channel_id=1, source_target_pairs={{0,64},{8,72},{16,80},{24,88},{32,96},{40,104},{48,112},{56,120},{... | collective-permute-start | bytes 248840 | tf_op jit(solution)/shard_map/ppermute | solution.py:381
  26.2 10.3 %copy-start = (bf16[1536,512]{1,0:T(8,128)(2,1)S(1)}, bf16[1536,512]{1,0:T(8,128)(2,1)}, u32[]{:S(2)}) copy-start(bf16[1536,512]{1,0:T(8,128)(2,1)} %w2.1) | copy-start | bytes 4718596
  26.2 10.3 %copy-start.2 = (f32[512]{0:T(512)S(1)}, f32[512]{0:T(512)}, u32[]{:S(2)}) copy-start(f32[512]{0:T(512)} %param.13) | copy-start | bytes 6148
  26.2 10.3 %copy-start.3 = (f32[512]{0:T(512)S(1)}, f32[512]{0:T(512)}, u32[]{:S(2)}) copy-start(f32[512]{0:T(512)} %param.14) | copy-start | bytes 6148
  26.7 5.9 %collective-permute-start.4 = (bf16[4,10368]{1,0:T(4,128)(2,1)S(1)}, bf16[4,10368]{1,0:T(4,128)(2,1)S(1)}, u32[]{:S(2)}, u32[]{:S(2)}) collective-permute-start(bf16[4,10368]{1,0:T(4,128)(2,1)S(1)} %broadcast_select_fusion.3), channel_id=1, source_target_pairs={{0,192},{8,200},{16,208},{24,216},{32,224},{40,232},{48,240},{56,2... | collective-permute-start | bytes 248840 | tf_op jit(solution)/shard_map/ppermute | solution.py:381
  36.5 1.2 copy-start.1
  68.4 2.4 %collective-permute-start.5 = (bf16[1056,384]{1,0:T(8,128)(2,1)S(1)}, bf16[1056,384]{1,0:T(8,128)(2,1)S(1)}, u32[]{:S(2)}, u32[]{:S(2)}) collective-permute-start(bf16[1056,384]{1,0:T(8,128)(2,1)S(1)} %get-tuple-element.34), channel_id=1, source_target_pairs={{0,1},{1,0},{2,3},{3,2},{4,5},{5,4},{6,7},{7,6},{8,9},{9,8},{10,11... | collective-permute-start | bytes 2433032 | tf_op jit(solution)/shard_map/ppermute | solution.py:381
  71.6 11.8 %collective-permute-start.6 = (bf16[544,384]{1,0:T(8,128)(2,1)S(1)}, bf16[544,384]{1,0:T(8,128)(2,1)S(1)}, u32[]{:S(2)}, u32[]{:S(2)}) collective-permute-start(bf16[544,384]{1,0:T(8,128)(2,1)S(1)} %get-tuple-element.37), channel_id=1, source_target_pairs={{0,2},{1,3},{2,0},{3,1},{4,6},{5,7},{6,4},{7,5},{8,10},{9,11},{10,... | collective-permute-start | bytes 1253384 | tf_op jit(solution)/shard_map/ppermute | solution.py:381
  84.0 6.7 %collective-permute-start.7 = (bf16[288,384]{1,0:T(8,128)(2,1)S(1)}, bf16[288,384]{1,0:T(8,128)(2,1)S(1)}, u32[]{:S(2)}, u32[]{:S(2)}) collective-permute-start(bf16[288,384]{1,0:T(8,128)(2,1)S(1)} %get-tuple-element.40), channel_id=1, source_target_pairs={{0,64},{8,72},{16,80},{24,88},{32,96},{40,104},{48,112},{56,120},{... | collective-permute-start | bytes 663560 | tf_op jit(solution)/shard_map/ppermute | solution.py:381
  91.4 6.2 %collective-permute-start.8 = (bf16[160,384]{1,0:T(8,128)(2,1)S(1)}, bf16[160,384]{1,0:T(8,128)(2,1)S(1)}, u32[]{:S(2)}, u32[]{:S(2)}) collective-permute-start(bf16[160,384]{1,0:T(8,128)(2,1)S(1)} %get-tuple-element.43), channel_id=1, source_target_pairs={{0,6},{1,7},{2,4},{3,5},{4,2},{5,3},{6,0},{7,1},{8,14},{9,15},{10,... | collective-permute-start | bytes 368648 | tf_op jit(solution)/shard_map/ppermute | solution.py:381
  98.1 6.2 %collective-permute-start.9 = (f32[80,384]{1,0:T(8,128)S(1)}, f32[80,384]{1,0:T(8,128)S(1)}, u32[]{:S(2)}, u32[]{:S(2)}) collective-permute-start(f32[80,384]{1,0:T(8,128)S(1)} %get-tuple-element.46), channel_id=1, source_target_pairs={{0,192},{8,200},{16,208},{24,216},{32,224},{40,232},{48,240},{56,2... | collective-permute-start | bytes 368648 | tf_op jit(solution)/shard_map/ppermute | solution.py:381
  105.1 4.5 %collective-permute-start.10 = (f32[144,128]{1,0:T(8,128)S(1)}, f32[144,128]{1,0:T(8,128)S(1)}, u32[]{:S(2)}, u32[]{:S(2)}) collective-permute-start(f32[144,128]{1,0:T(8,128)S(1)} %get-tuple-element.49), channel_id=1, source_target_pairs={{0,8},{8,0},{16,24},{24,16},{32,40},{40,32},{48,56},{56,48},{64,72... | collective-permute-start | bytes 221192 | tf_op jit(solution)/shard_map/ppermute | solution.py:381
  110.1 5.1 %collective-permute-start.11 = (f32[96,128]{1,0:T(8,128)S(1)}, f32[96,128]{1,0:T(8,128)S(1)}, u32[]{:S(2)}, u32[]{:S(2)}) collective-permute-start(f32[96,128]{1,0:T(8,128)S(1)} %get-tuple-element.52), channel_id=1, source_target_pairs={{0,16},{8,24},{16,0},{24,8},{32,48},{40,56},{48,32},{56,40},{64,80... | collective-permute-start | bytes 147464 | tf_op jit(solution)/shard_map/ppermute | solution.py:381
  115.8 7.3 %collective-permute-start.12 = (f32[96,128]{1,0:T(8,128)S(1)}, f32[96,128]{1,0:T(8,128)S(1)}, u32[]{:S(2)}, u32[]{:S(2)}) collective-permute-start(f32[96,128]{1,0:T(8,128)S(1)} %get-tuple-element.55), channel_id=1, source_target_pairs={{0,56},{8,48},{16,40},{24,32},{32,24},{40,16},{48,8},{56,0},{64,12... | collective-permute-start | bytes 147464 | tf_op jit(solution)/shard_map/ppermute | solution.py:381

commit v4 on v3

--- a/solution.py
+++ b/solution.py
@@ -239,14 +239,10 @@
             send[rows, :] = acc[
                 pl.ds(pl.multiple_of(x * 128 + (1 - core) * 64, 64), 64), lanes
             ].astype(BF16)
-        pack_small(small, send, 1024, True)
-
-
-def pack_small(small, send, at, coarse):
-    value = small[...]
-    if not coarse:
-        send[at : at + value.shape[0], :] = value
-        return
+        pack_small(small, small[...], send, 1024)
+
+
+def pack_small(small, value, send, at):
     high = value.astype(BF16)
     low = (value - high.astype(F32)).astype(BF16)
     send[at : at + 16, :] = high
@@ -260,48 +256,62 @@
     return recv[at : at + 16, :].astype(F32) + recv[at + 16 : at + 32, :].astype(F32)
 
 
-def combine_kernel(n, flag, coarse, sc, keep, small, recv, keep_out, small_out, send):
-    half = n // 2
-    mine = pl.ds(pl.multiple_of(sc[flag] * half, half), half)
-    other = pl.ds(pl.multiple_of((1 - sc[flag]) * half, half), half)
-    keep_out[...] = keep[mine, :] + recv[mine, :].astype(F32)
-    send[0:half, :] = (keep[other, :] + recv[other, :].astype(F32)).astype(send.dtype)
-    small_out[...] = small[...] + received_small(recv, n)
-    pack_small(small_out, send, half, coarse)
-
-
-def turn_kernel(sc, keep, small, recv, keep_out, small_out, send):
-    total = (keep[...] + recv[0:64, :]).T
-    low = sc[13]
+def quarters(sc, at):
+    a, b = sc[at], sc[at + 1]
+    return 2 * a + b, (2 * a + 1 - b, 2 * (1 - a) + b, 2 * (1 - a) + 1 - b)
+
+
+def add_small(small, recvs, at):
+    r = [received_small(recv, at) for recv in recvs]
+    return small[...] + r[0] if len(r) == 1 else (small[...] + r[0]) + (r[1] + r[2])
+
+
+def combine_kernel(n, recvs, flag, sc, keep, small, *refs):
+    recv, (keep_out, small_out, *sends) = refs[:recvs], refs[recvs:]
+    quarter = n // 4
+    mine, others = quarters(sc, flag)
+
+    def rows(index):
+        at = pl.ds(pl.multiple_of(index * quarter, quarter), quarter)
+        total = keep[at, :]
+        for r in recv:
+            total = total + r[at, :].astype(F32)
+        return total
+
+    keep_out[...] = rows(mine)
+    small_out[...] = add_small(small, recv, n)
+    for index, send in zip(others, sends):
+        send[0:quarter, :] = rows(index).astype(BF16)
+    value = small_out[...]
+    for send in sends:
+        pack_small(small_out, value, send, quarter)
+
+
+def turn_kernel(sc, keep, small, r0, r1, r2, keep_out, small_out, s0, s1, s2, turned):
+    total = keep[...]
+    for r in (r0, r1, r2):
+        total = total + r[0:64, :].astype(F32)
+    total = total.T
     for mid in range(2):
-        halves = []
-        for bit in range(2):
-            at = [192 * high + 96 * (mid ^ high) + 48 * (bit ^ high) for high in range(2)]
-            halves.append(jnp.concatenate([total[at[0] : at[0] + 48], total[at[1] : at[1] + 48]], axis=1))
-        rows = pl.ds(48 * mid, 48)
-        keep_out[rows, :] = jnp.where(low == 1, halves[1], halves[0])
-        send[rows, :] = jnp.where(low == 1, halves[0], halves[1])
-    sums = small[...] + recv[64:80, :]
+        for low in range(2):
+            at = [192 * high + 96 * (mid ^ high) + 48 * (low ^ high) for high in range(2)]
+            turned[96 * low + 48 * mid : 96 * low + 48 * mid + 48, :] = jnp.concatenate(
+                [total[at[0] : at[0] + 48], total[at[1] : at[1] + 48]], axis=1
+            )
+    mine, others = quarters(sc, 13)
+    keep_out[...] = turned[pl.ds(pl.multiple_of(mine * 48, 8), 48), :]
+    sums = add_small(small, (r0, r1, r2), 64)
     for j in range(3):
         small_out[16 * j : 16 * j + 16, :] = sums[:, 128 * j : 128 * (j + 1)]
-    send[96:144, :] = small_out[...]
-
-
-def middle_kernel(sc, keep, small, recv, keep_out, small_out, send):
-    mine = pl.ds(pl.multiple_of(sc[14] * 48, 8), 48)
-    other = pl.ds(pl.multiple_of((1 - sc[14]) * 48, 8), 48)
-    kept = keep[mine, :] + recv[mine, :]
-    keep_out[...] = kept
-    send[0:48, :] = keep[other, :] + recv[other, :]
-    sums = small[...] + recv[96:144, :]
-    small_out[...] = sums
-    send[48:96, :] = sums
-
-
-def last_kernel(sc, keep, small, recv, keep_out, small_out, send):
+    for index, send in zip(others, (s0, s1, s2)):
+        send[0:48, :] = turned[pl.ds(pl.multiple_of(index * 48, 8), 48), :]
+        send[48:96, :] = small_out[...]
+
+
+def last_kernel(sc, keep, small, r0, r1, r2, keep_out, small_out, send):
     del sc
-    kept = keep[...] + recv[0:48, :]
-    sums = small[...] + recv[48:96, :]
+    kept = keep[...] + r0[0:48, :] + r1[0:48, :] + r2[0:48, :]
+    sums = add_small(small, (r0, r1, r2), 48)
     keep_out[...] = kept
     small_out[...] = sums
     send[0:48, :] = kept
@@ -376,26 +386,21 @@
     )(sc, *args)
 
 
-def swap(value, axis, bit):
-    count = 8 if axis == "bulk" else 32
-    return lax.ppermute(value, axis, [(i, i ^ bit) for i in range(count)])
+def swap(value, wide, bulk=0):
+    return lax.ppermute(value, ("wide", "bulk"), [(i, i ^ (8 * wide + bulk)) for i in range(256)])
 
 
 def route(rows, sizes, masks):
-    high_z, high_y = masks & 4, masks & 16
-    steps = (
-        (1, (masks & 1) ^ (high_z // 4)),
-        (2, (masks & 2) ^ (high_z // 2)),
-        (7, high_z),
-        (8, (masks & 8) ^ (high_y // 2)),
-        (24, high_y),
-    )
+    z_high, y_high = (masks & 4) // 4, (masks & 16) // 16
+    z_low, z_mid, y_low = (masks & 1) ^ z_high, (masks & 2) // 2 ^ z_high, (masks & 8) // 8 ^ y_high
     units = sizes // TAPS
     extra = jnp.stack([(units // 32).astype(BF16), (units % 32).astype(BF16)], axis=1)
     value = jnp.concatenate([rows, jnp.pad(extra, ((0, 0), (0, 126)))], axis=1)
-    for bit, used in steps:
-        moved = swap(value, "wide", bit)
-        value = jnp.where((used != 0)[:, None], moved, value)
+    for a, use_a, b, use_b in ((1, z_low, 8, y_low), (2, z_mid, 24, y_high)):
+        got_a, got_b, got_both = swap(value, a), swap(value, b), swap(value, a ^ b)
+        far, use_a = (use_b != 0)[:, None], (use_a != 0)[:, None]
+        value = jnp.where(use_a, jnp.where(far, got_both, got_a), jnp.where(far, got_b, value))
+    value = jnp.where((z_high != 0)[:, None], swap(value, 7), value)
     tail = value[:, -128:-126].astype(F32)
     return value[:, :-128], (tail[:, 0] * 32.0 + tail[:, 1]).astype(jnp.int32)
 
@@ -429,26 +434,19 @@
         rows, units, jnp.bitwise_xor(masks, me), places, cotangent[0, 0],
         conv_first, norm_gain, norm_bias, conv_second,
     )
-    n = 1024
-    recv = swap(send, "bulk", 1)
-    for flag, axis, bit, coarse in ((9, "bulk", 2, True), (10, "wide", 8, True), (11, "bulk", 6, True), (12, "wide", 24, False)):
-        half = n // 2
-        out = [
-            ((half, 384), F32), ((16, 384), F32),
-            ((half + 32, 384), BF16) if coarse else ((half + 16, 384), F32),
-        ]
-        kernel = functools.partial(combine_kernel, n, flag, coarse)
-        keep, small, send = small_call(kernel, "combine%d" % n, sc, (keep, small, recv), out)
-        recv = swap(send, axis, bit)
-        n = half
-    out = [((96, 128), F32), ((48, 128), F32), ((144, 128), F32)]
-    keep, small, send = small_call(turn_kernel, "turn", sc, (keep, small, recv), out)
-    recv = swap(send, "wide", 1)
-    out = [((48, 128), F32), ((48, 128), F32), ((96, 128), F32)]
-    keep, small, send = small_call(middle_kernel, "middle", sc, (keep, small, recv), out)
-    recv = swap(send, "wide", 2)
-    keep, small, send = small_call(last_kernel, "last", sc, (keep, small, recv), out)
-    recv = swap(send, "wide", 7)
+    recv = [swap(send, 0, 1)]
+    for n, flag, y, x in ((1024, 9, 8, 2), (256, 11, 24, 6)):
+        out = [((n // 4, 384), F32), ((16, 384), F32)] + [((n // 4 + 32, 384), BF16)] * 3
+        kernel = functools.partial(combine_kernel, n, len(recv), flag)
+        keep, small, *sends = small_call(kernel, "combine%d" % n, sc, (keep, small, *recv), out)
+        recv = [swap(sends[0], y), swap(sends[1], 0, x), swap(sends[2], y, x)]
+    out = [((48, 128), F32), ((48, 128), F32)] + [((96, 128), F32)] * 3
+    keep, small, *sends = small_call(
+        turn_kernel, "turn", sc, (keep, small, *recv), out, [pltpu.VMEM((192, 128), F32)]
+    )
+    recv = [swap(sends[0], 2), swap(sends[1], 1), swap(sends[2], 3)]
+    keep, small, send = small_call(last_kernel, "last", sc, (keep, small, *recv), out[:3])
+    recv = swap(send, 7)
     out = [((48, 64), F32), ((10, CH), F32), ((1, CH), F32), ((1, CH), F32)]
     second, first, g_gain, g_bias = small_call(
         final_kernel, "final", sc, (keep, small, recv), out, [pltpu.VMEM((16, CH), F32)], jax.ShapeDtypeStruct

time: 126 us -> 115 us (0.913)
  waiting for transfers between devices: 42.9 us -> 33.5 us
  Pallas kernels: 36.4 us -> 34.7 us
    ppermute x13 -> x18, waiting for transfers between devices: 42.9 us -> 33.5 us  [swap(): lax.ppermute(value, ('wide', 'bulk'), [(i, i ^ 8 * wide + bulk) for i in...]
    pallas_call x8 -> x5, Pallas kernels: 5.76 us -> 4.05 us  [small_call(): pl.pallas_call(kernel, in_specs=[pl.BlockSpec(memory_space=pltpu.SMEM)] +...]
    ppermute x13 -> x18, starting transfers between devices: 33 us -> 32.6 us  [swap(): lax.ppermute(value, ('wide', 'bulk'), [(i, i ^ 8 * wide + bulk) for i in...]
  transfers between devices with their start and end apart: 13 -> 18, of which waited for: 13 -> 15; matrix products, arithmetic and copies ran while one was open for 3% -> 3% of each run, Pallas kernels for 0% -> 0%
where the time goes in v4:
time: 115 us; the launch traced here: 114 us
  Pallas kernels  34.7 us (30%)
  waiting for transfers between devices  33.5 us (29%)
  starting transfers between devices  32.6 us (28%)
  local copies, waits for them, and re-layouts  6.53 us (6%)
  other arithmetic  5.43 us (5%)
    ppermute x18, waiting for transfers between devices, swap(): lax.ppermute(value, ('wide', 'bulk'), [(i, i ^ 8 * wide + bulk) for i in...  33.5 us
    ppermute x18, starting transfers between devices, swap(): lax.ppermute(value, ('wide', 'bulk'), [(i, i ^ 8 * wide + bulk) for i in...  32.6 us
    pallas_call x1, Pallas kernels, window(): pl.pallas_call(window_kernel, grid_spec=pltpu.PrefetchScalarGridSpec(num_...  30.7 us
    pallas_call x5, Pallas kernels, small_call(): pl.pallas_call(kernel, in_specs=[pl.BlockSpec(memory_space=pltpu.SMEM)] +...  4.05 us
    reshape x1, local copies, waits for them, and re-layouts, local(): u = rows.reshape(SLOTS * GRAN, TAPS)  3.36 us
    unnamed x10, local copies, waits for them, and re-layouts  3.05 us
  transfers between devices with their start and end apart: 18, of which 15 were waited for; matrix products, arithmetic and copies ran while one was open for 3% of the time, Pallas kernels for 0%

profile of v4, /device:TPU:32, one launch (start us, length us, event | category | flops | bytes accessed | tf_op | source)
XLA Modules:
  0.0 113.6 jit_solution(2782429633837821763)
XLA Ops:
  2.4 1.7 %collective-permute-start.2 = (bf16[4,10368]{1,0:T(4,128)(2,1)S(1)}, bf16[4,10368]{1,0:T(4,128)(2,1)S(1)}, u32[]{:S(2)}, u32[]{:S(2)}) collective-permute-start(bf16[4,10368]{1,0:T(4,128)(2,1)S(1)} %fusion.1), channel_id=1, source_target_pairs={{0,64},{1,65},{2,66},{3,67},{4,68},{5,69},{6,70},{7,71},{8,72},{9,... | collective-permute-start | bytes 248840 | tf_op jit(solution)/shard_map/ppermute | solution.py:390
  4.4 1.5 %collective-permute-start = (bf16[4,10368]{1,0:T(4,128)(2,1)S(1)}, bf16[4,10368]{1,0:T(4,128)(2,1)S(1)}, u32[]{:S(2)}, u32[]{:S(2)}) collective-permute-start(bf16[4,10368]{1,0:T(4,128)(2,1)S(1)} %fusion.1), channel_id=1, source_target_pairs={{0,72},{1,73},{2,74},{3,75},{4,76},{5,77},{6,78},{7,79},{8,64},{9,... | collective-permute-start | bytes 248840 | tf_op jit(solution)/shard_map/ppermute | solution.py:390
  6.9 1.9 %collective-permute-done.1 = bf16[4,10368]{1,0:T(4,128)(2,1)S(1)} collective-permute-done((bf16[4,10368]{1,0:T(4,128)(2,1)S(1)}, bf16[4,10368]{1,0:T(4,128)(2,1)S(1)}, u32[]{:S(2)}, u32[]{:S(2)}) %collective-permute-start.1) | collective-permute-done | bytes 82976 | tf_op jit(solution)/shard_map/ppermute | solution.py:390
  10.8 3.0 %collective-permute-start.5 = (bf16[4,10368]{1,0:T(4,128)(2,1)S(1)}, bf16[4,10368]{1,0:T(4,128)(2,1)S(1)}, u32[]{:S(2)}, u32[]{:S(2)}) collective-permute-start(bf16[4,10368]{1,0:T(4,128)(2,1)S(1)} %select_select_fusion.1), channel_id=1, source_target_pairs={{0,192},{1,193},{2,194},{3,195},{4,196},{5,197},{6,198},{7,199},{8... | collective-permute-start | bytes 248840 | tf_op jit(solution)/shard_map/ppermute | solution.py:390
  13.8 3.3 %collective-permute-start.4 = (bf16[4,10368]{1,0:T(4,128)(2,1)S(1)}, bf16[4,10368]{1,0:T(4,128)(2,1)S(1)}, u32[]{:S(2)}, u32[]{:S(2)}) collective-permute-start(bf16[4,10368]{1,0:T(4,128)(2,1)S(1)} %select_select_fusion.1), channel_id=1, source_target_pairs={{0,16},{1,17},{2,18},{3,19},{4,20},{5,21},{6,22},{7,23},{8,24},{9,... | collective-permute-start | bytes 248840 | tf_op jit(solution)/shard_map/ppermute | solution.py:390
  17.8 1.7 %copy.15 = bf16[1536,512]{0,1:T(8,128)(2,1)S(1)} copy(bf16[1536,512]{1,0:T(8,128)(2,1)} %w2.1) | data formatting | bytes 3145728 | tf_op args[7]
  19.6 1.9 %collective-permute-done.4 = bf16[4,10368]{1,0:T(4,128)(2,1)S(1)} collective-permute-done((bf16[4,10368]{1,0:T(4,128)(2,1)S(1)}, bf16[4,10368]{1,0:T(4,128)(2,1)S(1)}, u32[]{:S(2)}, u32[]{:S(2)}) %collective-permute-start.4) | collective-permute-done | bytes 82976 | tf_op jit(solution)/shard_map/ppermute | solution.py:390
  21.5 3.3 %collective-permute-done.3 = bf16[4,10368]{1,0:T(4,128)(2,1)} collective-permute-done((bf16[4,10368]{1,0:T(4,128)(2,1)S(1)}, bf16[4,10368]{1,0:T(4,128)(2,1)}, u32[]{:S(2)}, u32[]{:S(2)}) %collective-permute-start.3) | collective-permute-done | bytes 82976 | tf_op jit(solution)/shard_map/ppermute | solution.py:390
  25.8 4.3 %collective-permute-start.6 = (bf16[4,10368]{1,0:T(4,128)(2,1)S(1)}, bf16[4,10368]{1,0:T(4,128)(2,1)S(1)}, u32[]{:S(2)}, u32[]{:S(2)}) collective-permute-start(bf16[4,10368]{1,0:T(4,128)(2,1)S(1)} %select_select_fusion), channel_id=1, source_target_pairs={{0,56},{1,57},{2,58},{3,59},{4,60},{5,61},{6,62},{7,63},{8,48},{9,... | collective-permute-start | bytes 248840 | tf_op jit(solution)/shard_map/ppermute | solution.py:390
  30.1 3.5 %collective-permute-done.6 = bf16[4,10368]{1,0:T(4,128)(2,1)S(1)} collective-permute-done((bf16[4,10368]{1,0:T(4,128)(2,1)S(1)}, bf16[4,10368]{1,0:T(4,128)(2,1)S(1)}, u32[]{:S(2)}, u32[]{:S(2)}) %collective-permute-start.6) | collective-permute-done | bytes 82976 | tf_op jit(solution)/shard_map/ppermute | solution.py:390
  33.9 3.4 %reshape.252.u = bf16[4096,10]{1,0:T(8,128)(2,1)} reshape(bf16[4,10240]{1,0:T(4,128)(2,1)S(1)} %slice.17) | data formatting | bytes 163840 | tf_op jit(solution)/shard_map/reshape | solution.py:416
  38.6 30.7 %window.1 = (f32[1024,384]{1,0:T(8,128)S(1)}, bf16[1056,384]{1,0:T(8,128)(2,1)S(1)}, f32[16,384]{1,0:T(8,128)S(1)}) custom-call(s32[16]{0:T(128)S(1)} %concatenate.10.sc, bf16[4096,10]{1,0:T(8,128)(2,1)S(1)} %copy-done.1, bf16[2048,512]{1,0:T(8,128)(2,1)} %bitcast.70, f32[32,512]{1,0:T(8,128)S(1)} %select_maximum_fusion.wst, f32[1,512]{1,0:T(1,128)S(1)} %bitcast.66, ...), custom_call_target="tpu_custom_call" | custom-call | flops 14000000000 | bytes 10000000 | tf_op jit(solution)/shard_map/window/pallas_call | solution.py:341
  69.4 2.3 %collective-permute-done.7.refs_0_ = bf16[1056,384]{1,0:T(8,128)(2,1)S(1)} collective-permute-done((bf16[1056,384]{1,0:T(8,128)(2,1)S(1)}, bf16[1056,384]{1,0:T(8,128)(2,1)S(1)}, u32[]{:S(2)}, u32[]{:S(2)}) %collective-permute-start.7) | collective-permute-done | bytes 811040 | tf_op jit(solution)/shard_map/ppermute | solution.py:390
  72.6 1.6 %collective-permute-start.9 = (bf16[288,384]{1,0:T(8,128)(2,1)S(1)}, bf16[288,384]{1,0:T(8,128)(2,1)S(1)}, u32[]{:S(2)}, u32[]{:S(2)}) collective-permute-start(bf16[288,384]{1,0:T(8,128)(2,1)S(1)} %get-tuple-element.35), channel_id=1, source_target_pairs={{0,2},{1,3},{2,0},{3,1},{4,6},{5,7},{6,4},{7,5},{8,10},{9,11},{10,... | collective-permute-start | bytes 663560 | tf_op jit(solution)/shard_map/ppermute | solution.py:390
  74.2 1.9 %collective-permute-start.10 = (bf16[288,384]{1,0:T(8,128)(2,1)S(1)}, bf16[288,384]{1,0:T(8,128)(2,1)S(1)}, u32[]{:S(2)}, u32[]{:S(2)}) collective-permute-start(bf16[288,384]{1,0:T(8,128)(2,1)S(1)} %get-tuple-element.36), channel_id=1, source_target_pairs={{0,66},{1,67},{2,64},{3,65},{4,70},{5,71},{6,68},{7,69},{8,74},{9,... | collective-permute-start | bytes 663560 | tf_op jit(solution)/shard_map/ppermute | solution.py:390
  76.1 4.0 %collective-permute-done.8.refs_0_ = bf16[288,384]{1,0:T(8,128)(2,1)S(1)} collective-permute-done((bf16[288,384]{1,0:T(8,128)(2,1)S(1)}, bf16[288,384]{1,0:T(8,128)(2,1)S(1)}, u32[]{:S(2)}, u32[]{:S(2)}) %collective-permute-start.8) | collective-permute-done | bytes 221216 | tf_op jit(solution)/shard_map/ppermute | solution.py:390
  81.0 5.0 %collective-permute-done.10.refs_2_ = bf16[288,384]{1,0:T(8,128)(2,1)S(1)} collective-permute-done((bf16[288,384]{1,0:T(8,128)(2,1)S(1)}, bf16[288,384]{1,0:T(8,128)(2,1)S(1)}, u32[]{:S(2)}, u32[]{:S(2)}) %collective-permute-start.10) | collective-permute-done | bytes 221216 | tf_op jit(solution)/shard_map/ppermute | solution.py:390
  87.0 2.8 %collective-permute-start.12 = (bf16[96,384]{1,0:T(8,128)(2,1)S(1)}, bf16[96,384]{1,0:T(8,128)(2,1)S(1)}, u32[]{:S(2)}, u32[]{:S(2)}) collective-permute-start(bf16[96,384]{1,0:T(8,128)(2,1)S(1)} %get-tuple-element.40), channel_id=1, source_target_pairs={{0,6},{1,7},{2,4},{3,5},{4,2},{5,3},{6,0},{7,1},{8,14},{9,15},{10,... | collective-permute-start | bytes 221192 | tf_op jit(solution)/shard_map/ppermute | solution.py:390
  89.7 2.9 %collective-permute-start.13 = (bf16[96,384]{1,0:T(8,128)(2,1)S(1)}, bf16[96,384]{1,0:T(8,128)(2,1)S(1)}, u32[]{:S(2)}, u32[]{:S(2)}) collective-permute-start(bf16[96,384]{1,0:T(8,128)(2,1)S(1)} %get-tuple-element.41), channel_id=1, source_target_pairs={{0,198},{1,199},{2,196},{3,197},{4,194},{5,195},{6,192},{7,193},{8... | collective-permute-start | bytes 221192 | tf_op jit(solution)/shard_map/ppermute | solution.py:390
  92.6 4.8 %collective-permute-done.13.r2 = bf16[96,384]{1,0:T(8,128)(2,1)S(1)} collective-permute-done((bf16[96,384]{1,0:T(8,128)(2,1)S(1)}, bf16[96,384]{1,0:T(8,128)(2,1)S(1)}, u32[]{:S(2)}, u32[]{:S(2)}) %collective-permute-start.13) | collective-permute-done | bytes 73760 | tf_op jit(solution)/shard_map/ppermute | solution.py:390
  98.2 2.1 %collective-permute-start.14 = (f32[96,128]{1,0:T(8,128)S(1)}, f32[96,128]{1,0:T(8,128)S(1)}, u32[]{:S(2)}, u32[]{:S(2)}) collective-permute-start(f32[96,128]{1,0:T(8,128)S(1)} %get-tuple-element.44), channel_id=1, source_target_pairs={{0,16},{1,17},{2,18},{3,19},{4,20},{5,21},{6,22},{7,23},{8,24},{9,... | collective-permute-start | bytes 147464 | tf_op jit(solution)/shard_map/ppermute | solution.py:390
  101.8 1.5 %collective-permute-done.14.r0 = f32[96,128]{1,0:T(8,128)S(1)} collective-permute-done((f32[96,128]{1,0:T(8,128)S(1)}, f32[96,128]{1,0:T(8,128)S(1)}, u32[]{:S(2)}, u32[]{:S(2)}) %collective-permute-start.14) | collective-permute-done | bytes 49184 | tf_op jit(solution)/shard_map/ppermute | solution.py:390
  105.0 5.2 %collective-permute-start.17 = (f32[96,128]{1,0:T(8,128)S(1)}, f32[96,128]{1,0:T(8,128)S(1)}, u32[]{:S(2)}, u32[]{:S(2)}) collective-permute-start(f32[96,128]{1,0:T(8,128)S(1)} %get-tuple-element.49), channel_id=1, source_target_pairs={{0,56},{1,57},{2,58},{3,59},{4,60},{5,61},{6,62},{7,63},{8,48},{9,... | collective-permute-start | bytes 147464 | tf_op jit(solution)/shard_map/ppermute | solution.py:390
  110.2 2.1 %collective-permute-done.17.recv = f32[96,128]{1,0:T(8,128)S(1)} collective-permute-done((f32[96,128]{1,0:T(8,128)S(1)}, f32[96,128]{1,0:T(8,128)S(1)}, u32[]{:S(2)}, u32[]{:S(2)}) %collective-permute-start.17) | collective-permute-done | bytes 49184 | tf_op jit(solution)/shard_map/ppermute | solution.py:390
  (45 shorter events, 16.6 us)
Async XLA Ops:
  2.4 4.5 %collective-permute-start.2 = (bf16[4,10368]{1,0:T(4,128)(2,1)S(1)}, bf16[4,10368]{1,0:T(4,128)(2,1)S(1)}, u32[]{:S(2)}, u32[]{:S(2)}) collective-permute-start(bf16[4,10368]{1,0:T(4,128)(2,1)S(1)} %fusion.1), channel_id=1, source_target_pairs={{0,64},{1,65},{2,66},{3,67},{4,68},{5,69},{6,70},{7,71},{8,72},{9,... | collective-permute-start | bytes 248840 | tf_op jit(solution)/shard_map/ppermute | solution.py:390
  4.0 4.8 %collective-permute-start.1 = (bf16[4,10368]{1,0:T(4,128)(2,1)S(1)}, bf16[4,10368]{1,0:T(4,128)(2,1)S(1)}, u32[]{:S(2)}, u32[]{:S(2)}) collective-permute-start(bf16[4,10368]{1,0:T(4,128)(2,1)S(1)} %fusion.1), channel_id=1, source_target_pairs={{0,8},{1,9},{2,10},{3,11},{4,12},{5,13},{6,14},{7,15},{8,0},{9,1},... | collective-permute-start | bytes 248840 | tf_op jit(solution)/shard_map/ppermute | solution.py:390
  4.4 5.4 %collective-permute-start = (bf16[4,10368]{1,0:T(4,128)(2,1)S(1)}, bf16[4,10368]{1,0:T(4,128)(2,1)S(1)}, u32[]{:S(2)}, u32[]{:S(2)}) collective-permute-start(bf16[4,10368]{1,0:T(4,128)(2,1)S(1)} %fusion.1), channel_id=1, source_target_pairs={{0,72},{1,73},{2,74},{3,75},{4,76},{5,77},{6,78},{7,79},{8,64},{9,... | collective-permute-start | bytes 248840 | tf_op jit(solution)/shard_map/ppermute | solution.py:390
  10.8 8.8 %collective-permute-start.5 = (bf16[4,10368]{1,0:T(4,128)(2,1)S(1)}, bf16[4,10368]{1,0:T(4,128)(2,1)S(1)}, u32[]{:S(2)}, u32[]{:S(2)}) collective-permute-start(bf16[4,10368]{1,0:T(4,128)(2,1)S(1)} %select_select_fusion.1), channel_id=1, source_target_pairs={{0,192},{1,193},{2,194},{3,195},{4,196},{5,197},{6,198},{7,199},{8... | collective-permute-start | bytes 248840 | tf_op jit(solution)/shard_map/ppermute | solution.py:390
  13.8 7.7 %collective-permute-start.4 = (bf16[4,10368]{1,0:T(4,128)(2,1)S(1)}, bf16[4,10368]{1,0:T(4,128)(2,1)S(1)}, u32[]{:S(2)}, u32[]{:S(2)}) collective-permute-start(bf16[4,10368]{1,0:T(4,128)(2,1)S(1)} %select_select_fusion.1), channel_id=1, source_target_pairs={{0,16},{1,17},{2,18},{3,19},{4,20},{5,21},{6,22},{7,23},{8,24},{9,... | collective-permute-start | bytes 248840 | tf_op jit(solution)/shard_map/ppermute | solution.py:390
  17.1 7.7 %collective-permute-start.3 = (bf16[4,10368]{1,0:T(4,128)(2,1)S(1)}, bf16[4,10368]{1,0:T(4,128)(2,1)}, u32[]{:S(2)}, u32[]{:S(2)}) collective-permute-start(bf16[4,10368]{1,0:T(4,128)(2,1)S(1)} %select_select_fusion.1), channel_id=1, source_target_pairs={{0,208},{1,209},{2,210},{3,211},{4,212},{5,213},{6,214},{7,215},{8... | collective-permute-start | bytes 248840 | tf_op jit(solution)/shard_map/ppermute | solution.py:390
  19.5 17.9 %copy-start = (bf16[1536,512]{1,0:T(8,128)(2,1)S(1)}, bf16[1536,512]{1,0:T(8,128)(2,1)}, u32[]{:S(2)}) copy-start(bf16[1536,512]{1,0:T(8,128)(2,1)} %w2.1) | copy-start | bytes 4718596
  19.5 17.9 %copy-start.2 = (f32[512]{0:T(512)S(1)}, f32[512]{0:T(512)}, u32[]{:S(2)}) copy-start(f32[512]{0:T(512)} %param.13) | copy-start | bytes 6148
  19.5 17.9 %copy-start.3 = (f32[512]{0:T(512)S(1)}, f32[512]{0:T(512)}, u32[]{:S(2)}) copy-start(f32[512]{0:T(512)} %param.14) | copy-start | bytes 6148
  25.8 7.8 %collective-permute-start.6 = (bf16[4,10368]{1,0:T(4,128)(2,1)S(1)}, bf16[4,10368]{1,0:T(4,128)(2,1)S(1)}, u32[]{:S(2)}, u32[]{:S(2)}) collective-permute-start(bf16[4,10368]{1,0:T(4,128)(2,1)S(1)} %select_select_fusion), channel_id=1, source_target_pairs={{0,56},{1,57},{2,58},{3,59},{4,60},{5,61},{6,62},{7,63},{8,48},{9,... | collective-permute-start | bytes 248840 | tf_op jit(solution)/shard_map/ppermute | solution.py:390
  37.4 1.2 %copy-start.1 = (bf16[4096,10]{1,0:T(8,128)(2,1)S(1)}, bf16[4096,10]{1,0:T(8,128)(2,1)}, u32[]{:S(2)}) copy-start(bf16[4096,10]{1,0:T(8,128)(2,1)} %reshape.252.u) | copy-start | bytes 245764
  69.3 2.4 %collective-permute-start.7 = (bf16[1056,384]{1,0:T(8,128)(2,1)S(1)}, bf16[1056,384]{1,0:T(8,128)(2,1)S(1)}, u32[]{:S(2)}, u32[]{:S(2)}) collective-permute-start(bf16[1056,384]{1,0:T(8,128)(2,1)S(1)} %get-tuple-element.31), channel_id=1, source_target_pairs={{0,1},{1,0},{2,3},{3,2},{4,5},{5,4},{6,7},{7,6},{8,9},{9,8},{10,11... | collective-permute-start | bytes 2433032 | tf_op jit(solution)/shard_map/ppermute | solution.py:390
  72.5 7.6 %collective-permute-start.8 = (bf16[288,384]{1,0:T(8,128)(2,1)S(1)}, bf16[288,384]{1,0:T(8,128)(2,1)S(1)}, u32[]{:S(2)}, u32[]{:S(2)}) collective-permute-start(bf16[288,384]{1,0:T(8,128)(2,1)S(1)} %get-tuple-element.34), channel_id=1, source_target_pairs={{0,64},{1,65},{2,66},{3,67},{4,68},{5,69},{6,70},{7,71},{8,72},{9,... | collective-permute-start | bytes 663560 | tf_op jit(solution)/shard_map/ppermute | solution.py:390
  72.6 8.4 %collective-permute-start.9 = (bf16[288,384]{1,0:T(8,128)(2,1)S(1)}, bf16[288,384]{1,0:T(8,128)(2,1)S(1)}, u32[]{:S(2)}, u32[]{:S(2)}) collective-permute-start(bf16[288,384]{1,0:T(8,128)(2,1)S(1)} %get-tuple-element.35), channel_id=1, source_target_pairs={{0,2},{1,3},{2,0},{3,1},{4,6},{5,7},{6,4},{7,5},{8,10},{9,11},{10,... | collective-permute-start | bytes 663560 | tf_op jit(solution)/shard_map/ppermute | solution.py:390
  74.2 11.8 %collective-permute-start.10 = (bf16[288,384]{1,0:T(8,128)(2,1)S(1)}, bf16[288,384]{1,0:T(8,128)(2,1)S(1)}, u32[]{:S(2)}, u32[]{:S(2)}) collective-permute-start(bf16[288,384]{1,0:T(8,128)(2,1)S(1)} %get-tuple-element.36), channel_id=1, source_target_pairs={{0,66},{1,67},{2,64},{3,65},{4,70},{5,71},{6,68},{7,69},{8,74},{9,... | collective-permute-start | bytes 663560 | tf_op jit(solution)/shard_map/ppermute | solution.py:390
  86.6 6.0 %collective-permute-start.11 = (bf16[96,384]{1,0:T(8,128)(2,1)S(1)}, bf16[96,384]{1,0:T(8,128)(2,1)S(1)}, u32[]{:S(2)}, u32[]{:S(2)}) collective-permute-start(bf16[96,384]{1,0:T(8,128)(2,1)S(1)} %get-tuple-element.39), channel_id=1, source_target_pairs={{0,192},{1,193},{2,194},{3,195},{4,196},{5,197},{6,198},{7,199},{8... | collective-permute-start | bytes 221192 | tf_op jit(solution)/shard_map/ppermute | solution.py:390
  87.0 5.7 %collective-permute-start.12 = (bf16[96,384]{1,0:T(8,128)(2,1)S(1)}, bf16[96,384]{1,0:T(8,128)(2,1)S(1)}, u32[]{:S(2)}, u32[]{:S(2)}) collective-permute-start(bf16[96,384]{1,0:T(8,128)(2,1)S(1)} %get-tuple-element.40), channel_id=1, source_target_pairs={{0,6},{1,7},{2,4},{3,5},{4,2},{5,3},{6,0},{7,1},{8,14},{9,15},{10,... | collective-permute-start | bytes 221192 | tf_op jit(solution)/shard_map/ppermute | solution.py:390
  89.7 7.7 %collective-permute-start.13 = (bf16[96,384]{1,0:T(8,128)(2,1)S(1)}, bf16[96,384]{1,0:T(8,128)(2,1)S(1)}, u32[]{:S(2)}, u32[]{:S(2)}) collective-permute-start(bf16[96,384]{1,0:T(8,128)(2,1)S(1)} %get-tuple-element.41), channel_id=1, source_target_pairs={{0,198},{1,199},{2,196},{3,197},{4,194},{5,195},{6,192},{7,193},{8... | collective-permute-start | bytes 221192 | tf_op jit(solution)/shard_map/ppermute | solution.py:390
  98.2 5.1 %collective-permute-start.14 = (f32[96,128]{1,0:T(8,128)S(1)}, f32[96,128]{1,0:T(8,128)S(1)}, u32[]{:S(2)}, u32[]{:S(2)}) collective-permute-start(f32[96,128]{1,0:T(8,128)S(1)} %get-tuple-element.44), channel_id=1, source_target_pairs={{0,16},{1,17},{2,18},{3,19},{4,20},{5,21},{6,22},{7,23},{8,24},{9,... | collective-permute-start | bytes 147464 | tf_op jit(solution)/shard_map/ppermute | solution.py:390
  100.3 4.1 %collective-permute-start.15 = (f32[96,128]{1,0:T(8,128)S(1)}, f32[96,128]{1,0:T(8,128)S(1)}, u32[]{:S(2)}, u32[]{:S(2)}) collective-permute-start(f32[96,128]{1,0:T(8,128)S(1)} %get-tuple-element.45), channel_id=1, source_target_pairs={{0,8},{1,9},{2,10},{3,11},{4,12},{5,13},{6,14},{7,15},{8,0},{9,1},... | collective-permute-start | bytes 147464 | tf_op jit(solution)/shard_map/ppermute | solution.py:390
  100.4 4.1 %collective-permute-start.16 = (f32[96,128]{1,0:T(8,128)S(1)}, f32[96,128]{1,0:T(8,128)S(1)}, u32[]{:S(2)}, u32[]{:S(2)}) collective-permute-start(f32[96,128]{1,0:T(8,128)S(1)} %get-tuple-element.46), channel_id=1, source_target_pairs={{0,24},{1,25},{2,26},{3,27},{4,28},{5,29},{6,30},{7,31},{8,16},{9,... | collective-permute-start | bytes 147464 | tf_op jit(solution)/shard_map/ppermute | solution.py:390
  105.0 7.3 %collective-permute-start.17 = (f32[96,128]{1,0:T(8,128)S(1)}, f32[96,128]{1,0:T(8,128)S(1)}, u32[]{:S(2)}, u32[]{:S(2)}) collective-permute-start(f32[96,128]{1,0:T(8,128)S(1)} %get-tuple-element.49), channel_id=1, source_target_pairs={{0,56},{1,57},{2,58},{3,59},{4,60},{5,61},{6,62},{7,63},{8,48},{9,... | collective-permute-start | bytes 147464 | tf_op jit(solution)/shard_map/ppermute | solution.py:390

commit v5 on v4

--- a/solution.py
+++ b/solution.py
@@ -15,7 +15,7 @@
 GRAN = 1024
 ROWS = 2048
 CH = 512
-BLK = 256
+BLK = 512
 BLOCKS = [
     (2 * xh + (xl ^ xh), 2 * yh + (yl ^ yh)) for xl in range(2) for yl in range(2) for xh in range(2) for yh in range(2)
 ]
@@ -32,16 +32,8 @@
 
 
 def cdf_slope(v):
-    e = jnp.exp2(v * v * (-0.5 * 1.4426950408889634))
-    d = 1.0 + jnp.abs(v) * (0.3275911 * 0.7071067811865476)
-    r = pl.reciprocal(d, approx=True)
-    t = r * (2.0 - d * r)
-    poly = 0.5 * 1.061405429
-    for c in (-1.453152027, 1.421413741, -0.284496736, 0.254829592):
-        poly = poly * t + 0.5 * c
-    tail = poly * t * e
-    cdf = jnp.where(v < 0.0, tail, 1.0 - tail)
-    return cdf, cdf + v * (e * 0.3989422804014327)
+    cdf = 0.5 + 0.5 * lax.erf(v * 0.7071067811865476)
+    return cdf, cdf + v * (jnp.exp2(v * v * (-0.5 * 1.4426950408889634)) * 0.3989422804014327)
 
 
 def plan(sc):
@@ -74,20 +66,31 @@
 
 
 def window_kernel(
-    sc, u, cot, wst, gain, bias, w2, wt,
+    sc, u, perm, cot, wst, gain, bias, w2, wt,
     keep, send, small,
-    buf, xd, xbig, xs, wbig, acc, nst, tc, im, grads, carry,
+    wide, lanes16, buf, xd, xbig, xs, wbig, acc, nst, tc, im, grads, carry,
 ):
     step = pl.program_id(0)
     segs = plan(sc)
 
     @pl.when(step == 0)
     def _():
-        buf[...] = jnp.zeros_like(buf)
+        samples = u[:, : GRAN * TAPS].astype(F32)
+        for s in range(SLOTS):
+            for r in range(16):
+                wide[16 * s + r : 16 * s + r + 1, :] = samples[s : s + 1, 640 * r : 640 * (r + 1)]
+        lanes16[...] = dot(wide[...].astype(BF16), perm[...])
+        buf[pl.ds(ROWS, 8), :] = jnp.zeros((8, 128), F32)
+        own = (
+            lax.broadcasted_iota(jnp.int32, (8, 1024), 1) % 128 // 16
+            == lax.broadcasted_iota(jnp.int32, (8, 1024), 0)
+        )
         for slot, off, _n in segs:
-            piece = u[pl.ds(pl.multiple_of(slot * GRAN, GRAN), GRAN), :].astype(F32)
-            buf[pl.ds(off, GRAN), 0:TAPS] = piece
-        src = lax.broadcasted_iota(jnp.int32, (128, 256), 0)
+            for r in range(16):
+                line = jnp.where(own, lanes16[pl.ds(16 * slot + r, 1), :], 0.0)
+                for j in range(8):
+                    buf[pl.ds(off + 64 * r + 8 * j, 8), :] = line[:, 128 * j : 128 * j + 128]
+        src = lax.broadcasted_iota(jnp.int32, (128, 256), 0) % 16
         tap = lax.broadcasted_iota(jnp.int32, (128, 256), 1) % 16
         r0 = ((tap == src) & (src < TAPS)).astype(F32).astype(BF16)
         r1 = ((tap == src + TAPS) & (src < 5)).astype(F32).astype(BF16)
@@ -120,15 +123,19 @@
             xs[1, pl.ds(base, BLK), :] = jnp.where(odd == 1, full, 0.0).astype(BF16)
         xbig[pl.ds(ROWS, 16), :] = jnp.zeros((16, 256), BF16)
         mu = sums / count
-        moment = jnp.zeros((128, 128), F32)
+        main = jnp.zeros((128, 128), F32)
+        rest = jnp.zeros((128, 128), F32)
         for rb in range(ROWS // BLK):
             base = rb * BLK
             row = lax.broadcasted_iota(jnp.int32, (BLK, 1), 0) + base
             d = jnp.where((row >= lo_d) & (row < hi_d), xd[pl.ds(base, BLK), :] - mu, 0.0)
-            moment = moment + dot_t(d, d, HIGHEST)
+            high = d.astype(BF16)
+            low = (d - high.astype(F32)).astype(BF16)
+            main = main + dot_t(high, high)
+            rest = rest + dot_t(high, low)
         ri = lax.broadcasted_iota(jnp.int32, (128, 128), 0)
         ci = lax.broadcasted_iota(jnp.int32, (128, 128), 1)
-        moment = jnp.where(ri // 16 == ci // 16, moment, 0.0)
+        moment = jnp.where(ri // 16 == ci // 16, main + (rest + rest.T), 0.0)
         wrow = jnp.concatenate([wst[...]] * SLOTS, axis=0)
         v = dot(moment, wrow, HIGHEST)
         block8 = (
@@ -335,7 +342,7 @@
     return pltpu.with_memory_space_constraint(value, pltpu.VMEM)
 
 
-def window(sc, u, cot, wst, gain, bias, w2, wt):
+def window(sc, u, perm, cot, wst, gain, bias, w2, wt):
     whole = pl.BlockSpec(memory_space=pltpu.VMEM)
     shapes = [((1024, 384), F32), ((1056, 384), BF16), ((16, 384), F32)]
     return pl.pallas_call(
@@ -344,12 +351,14 @@
             num_scalar_prefetch=1,
             grid=(ROWS // BLK,),
             in_specs=[
-                whole,
+                whole, whole,
                 pl.BlockSpec((BLK, CH), lambda i, sc: (i, 0)),
                 whole, whole, whole, whole, whole,
             ],
             out_specs=[pl.BlockSpec(memory_space=pltpu.VMEM)] * len(shapes),
             scratch_shapes=[
+                pltpu.VMEM((64, 640), F32),
+                pltpu.VMEM((64, 1024), F32),
                 pltpu.VMEM((ROWS + GRAN, 128), F32),
                 pltpu.VMEM((ROWS, 128), F32),
                 pltpu.VMEM((ROWS + 16, 256), BF16),
@@ -368,7 +377,7 @@
         cost_estimate=pl.CostEstimate(flops=14 * 10**9, bytes_accessed=10 * 10**6, transcendentals=0),
         name="window",
     )(
-        sc, in_vmem(u), pltpu.with_memory_space_constraint(cot, pltpu.HBM),
+        sc, in_vmem(u), in_vmem(perm), pltpu.with_memory_space_constraint(cot, pltpu.HBM),
         in_vmem(wst), in_vmem(gain), in_vmem(bias), in_vmem(w2), in_vmem(wt),
     )
 
@@ -402,7 +411,7 @@
         value = jnp.where(use_a, jnp.where(far, got_both, got_a), jnp.where(far, got_b, value))
     value = jnp.where((z_high != 0)[:, None], swap(value, 7), value)
     tail = value[:, -128:-126].astype(F32)
-    return value[:, :-128], (tail[:, 0] * 32.0 + tail[:, 1]).astype(jnp.int32)
+    return value, (tail[:, 0] * 32.0 + tail[:, 1]).astype(jnp.int32)
 
 
 def window_inputs(conv_first):
@@ -413,11 +422,12 @@
 
 
 def local(rows, units, sources, places, cot, conv_first, norm_gain, norm_bias, conv_second):
-    u = rows.reshape(SLOTS * GRAN, TAPS)
+    lane = jnp.arange(1024, dtype=jnp.int32)[None, :]
+    perm = (jnp.arange(640, dtype=jnp.int32)[:, None] == lane // 16 * TAPS + lane % 16) & (lane % 16 < TAPS)
     sc = jnp.concatenate([units, sources, places])
     wst = window_inputs(conv_first)
     gain, bias = norm_gain[None, :], norm_bias[None, :]
-    return sc, window(sc, u, cot, wst, gain, bias, conv_second, conv_second.T)
+    return sc, window(sc, rows, perm.astype(BF16), cot, wst, gain, bias, conv_second, conv_second.T)
 
 
 def per_device(waveforms, owner_of, lengths, cotangent, conv_first, norm_gain, norm_bias, conv_second):

time: 115 us -> 103 us (0.90)
  Pallas kernels: 34.7 us -> 25.2 us
  local copies, waits for them, and re-layouts: 6.53 us -> 2.33 us
  other arithmetic: 5.43 us -> 7.16 us
    pallas_call x1, Pallas kernels: 30.7 us -> 21.2 us  [window(): pl.pallas_call(window_kernel, grid_spec=pltpu.PrefetchScalarGridSpec(num_...]
    reshape x1 -> x0, local copies, waits for them, and re-layouts: 3.36 us -> none  [local(): u = rows.reshape(SLOTS * GRAN, TAPS)]
    convert_element_type x2, other arithmetic: 0.2 us -> 1.78 us  [the longest x1 1.6 us: local(): perm.astype(BF16)]
    unnamed x10 -> x11, local copies, waits for them, and re-layouts: 3.05 us -> 2.04 us
where the time goes in v5:
time: 103 us; the launch traced here: 102 us
  waiting for transfers between devices  33.6 us (33%)
  starting transfers between devices  32.6 us (32%)
  Pallas kernels  25.2 us (24%)
  other arithmetic  7.16 us (7%)
  local copies, waits for them, and re-layouts  2.33 us (2%)
    ppermute x18, waiting for transfers between devices, swap(): lax.ppermute(value, ('wide', 'bulk'), [(i, i ^ 8 * wide + bulk) for i in...  33.6 us
    ppermute x18, starting transfers between devices, swap(): lax.ppermute(value, ('wide', 'bulk'), [(i, i ^ 8 * wide + bulk) for i in...  32.6 us
    pallas_call x1, Pallas kernels, window(): pl.pallas_call(window_kernel, grid_spec=pltpu.PrefetchScalarGridSpec(num_...  21.2 us
    pallas_call x5, Pallas kernels, small_call(): pl.pallas_call(kernel, in_specs=[pl.BlockSpec(memory_space=pltpu.SMEM)] +...  4.05 us
    select_n x2, other arithmetic, route(): jnp.where(use_a, jnp.where(far, got_both, got_a), jnp.where(far, got_b, v...  2.08 us
  transfers between devices with their start and end apart: 18, of which 15 were waited for; matrix products, arithmetic and copies ran while one was open for 3% of the time, Pallas kernels for 0%

profile of v5, /device:TPU:32, one launch (start us, length us, event | category | flops | bytes accessed | tf_op | source)
XLA Modules:
  0.0 101.8 jit_solution(11523162005106704690)
XLA Ops:
  3.3 1.7 %collective-permute-start.2 = (bf16[4,10368]{1,0:T(4,128)(2,1)S(1)}, bf16[4,10368]{1,0:T(4,128)(2,1)S(1)}, u32[]{:S(2)}, u32[]{:S(2)}) collective-permute-start(bf16[4,10368]{1,0:T(4,128)(2,1)S(1)} %pad_maximum_fusion), channel_id=1, source_target_pairs={{0,64},{1,65},{2,66},{3,67},{4,68},{5,69},{6,70},{7,71},{8,72},{9,... | collective-permute-start | bytes 248840 | tf_op jit(solution)/shard_map/ppermute | solution.py:399
  5.4 1.5 %collective-permute-start = (bf16[4,10368]{1,0:T(4,128)(2,1)S(1)}, bf16[4,10368]{1,0:T(4,128)(2,1)S(1)}, u32[]{:S(2)}, u32[]{:S(2)}) collective-permute-start(bf16[4,10368]{1,0:T(4,128)(2,1)S(1)} %pad_maximum_fusion), channel_id=1, source_target_pairs={{0,72},{1,73},{2,74},{3,75},{4,76},{5,77},{6,78},{7,79},{8,64},{9,... | collective-permute-start | bytes 248840 | tf_op jit(solution)/shard_map/ppermute | solution.py:399
  7.9 1.9 %collective-permute-done.1 = bf16[4,10368]{1,0:T(4,128)(2,1)S(1)} collective-permute-done((bf16[4,10368]{1,0:T(4,128)(2,1)S(1)}, bf16[4,10368]{1,0:T(4,128)(2,1)S(1)}, u32[]{:S(2)}, u32[]{:S(2)}) %collective-permute-start.1) | collective-permute-done | bytes 82976 | tf_op jit(solution)/shard_map/ppermute | solution.py:399
  11.8 3.0 %collective-permute-start.5 = (bf16[4,10368]{1,0:T(4,128)(2,1)S(1)}, bf16[4,10368]{1,0:T(4,128)(2,1)S(1)}, u32[]{:S(2)}, u32[]{:S(2)}) collective-permute-start(bf16[4,10368]{1,0:T(4,128)(2,1)S(1)} %select_select_fusion.1), channel_id=1, source_target_pairs={{0,192},{1,193},{2,194},{3,195},{4,196},{5,197},{6,198},{7,199},{8... | collective-permute-start | bytes 248840 | tf_op jit(solution)/shard_map/ppermute | solution.py:399
  14.7 3.3 %collective-permute-start.4 = (bf16[4,10368]{1,0:T(4,128)(2,1)S(1)}, bf16[4,10368]{1,0:T(4,128)(2,1)S(1)}, u32[]{:S(2)}, u32[]{:S(2)}) collective-permute-start(bf16[4,10368]{1,0:T(4,128)(2,1)S(1)} %select_select_fusion.1), channel_id=1, source_target_pairs={{0,16},{1,17},{2,18},{3,19},{4,20},{5,21},{6,22},{7,23},{8,24},{9,... | collective-permute-start | bytes 248840 | tf_op jit(solution)/shard_map/ppermute | solution.py:399
  18.0 1.6 %fusion.1.perm = bf16[640,1024]{1,0:T(8,128)(2,1)} fusion(s32[1024]{0:T(1024)S(1)} %fusion.9, pred[1024]{0:T(1024)(128)(4,1)S(1)} %fusion.10), kind=kLoop, calls=%fused_computation.2 | loop fusion | flops 1966080 | bytes 1315840 | tf_op jit(solution)/shard_map/convert_element_type | solution.py:430
  20.4 2.0 %collective-permute-done.4 = bf16[4,10368]{1,0:T(4,128)(2,1)S(1)} collective-permute-done((bf16[4,10368]{1,0:T(4,128)(2,1)S(1)}, bf16[4,10368]{1,0:T(4,128)(2,1)S(1)}, u32[]{:S(2)}, u32[]{:S(2)}) %collective-permute-start.4) | collective-permute-done | bytes 82976 | tf_op jit(solution)/shard_map/ppermute | solution.py:399
  22.4 3.3 %collective-permute-done.3 = bf16[4,10368]{1,0:T(4,128)(2,1)} collective-permute-done((bf16[4,10368]{1,0:T(4,128)(2,1)S(1)}, bf16[4,10368]{1,0:T(4,128)(2,1)}, u32[]{:S(2)}, u32[]{:S(2)}) %collective-permute-start.3) | collective-permute-done | bytes 82976 | tf_op jit(solution)/shard_map/ppermute | solution.py:399
  26.7 4.3 %collective-permute-start.6 = (bf16[4,10368]{1,0:T(4,128)(2,1)S(1)}, bf16[4,10368]{1,0:T(4,128)(2,1)S(1)}, u32[]{:S(2)}, u32[]{:S(2)}) collective-permute-start(bf16[4,10368]{1,0:T(4,128)(2,1)S(1)} %select_select_fusion), channel_id=1, source_target_pairs={{0,56},{1,57},{2,58},{3,59},{4,60},{5,61},{6,62},{7,63},{8,48},{9,... | collective-permute-start | bytes 248840 | tf_op jit(solution)/shard_map/ppermute | solution.py:399
  31.0 3.5 %collective-permute-done.6 = bf16[4,10368]{1,0:T(4,128)(2,1)S(1)} collective-permute-done((bf16[4,10368]{1,0:T(4,128)(2,1)S(1)}, bf16[4,10368]{1,0:T(4,128)(2,1)S(1)}, u32[]{:S(2)}, u32[]{:S(2)}) %collective-permute-start.6) | collective-permute-done | bytes 82976 | tf_op jit(solution)/shard_map/ppermute | solution.py:399
  36.3 21.2 %window.1 = (f32[1024,384]{1,0:T(8,128)S(1)}, bf16[1056,384]{1,0:T(8,128)(2,1)S(1)}, f32[16,384]{1,0:T(8,128)S(1)}) custom-call(s32[16]{0:T(128)S(1)} %concatenate.10.sc, bf16[4,10368]{1,0:T(4,128)(2,1)S(1)} %broadcast_select_fusion.u, bf16[640,1024]{1,0:T(8,128)(2,1)S(1)} %copy-done.1, bf16[2048,512]{1,0:T(8,128)(2,1)} %bitcast.68, ...), custom_call_target="tpu_custom_call" | custom-call | flops 14000000000 | bytes 10000000 | tf_op jit(solution)/shard_map/window/pallas_call | solution.py:348
  57.6 2.3 %collective-permute-done.7.refs_0_ = bf16[1056,384]{1,0:T(8,128)(2,1)S(1)} collective-permute-done((bf16[1056,384]{1,0:T(8,128)(2,1)S(1)}, bf16[1056,384]{1,0:T(8,128)(2,1)S(1)}, u32[]{:S(2)}, u32[]{:S(2)}) %collective-permute-start.7) | collective-permute-done | bytes 811040 | tf_op jit(solution)/shard_map/ppermute | solution.py:399
  60.8 1.6 %collective-permute-start.9 = (bf16[288,384]{1,0:T(8,128)(2,1)S(1)}, bf16[288,384]{1,0:T(8,128)(2,1)S(1)}, u32[]{:S(2)}, u32[]{:S(2)}) collective-permute-start(bf16[288,384]{1,0:T(8,128)(2,1)S(1)} %get-tuple-element.35), channel_id=1, source_target_pairs={{0,2},{1,3},{2,0},{3,1},{4,6},{5,7},{6,4},{7,5},{8,10},{9,11},{10,... | collective-permute-start | bytes 663560 | tf_op jit(solution)/shard_map/ppermute | solution.py:399
  62.3 1.9 %collective-permute-start.10 = (bf16[288,384]{1,0:T(8,128)(2,1)S(1)}, bf16[288,384]{1,0:T(8,128)(2,1)S(1)}, u32[]{:S(2)}, u32[]{:S(2)}) collective-permute-start(bf16[288,384]{1,0:T(8,128)(2,1)S(1)} %get-tuple-element.36), channel_id=1, source_target_pairs={{0,66},{1,67},{2,64},{3,65},{4,70},{5,71},{6,68},{7,69},{8,74},{9,... | collective-permute-start | bytes 663560 | tf_op jit(solution)/shard_map/ppermute | solution.py:399
  64.2 4.0 %collective-permute-done.8.refs_0_ = bf16[288,384]{1,0:T(8,128)(2,1)S(1)} collective-permute-done((bf16[288,384]{1,0:T(8,128)(2,1)S(1)}, bf16[288,384]{1,0:T(8,128)(2,1)S(1)}, u32[]{:S(2)}, u32[]{:S(2)}) %collective-permute-start.8) | collective-permute-done | bytes 221216 | tf_op jit(solution)/shard_map/ppermute | solution.py:399
  69.1 5.0 %collective-permute-done.10.refs_2_ = bf16[288,384]{1,0:T(8,128)(2,1)S(1)} collective-permute-done((bf16[288,384]{1,0:T(8,128)(2,1)S(1)}, bf16[288,384]{1,0:T(8,128)(2,1)S(1)}, u32[]{:S(2)}, u32[]{:S(2)}) %collective-permute-start.10) | collective-permute-done | bytes 221216 | tf_op jit(solution)/shard_map/ppermute | solution.py:399
  75.1 2.8 %collective-permute-start.12 = (bf16[96,384]{1,0:T(8,128)(2,1)S(1)}, bf16[96,384]{1,0:T(8,128)(2,1)S(1)}, u32[]{:S(2)}, u32[]{:S(2)}) collective-permute-start(bf16[96,384]{1,0:T(8,128)(2,1)S(1)} %get-tuple-element.40), channel_id=1, source_target_pairs={{0,6},{1,7},{2,4},{3,5},{4,2},{5,3},{6,0},{7,1},{8,14},{9,15},{10,... | collective-permute-start | bytes 221192 | tf_op jit(solution)/shard_map/ppermute | solution.py:399
  77.9 2.9 %collective-permute-start.13 = (bf16[96,384]{1,0:T(8,128)(2,1)S(1)}, bf16[96,384]{1,0:T(8,128)(2,1)S(1)}, u32[]{:S(2)}, u32[]{:S(2)}) collective-permute-start(bf16[96,384]{1,0:T(8,128)(2,1)S(1)} %get-tuple-element.41), channel_id=1, source_target_pairs={{0,198},{1,199},{2,196},{3,197},{4,194},{5,195},{6,192},{7,193},{8... | collective-permute-start | bytes 221192 | tf_op jit(solution)/shard_map/ppermute | solution.py:399
  80.8 4.8 %collective-permute-done.13.r2 = bf16[96,384]{1,0:T(8,128)(2,1)S(1)} collective-permute-done((bf16[96,384]{1,0:T(8,128)(2,1)S(1)}, bf16[96,384]{1,0:T(8,128)(2,1)S(1)}, u32[]{:S(2)}, u32[]{:S(2)}) %collective-permute-start.13) | collective-permute-done | bytes 73760 | tf_op jit(solution)/shard_map/ppermute | solution.py:399
  86.4 2.1 %collective-permute-start.14 = (f32[96,128]{1,0:T(8,128)S(1)}, f32[96,128]{1,0:T(8,128)S(1)}, u32[]{:S(2)}, u32[]{:S(2)}) collective-permute-start(f32[96,128]{1,0:T(8,128)S(1)} %get-tuple-element.44), channel_id=1, source_target_pairs={{0,16},{1,17},{2,18},{3,19},{4,20},{5,21},{6,22},{7,23},{8,24},{9,... | collective-permute-start | bytes 147464 | tf_op jit(solution)/shard_map/ppermute | solution.py:399
  88.6 1.4 %collective-permute-start.16 = (f32[96,128]{1,0:T(8,128)S(1)}, f32[96,128]{1,0:T(8,128)S(1)}, u32[]{:S(2)}, u32[]{:S(2)}) collective-permute-start(f32[96,128]{1,0:T(8,128)S(1)} %get-tuple-element.46), channel_id=1, source_target_pairs={{0,24},{1,25},{2,26},{3,27},{4,28},{5,29},{6,30},{7,31},{8,16},{9,... | collective-permute-start | bytes 147464 | tf_op jit(solution)/shard_map/ppermute | solution.py:399
  89.9 1.5 %collective-permute-done.14.r0 = f32[96,128]{1,0:T(8,128)S(1)} collective-permute-done((f32[96,128]{1,0:T(8,128)S(1)}, f32[96,128]{1,0:T(8,128)S(1)}, u32[]{:S(2)}, u32[]{:S(2)}) %collective-permute-start.14) | collective-permute-done | bytes 49184 | tf_op jit(solution)/shard_map/ppermute | solution.py:399
  93.2 5.2 %collective-permute-start.17 = (f32[96,128]{1,0:T(8,128)S(1)}, f32[96,128]{1,0:T(8,128)S(1)}, u32[]{:S(2)}, u32[]{:S(2)}) collective-permute-start(f32[96,128]{1,0:T(8,128)S(1)} %get-tuple-element.49), channel_id=1, source_target_pairs={{0,56},{1,57},{2,58},{3,59},{4,60},{5,61},{6,62},{7,63},{8,48},{9,... | collective-permute-start | bytes 147464 | tf_op jit(solution)/shard_map/ppermute | solution.py:399
  98.4 2.1 %collective-permute-done.17.recv = f32[96,128]{1,0:T(8,128)S(1)} collective-permute-done((f32[96,128]{1,0:T(8,128)S(1)}, f32[96,128]{1,0:T(8,128)S(1)}, u32[]{:S(2)}, u32[]{:S(2)}) %collective-permute-start.17) | collective-permute-done | bytes 49184 | tf_op jit(solution)/shard_map/ppermute | solution.py:399
  (50 shorter events, 16.2 us)
Async XLA Ops:
  0.6 19.0 %copy-start.4 = (bf16[10,512]{1,0:T(8,128)(2,1)S(1)}, bf16[10,512]{1,0:T(8,128)(2,1)}, u32[]{:S(2)}) copy-start(bf16[10,512]{1,0:T(8,128)(2,1)} %param.12) | copy-start | bytes 30724
  0.6 19.0 %copy-start = (bf16[1536,512]{1,0:T(8,128)(2,1)S(1)}, bf16[1536,512]{1,0:T(8,128)(2,1)}, u32[]{:S(2)}) copy-start(bf16[1536,512]{1,0:T(8,128)(2,1)} %w2.1) | copy-start | bytes 4718596
  3.3 4.5 %collective-permute-start.2 = (bf16[4,10368]{1,0:T(4,128)(2,1)S(1)}, bf16[4,10368]{1,0:T(4,128)(2,1)S(1)}, u32[]{:S(2)}, u32[]{:S(2)}) collective-permute-start(bf16[4,10368]{1,0:T(4,128)(2,1)S(1)} %pad_maximum_fusion), channel_id=1, source_target_pairs={{0,64},{1,65},{2,66},{3,67},{4,68},{5,69},{6,70},{7,71},{8,72},{9,... | collective-permute-start | bytes 248840 | tf_op jit(solution)/shard_map/ppermute | solution.py:399
  5.0 4.8 %collective-permute-start.1 = (bf16[4,10368]{1,0:T(4,128)(2,1)S(1)}, bf16[4,10368]{1,0:T(4,128)(2,1)S(1)}, u32[]{:S(2)}, u32[]{:S(2)}) collective-permute-start(bf16[4,10368]{1,0:T(4,128)(2,1)S(1)} %pad_maximum_fusion), channel_id=1, source_target_pairs={{0,8},{1,9},{2,10},{3,11},{4,12},{5,13},{6,14},{7,15},{8,0},{9,1},... | collective-permute-start | bytes 248840 | tf_op jit(solution)/shard_map/ppermute | solution.py:399
  5.4 5.4 %collective-permute-start = (bf16[4,10368]{1,0:T(4,128)(2,1)S(1)}, bf16[4,10368]{1,0:T(4,128)(2,1)S(1)}, u32[]{:S(2)}, u32[]{:S(2)}) collective-permute-start(bf16[4,10368]{1,0:T(4,128)(2,1)S(1)} %pad_maximum_fusion), channel_id=1, source_target_pairs={{0,72},{1,73},{2,74},{3,75},{4,76},{5,77},{6,78},{7,79},{8,64},{9,... | collective-permute-start | bytes 248840 | tf_op jit(solution)/shard_map/ppermute | solution.py:399
  11.8 8.6 %collective-permute-start.5 = (bf16[4,10368]{1,0:T(4,128)(2,1)S(1)}, bf16[4,10368]{1,0:T(4,128)(2,1)S(1)}, u32[]{:S(2)}, u32[]{:S(2)}) collective-permute-start(bf16[4,10368]{1,0:T(4,128)(2,1)S(1)} %select_select_fusion.1), channel_id=1, source_target_pairs={{0,192},{1,193},{2,194},{3,195},{4,196},{5,197},{6,198},{7,199},{8... | collective-permute-start | bytes 248840 | tf_op jit(solution)/shard_map/ppermute | solution.py:399
  14.7 7.7 %collective-permute-start.4 = (bf16[4,10368]{1,0:T(4,128)(2,1)S(1)}, bf16[4,10368]{1,0:T(4,128)(2,1)S(1)}, u32[]{:S(2)}, u32[]{:S(2)}) collective-permute-start(bf16[4,10368]{1,0:T(4,128)(2,1)S(1)} %select_select_fusion.1), channel_id=1, source_target_pairs={{0,16},{1,17},{2,18},{3,19},{4,20},{5,21},{6,22},{7,23},{8,24},{9,... | collective-permute-start | bytes 248840 | tf_op jit(solution)/shard_map/ppermute | solution.py:399
  18.0 7.7 %collective-permute-start.3 = (bf16[4,10368]{1,0:T(4,128)(2,1)S(1)}, bf16[4,10368]{1,0:T(4,128)(2,1)}, u32[]{:S(2)}, u32[]{:S(2)}) collective-permute-start(bf16[4,10368]{1,0:T(4,128)(2,1)S(1)} %select_select_fusion.1), channel_id=1, source_target_pairs={{0,208},{1,209},{2,210},{3,211},{4,212},{5,213},{6,214},{7,215},{8... | collective-permute-start | bytes 248840 | tf_op jit(solution)/shard_map/ppermute | solution.py:399
  19.6 15.3 %copy-start.2 = (f32[512]{0:T(512)S(1)}, f32[512]{0:T(512)}, u32[]{:S(2)}) copy-start(f32[512]{0:T(512)} %param.13) | copy-start | bytes 6148
  19.6 15.3 %copy-start.3 = (f32[512]{0:T(512)S(1)}, f32[512]{0:T(512)}, u32[]{:S(2)}) copy-start(f32[512]{0:T(512)} %param.14) | copy-start | bytes 6148
  26.7 7.8 %collective-permute-start.6 = (bf16[4,10368]{1,0:T(4,128)(2,1)S(1)}, bf16[4,10368]{1,0:T(4,128)(2,1)S(1)}, u32[]{:S(2)}, u32[]{:S(2)}) collective-permute-start(bf16[4,10368]{1,0:T(4,128)(2,1)S(1)} %select_select_fusion), channel_id=1, source_target_pairs={{0,56},{1,57},{2,58},{3,59},{4,60},{5,61},{6,62},{7,63},{8,48},{9,... | collective-permute-start | bytes 248840 | tf_op jit(solution)/shard_map/ppermute | solution.py:399
  35.0 1.3 %copy-start.1 = (bf16[640,1024]{1,0:T(8,128)(2,1)S(1)}, bf16[640,1024]{1,0:T(8,128)(2,1)}, u32[]{:S(2)}) copy-start(bf16[640,1024]{1,0:T(8,128)(2,1)} %fusion.1.perm) | copy-start | bytes 3932164
  57.5 2.4 %collective-permute-start.7 = (bf16[1056,384]{1,0:T(8,128)(2,1)S(1)}, bf16[1056,384]{1,0:T(8,128)(2,1)S(1)}, u32[]{:S(2)}, u32[]{:S(2)}) collective-permute-start(bf16[1056,384]{1,0:T(8,128)(2,1)S(1)} %get-tuple-element.31), channel_id=1, source_target_pairs={{0,1},{1,0},{2,3},{3,2},{4,5},{5,4},{6,7},{7,6},{8,9},{9,8},{10,11... | collective-permute-start | bytes 2433032 | tf_op jit(solution)/shard_map/ppermute | solution.py:399
  60.7 7.6 %collective-permute-start.8 = (bf16[288,384]{1,0:T(8,128)(2,1)S(1)}, bf16[288,384]{1,0:T(8,128)(2,1)S(1)}, u32[]{:S(2)}, u32[]{:S(2)}) collective-permute-start(bf16[288,384]{1,0:T(8,128)(2,1)S(1)} %get-tuple-element.34), channel_id=1, source_target_pairs={{0,64},{1,65},{2,66},{3,67},{4,68},{5,69},{6,70},{7,71},{8,72},{9,... | collective-permute-start | bytes 663560 | tf_op jit(solution)/shard_map/ppermute | solution.py:399
  60.8 8.4 %collective-permute-start.9 = (bf16[288,384]{1,0:T(8,128)(2,1)S(1)}, bf16[288,384]{1,0:T(8,128)(2,1)S(1)}, u32[]{:S(2)}, u32[]{:S(2)}) collective-permute-start(bf16[288,384]{1,0:T(8,128)(2,1)S(1)} %get-tuple-element.35), channel_id=1, source_target_pairs={{0,2},{1,3},{2,0},{3,1},{4,6},{5,7},{6,4},{7,5},{8,10},{9,11},{10,... | collective-permute-start | bytes 663560 | tf_op jit(solution)/shard_map/ppermute | solution.py:399
  62.3 11.8 %collective-permute-start.10 = (bf16[288,384]{1,0:T(8,128)(2,1)S(1)}, bf16[288,384]{1,0:T(8,128)(2,1)S(1)}, u32[]{:S(2)}, u32[]{:S(2)}) collective-permute-start(bf16[288,384]{1,0:T(8,128)(2,1)S(1)} %get-tuple-element.36), channel_id=1, source_target_pairs={{0,66},{1,67},{2,64},{3,65},{4,70},{5,71},{6,68},{7,69},{8,74},{9,... | collective-permute-start | bytes 663560 | tf_op jit(solution)/shard_map/ppermute | solution.py:399
  74.8 6.0 %collective-permute-start.11 = (bf16[96,384]{1,0:T(8,128)(2,1)S(1)}, bf16[96,384]{1,0:T(8,128)(2,1)S(1)}, u32[]{:S(2)}, u32[]{:S(2)}) collective-permute-start(bf16[96,384]{1,0:T(8,128)(2,1)S(1)} %get-tuple-element.39), channel_id=1, source_target_pairs={{0,192},{1,193},{2,194},{3,195},{4,196},{5,197},{6,198},{7,199},{8... | collective-permute-start | bytes 221192 | tf_op jit(solution)/shard_map/ppermute | solution.py:399
  75.1 5.7 %collective-permute-start.12 = (bf16[96,384]{1,0:T(8,128)(2,1)S(1)}, bf16[96,384]{1,0:T(8,128)(2,1)S(1)}, u32[]{:S(2)}, u32[]{:S(2)}) collective-permute-start(bf16[96,384]{1,0:T(8,128)(2,1)S(1)} %get-tuple-element.40), channel_id=1, source_target_pairs={{0,6},{1,7},{2,4},{3,5},{4,2},{5,3},{6,0},{7,1},{8,14},{9,15},{10,... | collective-permute-start | bytes 221192 | tf_op jit(solution)/shard_map/ppermute | solution.py:399
  77.9 7.7 %collective-permute-start.13 = (bf16[96,384]{1,0:T(8,128)(2,1)S(1)}, bf16[96,384]{1,0:T(8,128)(2,1)S(1)}, u32[]{:S(2)}, u32[]{:S(2)}) collective-permute-start(bf16[96,384]{1,0:T(8,128)(2,1)S(1)} %get-tuple-element.41), channel_id=1, source_target_pairs={{0,198},{1,199},{2,196},{3,197},{4,194},{5,195},{6,192},{7,193},{8... | collective-permute-start | bytes 221192 | tf_op jit(solution)/shard_map/ppermute | solution.py:399
  86.4 5.1 %collective-permute-start.14 = (f32[96,128]{1,0:T(8,128)S(1)}, f32[96,128]{1,0:T(8,128)S(1)}, u32[]{:S(2)}, u32[]{:S(2)}) collective-permute-start(f32[96,128]{1,0:T(8,128)S(1)} %get-tuple-element.44), channel_id=1, source_target_pairs={{0,16},{1,17},{2,18},{3,19},{4,20},{5,21},{6,22},{7,23},{8,24},{9,... | collective-permute-start | bytes 147464 | tf_op jit(solution)/shard_map/ppermute | solution.py:399
  88.4 4.1 %collective-permute-start.15 = (f32[96,128]{1,0:T(8,128)S(1)}, f32[96,128]{1,0:T(8,128)S(1)}, u32[]{:S(2)}, u32[]{:S(2)}) collective-permute-start(f32[96,128]{1,0:T(8,128)S(1)} %get-tuple-element.45), channel_id=1, source_target_pairs={{0,8},{1,9},{2,10},{3,11},{4,12},{5,13},{6,14},{7,15},{8,0},{9,1},... | collective-permute-start | bytes 147464 | tf_op jit(solution)/shard_map/ppermute | solution.py:399
  88.6 4.1 %collective-permute-start.16 = (f32[96,128]{1,0:T(8,128)S(1)}, f32[96,128]{1,0:T(8,128)S(1)}, u32[]{:S(2)}, u32[]{:S(2)}) collective-permute-start(f32[96,128]{1,0:T(8,128)S(1)} %get-tuple-element.46), channel_id=1, source_target_pairs={{0,24},{1,25},{2,26},{3,27},{4,28},{5,29},{6,30},{7,31},{8,16},{9,... | collective-permute-start | bytes 147464 | tf_op jit(solution)/shard_map/ppermute | solution.py:399
  93.2 7.3 %collective-permute-start.17 = (f32[96,128]{1,0:T(8,128)S(1)}, f32[96,128]{1,0:T(8,128)S(1)}, u32[]{:S(2)}, u32[]{:S(2)}) collective-permute-start(f32[96,128]{1,0:T(8,128)S(1)} %get-tuple-element.49), channel_id=1, source_target_pairs={{0,56},{1,57},{2,58},{3,59},{4,60},{5,61},{6,62},{7,63},{8,48},{9,... | collective-permute-start | bytes 147464 | tf_op jit(solution)/shard_map/ppermute | solution.py:399

commit v6 on v5

--- a/solution.py
+++ b/solution.py
@@ -15,7 +15,7 @@
 GRAN = 1024
 ROWS = 2048
 CH = 512
-BLK = 512
+BLK = 1024
 BLOCKS = [
     (2 * xh + (xl ^ xh), 2 * yh + (yl ^ yh)) for xl in range(2) for yl in range(2) for xh in range(2) for yh in range(2)
 ]
@@ -25,6 +25,10 @@
     return jnp.dot(a, b, preferred_element_type=F32, precision=precision)
 
 
+def dot_b(a, b):
+    return lax.dot_general(a, b, (((1,), (1,)), ((), ())), preferred_element_type=F32)
+
+
 def dot_t(a, b, precision=None):
     return lax.dot_general(
         a, b, (((0,), (0,)), ((), ())), preferred_element_type=F32, precision=precision
@@ -38,7 +42,7 @@
 
 def plan(sc):
     size = [sc[s] for s in range(SLOTS)]
-    src = [sc[SLOTS + s] for s in range(SLOTS)]
+    src = [sc[SLOTS + s] ^ sc[16] for s in range(SLOTS)]
     rank, off = [], []
     for s in range(SLOTS):
         before = [(src[q] < src[s]).astype(jnp.int32) for q in range(SLOTS) if q != s]
@@ -66,20 +70,24 @@
 
 
 def window_kernel(
-    sc, u, perm, cot, wst, gain, bias, w2, wt,
+    sc, own_rows, moved, cot, wst, gain, bias, w2,
     keep, send, small,
-    wide, lanes16, buf, xd, xbig, xs, wbig, acc, nst, tc, im, grads, carry,
+    lines, wide, lanes16, buf, xd, xbig, xs, wbig, acc, nst, tc, im, grads, carry,
 ):
     step = pl.program_id(0)
     segs = plan(sc)
 
     @pl.when(step == 0)
     def _():
-        samples = u[:, : GRAN * TAPS].astype(F32)
         for s in range(SLOTS):
-            for r in range(16):
-                wide[16 * s + r : 16 * s + r + 1, :] = samples[s : s + 1, 640 * r : 640 * (r + 1)]
-        lanes16[...] = dot(wide[...].astype(BF16), perm[...])
+            at = pl.ds(80 * s, 80)
+            lines[at, :] = jnp.where((sc[SLOTS + s] & 4) != 0, moved[at, :], own_rows[at, :]).astype(F32)
+            for c in range(5):
+                wide[16 * s : 16 * s + 16, 128 * c : 128 * c + 128] = lines[pl.ds(80 * s + c, 16, stride=5), :]
+        place = lax.broadcasted_iota(jnp.int32, (1, 1024), 1)
+        place = jnp.where(place % 16 < TAPS, place // 16 * TAPS + place % 16, -1)
+        perm = (lax.broadcasted_iota(jnp.int32, (640, 1), 0) == place).astype(F32).astype(BF16)
+        lanes16[...] = dot(wide[...].astype(BF16), perm)
         buf[pl.ds(ROWS, 8), :] = jnp.zeros((8, 128), F32)
         own = (
             lax.broadcasted_iota(jnp.int32, (8, 1024), 1) % 128 // 16
@@ -119,8 +127,8 @@
             sums = sums + jnp.sum(raw, axis=0, keepdims=True)
             xd[pl.ds(base, BLK), :] = x1
             full = jnp.where((row >= lo_d) & (row < hi_all), x1, 0.0)
-            xs[0, pl.ds(base, BLK), :] = jnp.where(odd == 0, full, 0.0).astype(BF16)
-            xs[1, pl.ds(base, BLK), :] = jnp.where(odd == 1, full, 0.0).astype(BF16)
+            xs[0, :, base : base + BLK] = jnp.where(odd == 0, full, 0.0).T.astype(BF16)
+            xs[1, :, base : base + BLK] = jnp.where(odd == 1, full, 0.0).T.astype(BF16)
         xbig[pl.ds(ROWS, 16), :] = jnp.zeros((16, 256), BF16)
         mu = sums / count
         main = jnp.zeros((128, 128), F32)
@@ -198,18 +206,18 @@
     grad = jnp.where(drop, 0.0, cot[...].astype(F32) * slope).astype(BF16)
     acc[...] += dot_t(grad, taps)
 
-    third = dot(grad, wt[:, 2 * CH :])
+    third = dot_b(grad, w2[2 * CH :, :])
     row = lax.broadcasted_iota(jnp.int32, (BLK, 1), 0)
     shifted = jnp.where(row == 0, carry[0:1, :], pltpu.roll(third, 1, 0))
     carry[0:1, :] = third[BLK - 1 : BLK]
-    ag_e = (dot(grad, wt[:, :CH]) + shifted) * s_e[:BLK]
-    ag_o = dot(grad, wt[:, CH : 2 * CH]) * s_o
+    ag_e = (dot_b(grad, w2[:CH, :]) + shifted) * s_e[:BLK]
+    ag_o = dot_b(grad, w2[CH : 2 * CH, :]) * s_o
     total = grads[...]
     for g, ag in enumerate((ag_e, ag_o)):
-        part = xs[g, pl.ds(base, BLK), :]
+        part = xs[g, :, pl.ds(base, BLK)]
         high = ag.astype(BF16)
         low = (ag - high.astype(F32)).astype(BF16)
-        total = total + dot_t(part, high) + dot_t(part, low)
+        total = total + dot(part, high) + dot(part, low)
     grads[...] = total
 
     @pl.when(step == pl.num_programs(0) - 1)
@@ -342,7 +350,7 @@
     return pltpu.with_memory_space_constraint(value, pltpu.VMEM)
 
 
-def window(sc, u, perm, cot, wst, gain, bias, w2, wt):
+def window(sc, own_rows, moved, cot, wst, gain, bias, w2):
     whole = pl.BlockSpec(memory_space=pltpu.VMEM)
     shapes = [((1024, 384), F32), ((1056, 384), BF16), ((16, 384), F32)]
     return pl.pallas_call(
@@ -353,16 +361,17 @@
             in_specs=[
                 whole, whole,
                 pl.BlockSpec((BLK, CH), lambda i, sc: (i, 0)),
-                whole, whole, whole, whole, whole,
+                whole, whole, whole, whole,
             ],
             out_specs=[pl.BlockSpec(memory_space=pltpu.VMEM)] * len(shapes),
             scratch_shapes=[
+                pltpu.VMEM((320, 128), F32),
                 pltpu.VMEM((64, 640), F32),
                 pltpu.VMEM((64, 1024), F32),
                 pltpu.VMEM((ROWS + GRAN, 128), F32),
                 pltpu.VMEM((ROWS, 128), F32),
                 pltpu.VMEM((ROWS + 16, 256), BF16),
-                pltpu.VMEM((2, ROWS, 128), BF16),
+                pltpu.VMEM((2, 128, ROWS), BF16),
                 pltpu.VMEM((256, 2 * CH), BF16),
                 pltpu.VMEM((CH, 3 * CH), F32),
                 pltpu.VMEM((128, CH), F32),
@@ -377,8 +386,8 @@
         cost_estimate=pl.CostEstimate(flops=14 * 10**9, bytes_accessed=10 * 10**6, transcendentals=0),
         name="window",
     )(
-        sc, in_vmem(u), in_vmem(perm), pltpu.with_memory_space_constraint(cot, pltpu.HBM),
-        in_vmem(wst), in_vmem(gain), in_vmem(bias), in_vmem(w2), in_vmem(wt),
+        sc, in_vmem(own_rows), in_vmem(moved), pltpu.with_memory_space_constraint(cot, pltpu.HBM),
+        in_vmem(wst), in_vmem(gain), in_vmem(bias), in_vmem(w2),
     )
 
 
@@ -399,19 +408,54 @@
     return lax.ppermute(value, ("wide", "bulk"), [(i, i ^ (8 * wide + bulk)) for i in range(256)])
 
 
-def route(rows, sizes, masks):
-    z_high, y_high = (masks & 4) // 4, (masks & 16) // 16
-    z_low, z_mid, y_low = (masks & 1) ^ z_high, (masks & 2) // 2 ^ z_high, (masks & 8) // 8 ^ y_high
-    units = sizes // TAPS
-    extra = jnp.stack([(units // 32).astype(BF16), (units % 32).astype(BF16)], axis=1)
-    value = jnp.concatenate([rows, jnp.pad(extra, ((0, 0), (0, 126)))], axis=1)
-    for a, use_a, b, use_b in ((1, z_low, 8, y_low), (2, z_mid, 24, y_high)):
-        got_a, got_b, got_both = swap(value, a), swap(value, b), swap(value, a ^ b)
-        far, use_a = (use_b != 0)[:, None], (use_a != 0)[:, None]
-        value = jnp.where(use_a, jnp.where(far, got_both, got_a), jnp.where(far, got_b, value))
-    value = jnp.where((z_high != 0)[:, None], swap(value, 7), value)
-    tail = value[:, -128:-126].astype(F32)
-    return value, (tail[:, 0] * 32.0 + tail[:, 1]).astype(jnp.int32)
+def rows_kernel(lengths, waves, out):
+    for s in range(SLOTS):
+        for i in range(80):
+            lines_at = 80 * s + i
+            out[lines_at : lines_at + 1, :] = waves[s : s + 1, 128 * i : 128 * i + 128]
+    lane = lax.broadcasted_iota(jnp.int32, (16, 128), 1)
+    tail = jnp.zeros((16, 128), F32)
+    for s in range(SLOTS):
+        units = lengths[s] // TAPS
+        tail = jnp.where(lane == 32 * s, (units // 32).astype(F32), tail)
+        tail = jnp.where(lane == 32 * s + 1, (units % 32).astype(F32), tail)
+    out[320:336, :] = tail.astype(BF16)
+
+
+def pick_kernel(first, sc, own, got_a, got_b, got_both, out):
+    lane = lax.broadcasted_iota(jnp.int32, (16, 128), 1)
+    refs = (own, got_b, got_a, got_both)
+    tails = [r[320:336, :].astype(F32) for r in refs]
+    tail = tails[0]
+    for s in range(SLOTS):
+        mask = sc[s]
+        z_high, y_high = (mask >> 2) & 1, (mask >> 4) & 1
+        if first:
+            code = 2 * ((mask & 1) ^ z_high) + (((mask >> 3) & 1) ^ y_high)
+        else:
+            code = 2 * (((mask >> 1) & 1) ^ z_high) + y_high
+        at = pl.ds(80 * s, 80)
+        for k, ref in enumerate(refs):
+
+            @pl.when(code == k)
+            def _(ref=ref):
+                out[at, :] = ref[at, :]
+
+            if k:
+                tail = jnp.where((lane // 32 == s) & (code == k), tails[k], tail)
+    out[320:336, :] = tail.astype(BF16)
+
+
+def route(waves, lengths, masks):
+    out = [((336, 128), BF16)]
+    (value,) = small_call(rows_kernel, "rows", lengths, (waves,), out)
+    for a, b in ((1, 8), (2, 24)):
+        got = [swap(value, a), swap(value, b), swap(value, a ^ b)]
+        (value,) = small_call(functools.partial(pick_kernel, a == 1), "pick%d" % a, masks, (value, *got), out)
+    moved = swap(value, 7)
+    far = ((masks & 4) != 0)[:, None]
+    tail = jnp.where(far, moved[320].reshape(4, 32), value[320].reshape(4, 32)).astype(F32)
+    return value, moved, (tail[:, 0] * 32.0 + tail[:, 1]).astype(jnp.int32)
 
 
 def window_inputs(conv_first):
@@ -421,27 +465,24 @@
     return jnp.concatenate([even, odd], axis=0)
 
 
-def local(rows, units, sources, places, cot, conv_first, norm_gain, norm_bias, conv_second):
-    lane = jnp.arange(1024, dtype=jnp.int32)[None, :]
-    perm = (jnp.arange(640, dtype=jnp.int32)[:, None] == lane // 16 * TAPS + lane % 16) & (lane % 16 < TAPS)
-    sc = jnp.concatenate([units, sources, places])
-    wst = window_inputs(conv_first)
+def local(value, moved, units, masks, places, cot, conv_first, norm_gain, norm_bias, conv_second):
+    sc = jnp.concatenate([units, masks, places])
     gain, bias = norm_gain[None, :], norm_bias[None, :]
-    return sc, window(sc, rows, perm.astype(BF16), cot, wst, gain, bias, conv_second, conv_second.T)
+    return sc, window(sc, value, moved, cot, window_inputs(conv_first), gain, bias, conv_second)
 
 
 def per_device(waveforms, owner_of, lengths, cotangent, conv_first, norm_gain, norm_bias, conv_second):
     me = lax.axis_index("wide")
     place = lax.axis_index("bulk")
     masks = jnp.bitwise_xor(owner_of[0], me)
-    rows, units = route(waveforms[0], lengths[0], masks)
+    value, moved, units = route(waveforms[0], lengths[0], masks)
     x_low, x_high, y_low, y_high = (place // 2) % 2, place // 4, (me // 8) % 2, me // 16
     z_low, z_mid, z_high = me % 2, (me // 2) % 2, (me // 4) % 2
     places = jnp.stack(
-        [place % 2, x_low ^ x_high, y_low ^ y_high, x_high, y_high, z_low ^ z_high, z_mid ^ z_high, z_high]
+        [place % 2, x_low ^ x_high, y_low ^ y_high, x_high, y_high, z_low ^ z_high, z_mid ^ z_high, z_high, me]
     ).astype(jnp.int32)
     sc, (keep, send, small) = local(
-        rows, units, jnp.bitwise_xor(masks, me), places, cotangent[0, 0],
+        value, moved, units, masks, places, cotangent[0, 0],
         conv_first, norm_gain, norm_bias, conv_second,
     )
     recv = [swap(send, 0, 1)]

time: 103 us -> 103 us (level)
  other arithmetic: 7.16 us -> 1.65 us
  local copies, waits for them, and re-layouts: 2.33 us -> 4.61 us
  Pallas kernels: 25.2 us -> 26.9 us
    unnamed x11 -> x10, local copies, waits for them, and re-layouts: 2.04 us -> 4.31 us
    select_n x3 -> x0, other arithmetic: 2.19 us -> none  [the longest x2 2.08 us: route(): jnp.where(use_a, jnp.where(far, got_both, got_a), jnp.where(far, got_b, v...]
    pallas_call x5 -> x8, Pallas kernels: 4.05 us -> 6.17 us  [small_call(): pl.pallas_call(kernel, in_specs=[pl.BlockSpec(memory_space=pltpu.SMEM)] +...]
    convert_element_type x4 -> x2, other arithmetic: 1.8 us -> 0.26 us  [the longest x1 0.19 us: route(): return (value, moved, (tail[:, 0] * 32.0 + tail[:, 1]).astype(jnp.int32))]
  transfers between devices with their start and end apart: 18 -> 18, of which waited for: 15 -> 16; matrix products, arithmetic and copies ran while one was open for 3% -> 1% of each run, Pallas kernels for 0% -> 0%
where the time goes in v6:
time: 103 us; the launch traced here: 101 us
  waiting for transfers between devices  34 us (33%)
  starting transfers between devices  33.2 us (32%)
  Pallas kernels  26.9 us (26%)
  local copies, waits for them, and re-layouts  4.61 us (4%)
  other arithmetic  1.65 us (2%)
    ppermute x18, waiting for transfers between devices, swap(): lax.ppermute(value, ('wide', 'bulk'), [(i, i ^ 8 * wide + bulk) for i in...  34 us
    ppermute x18, starting transfers between devices, swap(): lax.ppermute(value, ('wide', 'bulk'), [(i, i ^ 8 * wide + bulk) for i in...  33.2 us
    pallas_call x1, Pallas kernels, window(): pl.pallas_call(window_kernel, grid_spec=pltpu.PrefetchScalarGridSpec(num_...  20.7 us
    pallas_call x8, Pallas kernels, small_call(): pl.pallas_call(kernel, in_specs=[pl.BlockSpec(memory_space=pltpu.SMEM)] +...  6.17 us
    unnamed x10, local copies, waits for them, and re-layouts  4.31 us
  transfers between devices with their start and end apart: 18, of which 16 were waited for; matrix products, arithmetic and copies ran while one was open for 1% of the time, Pallas kernels for 0%

profile of v6, /device:TPU:32, one launch (start us, length us, event | category | flops | bytes accessed | tf_op | source)
XLA Modules:
  0.0 101.1 jit_solution(12893275455856621217)
XLA Ops:
  4.2 2.2 %collective-permute-start.1 = (bf16[336,128]{1,0:T(8,128)(2,1)S(1)}, bf16[336,128]{1,0:T(8,128)(2,1)S(1)}, u32[]{:S(2)}, u32[]{:S(2)}) collective-permute-start(bf16[336,128]{1,0:T(8,128)(2,1)S(1)} %rows.1.own), channel_id=1, source_target_pairs={{0,64},{1,65},{2,66},{3,67},{4,68},{5,69},{6,70},{7,71},{8,72},{9,... | collective-permute-start | bytes 258056 | tf_op jit(solution)/shard_map/ppermute | solution.py:408
  8.0 1.3 %collective-permute-done.2.got_both = bf16[336,128]{1,0:T(8,128)(2,1)S(1)} collective-permute-done((bf16[336,128]{1,0:T(8,128)(2,1)S(1)}, bf16[336,128]{1,0:T(8,128)(2,1)S(1)}, u32[]{:S(2)}, u32[]{:S(2)}) %collective-permute-start.2) | collective-permute-done | bytes 86048 | tf_op jit(solution)/shard_map/ppermute | solution.py:408
  11.6 4.4 %collective-permute-start.5 = (bf16[336,128]{1,0:T(8,128)(2,1)S(1)}, bf16[336,128]{1,0:T(8,128)(2,1)S(1)}, u32[]{:S(2)}, u32[]{:S(2)}) collective-permute-start(bf16[336,128]{1,0:T(8,128)(2,1)S(1)} %pick1.1.own), channel_id=1, source_target_pairs={{0,208},{1,209},{2,210},{3,211},{4,212},{5,213},{6,214},{7,215},{8... | collective-permute-start | bytes 258056 | tf_op jit(solution)/shard_map/ppermute | solution.py:408
  17.2 4.2 %collective-permute-done.5.got_both = bf16[336,128]{1,0:T(8,128)(2,1)S(1)} collective-permute-done((bf16[336,128]{1,0:T(8,128)(2,1)S(1)}, bf16[336,128]{1,0:T(8,128)(2,1)S(1)}, u32[]{:S(2)}, u32[]{:S(2)}) %collective-permute-start.5) | collective-permute-done | bytes 86048 | tf_op jit(solution)/shard_map/ppermute | solution.py:408
  23.1 5.7 %collective-permute-start.6 = (bf16[336,128]{1,0:T(8,128)(2,1)S(1)}, bf16[336,128]{1,0:T(8,128)(2,1)S(1)}, u32[]{:S(2)}, u32[]{:S(2)}) collective-permute-start(bf16[336,128]{1,0:T(8,128)(2,1)S(1)} %pick2.1.own_rows), channel_id=1, source_target_pairs={{0,56},{1,57},{2,58},{3,59},{4,60},{5,61},{6,62},{7,63},{8,48},{9,... | collective-permute-start | bytes 258056 | tf_op jit(solution)/shard_map/ppermute | solution.py:408
  28.9 2.4 %collective-permute-done.6.moved = bf16[336,128]{1,0:T(8,128)(2,1)S(1)} collective-permute-done((bf16[336,128]{1,0:T(8,128)(2,1)S(1)}, bf16[336,128]{1,0:T(8,128)(2,1)S(1)}, u32[]{:S(2)}, u32[]{:S(2)}) %collective-permute-start.6) | collective-permute-done | bytes 86048 | tf_op jit(solution)/shard_map/ppermute | solution.py:408
  31.8 1.4 %copy-done.2 = bf16[1536,512]{1,0:T(8,128)(2,1)S(1)} copy-done((bf16[1536,512]{1,0:T(8,128)(2,1)S(1)}, bf16[1536,512]{1,0:T(8,128)(2,1)}, u32[]{:S(2)}) %copy-start.2) | copy-done | bytes 1572888
  34.6 20.7 %window.1 = (f32[1024,384]{1,0:T(8,128)S(1)}, bf16[1056,384]{1,0:T(8,128)(2,1)S(1)}, f32[16,384]{1,0:T(8,128)S(1)}) custom-call(s32[17]{0:T(128)S(1)} %concatenate.6.sc, bf16[336,128]{1,0:T(8,128)(2,1)S(1)} %pick2.1.own_rows, bf16[336,128]{1,0:T(8,128)(2,1)S(1)} %collective-permute-done.6.moved, bf16[2048,512]{1,0:T(8,128)(2,1)} %bitcast.23, ...), custom_call_target="tpu_custom_call" | custom-call | flops 14000000000 | bytes 10000000 | tf_op jit(solution)/shard_map/window/pallas_call | solution.py:356
  55.4 2.3 %collective-permute-done.7.refs_0_ = bf16[1056,384]{1,0:T(8,128)(2,1)S(1)} collective-permute-done((bf16[1056,384]{1,0:T(8,128)(2,1)S(1)}, bf16[1056,384]{1,0:T(8,128)(2,1)S(1)}, u32[]{:S(2)}, u32[]{:S(2)}) %collective-permute-start.7) | collective-permute-done | bytes 811040 | tf_op jit(solution)/shard_map/ppermute | solution.py:408
  58.9 1.5 %collective-permute-start.9 = (bf16[288,384]{1,0:T(8,128)(2,1)S(1)}, bf16[288,384]{1,0:T(8,128)(2,1)S(1)}, u32[]{:S(2)}, u32[]{:S(2)}) collective-permute-start(bf16[288,384]{1,0:T(8,128)(2,1)S(1)} %get-tuple-element.35), channel_id=1, source_target_pairs={{0,2},{1,3},{2,0},{3,1},{4,6},{5,7},{6,4},{7,5},{8,10},{9,11},{10,... | collective-permute-start | bytes 663560 | tf_op jit(solution)/shard_map/ppermute | solution.py:408
  60.4 1.6 %collective-permute-start.10 = (bf16[288,384]{1,0:T(8,128)(2,1)S(1)}, bf16[288,384]{1,0:T(8,128)(2,1)S(1)}, u32[]{:S(2)}, u32[]{:S(2)}) collective-permute-start(bf16[288,384]{1,0:T(8,128)(2,1)S(1)} %get-tuple-element.36), channel_id=1, source_target_pairs={{0,66},{1,67},{2,64},{3,65},{4,70},{5,71},{6,68},{7,69},{8,74},{9,... | collective-permute-start | bytes 663560 | tf_op jit(solution)/shard_map/ppermute | solution.py:408
  62.0 4.0 %collective-permute-done.8.refs_0_ = bf16[288,384]{1,0:T(8,128)(2,1)S(1)} collective-permute-done((bf16[288,384]{1,0:T(8,128)(2,1)S(1)}, bf16[288,384]{1,0:T(8,128)(2,1)S(1)}, u32[]{:S(2)}, u32[]{:S(2)}) %collective-permute-start.8) | collective-permute-done | bytes 221216 | tf_op jit(solution)/shard_map/ppermute | solution.py:408
  67.2 4.7 %collective-permute-done.10.refs_2_ = bf16[288,384]{1,0:T(8,128)(2,1)S(1)} collective-permute-done((bf16[288,384]{1,0:T(8,128)(2,1)S(1)}, bf16[288,384]{1,0:T(8,128)(2,1)S(1)}, u32[]{:S(2)}, u32[]{:S(2)}) %collective-permute-start.10) | collective-permute-done | bytes 221216 | tf_op jit(solution)/shard_map/ppermute | solution.py:408
  72.6 1.9 %collective-permute-start.11 = (bf16[96,384]{1,0:T(8,128)(2,1)S(1)}, bf16[96,384]{1,0:T(8,128)(2,1)S(1)}, u32[]{:S(2)}, u32[]{:S(2)}) collective-permute-start(bf16[96,384]{1,0:T(8,128)(2,1)S(1)} %get-tuple-element.39), channel_id=1, source_target_pairs={{0,192},{1,193},{2,194},{3,195},{4,196},{5,197},{6,198},{7,199},{8... | collective-permute-start | bytes 221192 | tf_op jit(solution)/shard_map/ppermute | solution.py:408
  74.5 2.8 %collective-permute-start.12 = (bf16[96,384]{1,0:T(8,128)(2,1)S(1)}, bf16[96,384]{1,0:T(8,128)(2,1)S(1)}, u32[]{:S(2)}, u32[]{:S(2)}) collective-permute-start(bf16[96,384]{1,0:T(8,128)(2,1)S(1)} %get-tuple-element.40), channel_id=1, source_target_pairs={{0,6},{1,7},{2,4},{3,5},{4,2},{5,3},{6,0},{7,1},{8,14},{9,15},{10,... | collective-permute-start | bytes 221192 | tf_op jit(solution)/shard_map/ppermute | solution.py:408
  77.3 1.3 %collective-permute-start.13 = (bf16[96,384]{1,0:T(8,128)(2,1)S(1)}, bf16[96,384]{1,0:T(8,128)(2,1)S(1)}, u32[]{:S(2)}, u32[]{:S(2)}) collective-permute-start(bf16[96,384]{1,0:T(8,128)(2,1)S(1)} %get-tuple-element.41), channel_id=1, source_target_pairs={{0,198},{1,199},{2,196},{3,197},{4,194},{5,195},{6,192},{7,193},{8... | collective-permute-start | bytes 221192 | tf_op jit(solution)/shard_map/ppermute | solution.py:408
  78.6 1.5 %collective-permute-done.12.r1 = bf16[96,384]{1,0:T(8,128)(2,1)S(1)} collective-permute-done((bf16[96,384]{1,0:T(8,128)(2,1)S(1)}, bf16[96,384]{1,0:T(8,128)(2,1)S(1)}, u32[]{:S(2)}, u32[]{:S(2)}) %collective-permute-start.12) | collective-permute-done | bytes 73760 | tf_op jit(solution)/shard_map/ppermute | solution.py:408
  80.1 4.9 %collective-permute-done.13.r2 = bf16[96,384]{1,0:T(8,128)(2,1)S(1)} collective-permute-done((bf16[96,384]{1,0:T(8,128)(2,1)S(1)}, bf16[96,384]{1,0:T(8,128)(2,1)S(1)}, u32[]{:S(2)}, u32[]{:S(2)}) %collective-permute-start.13) | collective-permute-done | bytes 73760 | tf_op jit(solution)/shard_map/ppermute | solution.py:408
  85.7 2.2 %collective-permute-start.14 = (f32[96,128]{1,0:T(8,128)S(1)}, f32[96,128]{1,0:T(8,128)S(1)}, u32[]{:S(2)}, u32[]{:S(2)}) collective-permute-start(f32[96,128]{1,0:T(8,128)S(1)} %get-tuple-element.44), channel_id=1, source_target_pairs={{0,16},{1,17},{2,18},{3,19},{4,20},{5,21},{6,22},{7,23},{8,24},{9,... | collective-permute-start | bytes 147464 | tf_op jit(solution)/shard_map/ppermute | solution.py:408
  88.0 1.3 %collective-permute-start.16 = (f32[96,128]{1,0:T(8,128)S(1)}, f32[96,128]{1,0:T(8,128)S(1)}, u32[]{:S(2)}, u32[]{:S(2)}) collective-permute-start(f32[96,128]{1,0:T(8,128)S(1)} %get-tuple-element.46), channel_id=1, source_target_pairs={{0,24},{1,25},{2,26},{3,27},{4,28},{5,29},{6,30},{7,31},{8,16},{9,... | collective-permute-start | bytes 147464 | tf_op jit(solution)/shard_map/ppermute | solution.py:408
  89.3 1.5 %collective-permute-done.14.r0 = f32[96,128]{1,0:T(8,128)S(1)} collective-permute-done((f32[96,128]{1,0:T(8,128)S(1)}, f32[96,128]{1,0:T(8,128)S(1)}, u32[]{:S(2)}, u32[]{:S(2)}) %collective-permute-start.14) | collective-permute-done | bytes 49184 | tf_op jit(solution)/shard_map/ppermute | solution.py:408
  92.6 5.1 %collective-permute-start.17 = (f32[96,128]{1,0:T(8,128)S(1)}, f32[96,128]{1,0:T(8,128)S(1)}, u32[]{:S(2)}, u32[]{:S(2)}) collective-permute-start(f32[96,128]{1,0:T(8,128)S(1)} %get-tuple-element.49), channel_id=1, source_target_pairs={{0,56},{1,57},{2,58},{3,59},{4,60},{5,61},{6,62},{7,63},{8,48},{9,... | collective-permute-start | bytes 147464 | tf_op jit(solution)/shard_map/ppermute | solution.py:408
  97.7 2.1 %collective-permute-done.17.recv = f32[96,128]{1,0:T(8,128)S(1)} collective-permute-done((f32[96,128]{1,0:T(8,128)S(1)}, f32[96,128]{1,0:T(8,128)S(1)}, u32[]{:S(2)}, u32[]{:S(2)}) %collective-permute-start.17) | collective-permute-done | bytes 49184 | tf_op jit(solution)/shard_map/ppermute | solution.py:408
  99.8 1.3 %final.1 = (f32[48,64]{1,0:T(8,128)}, f32[10,512]{1,0:T(8,128)}, f32[1,512]{1,0:T(1,128)}, f32[1,512]{1,0:T(1,128)}) custom-call(s32[17]{0:T(128)S(1)} %concatenate.6.sc, f32[48,128]{1,0:T(8,128)S(1)} %get-tuple-element.47.keep, f32[48,128]{1,0:T(8,128)S(1)} %get-tuple-element.48.small, f32[96,128]{1,0:T(8,128)S(1)} %collective-permute-done.17.recv), custom_call_target="tpu_custom_call" | custom-call | tf_op jit(solution)/shard_map/final/pallas_call | solution.py:396
  (41 shorter events, 18.1 us)
Async XLA Ops:
  0.6 0.9 copy-start
  1.5 0.7 copy-start.1
  3.0 6.2 %collective-permute-start.2 = (bf16[336,128]{1,0:T(8,128)(2,1)S(1)}, bf16[336,128]{1,0:T(8,128)(2,1)S(1)}, u32[]{:S(2)}, u32[]{:S(2)}) collective-permute-start(bf16[336,128]{1,0:T(8,128)(2,1)S(1)} %rows.1.own), channel_id=1, source_target_pairs={{0,72},{1,73},{2,74},{3,75},{4,76},{5,77},{6,78},{7,79},{8,64},{9,... | collective-permute-start | bytes 258056 | tf_op jit(solution)/shard_map/ppermute | solution.py:408
  4.2 5.8 %collective-permute-start.1 = (bf16[336,128]{1,0:T(8,128)(2,1)S(1)}, bf16[336,128]{1,0:T(8,128)(2,1)S(1)}, u32[]{:S(2)}, u32[]{:S(2)}) collective-permute-start(bf16[336,128]{1,0:T(8,128)(2,1)S(1)} %rows.1.own), channel_id=1, source_target_pairs={{0,64},{1,65},{2,66},{3,67},{4,68},{5,69},{6,70},{7,71},{8,72},{9,... | collective-permute-start | bytes 258056 | tf_op jit(solution)/shard_map/ppermute | solution.py:408
  6.4 4.5 %collective-permute-start = (bf16[336,128]{1,0:T(8,128)(2,1)S(1)}, bf16[336,128]{1,0:T(8,128)(2,1)S(1)}, u32[]{:S(2)}, u32[]{:S(2)}) collective-permute-start(bf16[336,128]{1,0:T(8,128)(2,1)S(1)} %rows.1.own), channel_id=1, source_target_pairs={{0,8},{1,9},{2,10},{3,11},{4,12},{5,13},{6,14},{7,15},{8,0},{9,1},... | collective-permute-start | bytes 258056 | tf_op jit(solution)/shard_map/ppermute | solution.py:408
  11.6 9.9 %collective-permute-start.5 = (bf16[336,128]{1,0:T(8,128)(2,1)S(1)}, bf16[336,128]{1,0:T(8,128)(2,1)S(1)}, u32[]{:S(2)}, u32[]{:S(2)}) collective-permute-start(bf16[336,128]{1,0:T(8,128)(2,1)S(1)} %pick1.1.own), channel_id=1, source_target_pairs={{0,208},{1,209},{2,210},{3,211},{4,212},{5,213},{6,214},{7,215},{8... | collective-permute-start | bytes 258056 | tf_op jit(solution)/shard_map/ppermute | solution.py:408
  15.9 5.7 %collective-permute-start.4 = (bf16[336,128]{1,0:T(8,128)(2,1)S(1)}, bf16[336,128]{1,0:T(8,128)(2,1)S(1)}, u32[]{:S(2)}, u32[]{:S(2)}) collective-permute-start(bf16[336,128]{1,0:T(8,128)(2,1)S(1)} %pick1.1.own), channel_id=1, source_target_pairs={{0,192},{1,193},{2,194},{3,195},{4,196},{5,197},{6,198},{7,199},{8... | collective-permute-start | bytes 258056 | tf_op jit(solution)/shard_map/ppermute | solution.py:408
  16.9 5.6 %collective-permute-start.3 = (bf16[336,128]{1,0:T(8,128)(2,1)S(1)}, bf16[336,128]{1,0:T(8,128)(2,1)S(1)}, u32[]{:S(2)}, u32[]{:S(2)}) collective-permute-start(bf16[336,128]{1,0:T(8,128)(2,1)S(1)} %pick1.1.own), channel_id=1, source_target_pairs={{0,16},{1,17},{2,18},{3,19},{4,20},{5,21},{6,22},{7,23},{8,24},{9,... | collective-permute-start | bytes 258056 | tf_op jit(solution)/shard_map/ppermute | solution.py:408
  23.1 8.2 %collective-permute-start.6 = (bf16[336,128]{1,0:T(8,128)(2,1)S(1)}, bf16[336,128]{1,0:T(8,128)(2,1)S(1)}, u32[]{:S(2)}, u32[]{:S(2)}) collective-permute-start(bf16[336,128]{1,0:T(8,128)(2,1)S(1)} %pick2.1.own_rows), channel_id=1, source_target_pairs={{0,56},{1,57},{2,58},{3,59},{4,60},{5,61},{6,62},{7,63},{8,48},{9,... | collective-permute-start | bytes 258056 | tf_op jit(solution)/shard_map/ppermute | solution.py:408
  31.8 1.4 %copy-start.2 = (bf16[1536,512]{1,0:T(8,128)(2,1)S(1)}, bf16[1536,512]{1,0:T(8,128)(2,1)}, u32[]{:S(2)}) copy-start(bf16[1536,512]{1,0:T(8,128)(2,1)} %w2.1) | copy-start | bytes 4718596
  33.2 0.7 copy-start.3
  33.9 0.7 copy-start.4
  55.3 2.4 %collective-permute-start.7 = (bf16[1056,384]{1,0:T(8,128)(2,1)S(1)}, bf16[1056,384]{1,0:T(8,128)(2,1)S(1)}, u32[]{:S(2)}, u32[]{:S(2)}) collective-permute-start(bf16[1056,384]{1,0:T(8,128)(2,1)S(1)} %get-tuple-element.31), channel_id=1, source_target_pairs={{0,1},{1,0},{2,3},{3,2},{4,5},{5,4},{6,7},{7,6},{8,9},{9,8},{10,11... | collective-permute-start | bytes 2433032 | tf_op jit(solution)/shard_map/ppermute | solution.py:408
  58.5 7.6 %collective-permute-start.8 = (bf16[288,384]{1,0:T(8,128)(2,1)S(1)}, bf16[288,384]{1,0:T(8,128)(2,1)S(1)}, u32[]{:S(2)}, u32[]{:S(2)}) collective-permute-start(bf16[288,384]{1,0:T(8,128)(2,1)S(1)} %get-tuple-element.34), channel_id=1, source_target_pairs={{0,64},{1,65},{2,66},{3,67},{4,68},{5,69},{6,70},{7,71},{8,72},{9,... | collective-permute-start | bytes 663560 | tf_op jit(solution)/shard_map/ppermute | solution.py:408
  58.9 8.3 %collective-permute-start.9 = (bf16[288,384]{1,0:T(8,128)(2,1)S(1)}, bf16[288,384]{1,0:T(8,128)(2,1)S(1)}, u32[]{:S(2)}, u32[]{:S(2)}) collective-permute-start(bf16[288,384]{1,0:T(8,128)(2,1)S(1)} %get-tuple-element.35), channel_id=1, source_target_pairs={{0,2},{1,3},{2,0},{3,1},{4,6},{5,7},{6,4},{7,5},{8,10},{9,11},{10,... | collective-permute-start | bytes 663560 | tf_op jit(solution)/shard_map/ppermute | solution.py:408
  60.4 11.5 %collective-permute-start.10 = (bf16[288,384]{1,0:T(8,128)(2,1)S(1)}, bf16[288,384]{1,0:T(8,128)(2,1)S(1)}, u32[]{:S(2)}, u32[]{:S(2)}) collective-permute-start(bf16[288,384]{1,0:T(8,128)(2,1)S(1)} %get-tuple-element.36), channel_id=1, source_target_pairs={{0,66},{1,67},{2,64},{3,65},{4,70},{5,71},{6,68},{7,69},{8,74},{9,... | collective-permute-start | bytes 663560 | tf_op jit(solution)/shard_map/ppermute | solution.py:408
  72.6 6.0 %collective-permute-start.11 = (bf16[96,384]{1,0:T(8,128)(2,1)S(1)}, bf16[96,384]{1,0:T(8,128)(2,1)S(1)}, u32[]{:S(2)}, u32[]{:S(2)}) collective-permute-start(bf16[96,384]{1,0:T(8,128)(2,1)S(1)} %get-tuple-element.39), channel_id=1, source_target_pairs={{0,192},{1,193},{2,194},{3,195},{4,196},{5,197},{6,198},{7,199},{8... | collective-permute-start | bytes 221192 | tf_op jit(solution)/shard_map/ppermute | solution.py:408
  74.5 5.6 %collective-permute-start.12 = (bf16[96,384]{1,0:T(8,128)(2,1)S(1)}, bf16[96,384]{1,0:T(8,128)(2,1)S(1)}, u32[]{:S(2)}, u32[]{:S(2)}) collective-permute-start(bf16[96,384]{1,0:T(8,128)(2,1)S(1)} %get-tuple-element.40), channel_id=1, source_target_pairs={{0,6},{1,7},{2,4},{3,5},{4,2},{5,3},{6,0},{7,1},{8,14},{9,15},{10,... | collective-permute-start | bytes 221192 | tf_op jit(solution)/shard_map/ppermute | solution.py:408
  77.3 7.7 %collective-permute-start.13 = (bf16[96,384]{1,0:T(8,128)(2,1)S(1)}, bf16[96,384]{1,0:T(8,128)(2,1)S(1)}, u32[]{:S(2)}, u32[]{:S(2)}) collective-permute-start(bf16[96,384]{1,0:T(8,128)(2,1)S(1)} %get-tuple-element.41), channel_id=1, source_target_pairs={{0,198},{1,199},{2,196},{3,197},{4,194},{5,195},{6,192},{7,193},{8... | collective-permute-start | bytes 221192 | tf_op jit(solution)/shard_map/ppermute | solution.py:408
  85.7 5.1 %collective-permute-start.14 = (f32[96,128]{1,0:T(8,128)S(1)}, f32[96,128]{1,0:T(8,128)S(1)}, u32[]{:S(2)}, u32[]{:S(2)}) collective-permute-start(f32[96,128]{1,0:T(8,128)S(1)} %get-tuple-element.44), channel_id=1, source_target_pairs={{0,16},{1,17},{2,18},{3,19},{4,20},{5,21},{6,22},{7,23},{8,24},{9,... | collective-permute-start | bytes 147464 | tf_op jit(solution)/shard_map/ppermute | solution.py:408
  87.9 4.1 %collective-permute-start.15 = (f32[96,128]{1,0:T(8,128)S(1)}, f32[96,128]{1,0:T(8,128)S(1)}, u32[]{:S(2)}, u32[]{:S(2)}) collective-permute-start(f32[96,128]{1,0:T(8,128)S(1)} %get-tuple-element.45), channel_id=1, source_target_pairs={{0,8},{1,9},{2,10},{3,11},{4,12},{5,13},{6,14},{7,15},{8,0},{9,1},... | collective-permute-start | bytes 147464 | tf_op jit(solution)/shard_map/ppermute | solution.py:408
  88.0 4.1 %collective-permute-start.16 = (f32[96,128]{1,0:T(8,128)S(1)}, f32[96,128]{1,0:T(8,128)S(1)}, u32[]{:S(2)}, u32[]{:S(2)}) collective-permute-start(f32[96,128]{1,0:T(8,128)S(1)} %get-tuple-element.46), channel_id=1, source_target_pairs={{0,24},{1,25},{2,26},{3,27},{4,28},{5,29},{6,30},{7,31},{8,16},{9,... | collective-permute-start | bytes 147464 | tf_op jit(solution)/shard_map/ppermute | solution.py:408
  92.6 7.2 %collective-permute-start.17 = (f32[96,128]{1,0:T(8,128)S(1)}, f32[96,128]{1,0:T(8,128)S(1)}, u32[]{:S(2)}, u32[]{:S(2)}) collective-permute-start(f32[96,128]{1,0:T(8,128)S(1)} %get-tuple-element.49), channel_id=1, source_target_pairs={{0,56},{1,57},{2,58},{3,59},{4,60},{5,61},{6,62},{7,63},{8,48},{9,... | collective-permute-start | bytes 147464 | tf_op jit(solution)/shard_map/ppermute | solution.py:408

commit v7 on v6

--- a/solution.py
+++ b/solution.py
@@ -70,15 +70,25 @@
 
 
 def window_kernel(
-    sc, own_rows, moved, cot, wst, gain, bias, w2,
+    sc, own_rows, moved, params, cot_hbm, w2_hbm,
     keep, send, small,
-    lines, wide, lanes16, buf, xd, xbig, xs, wbig, acc, nst, tc, im, grads, carry,
+    lines, wide, lanes16, buf, xd, xbig, xs, wbig, acc, nst, tc, im, grads, carry, cot, w2, cot_sem, w2_sem,
 ):
     step = pl.program_id(0)
     segs = plan(sc)
 
+    wst = params.at[0:32]
+    gain = params.at[32:33]
+    bias = params.at[33:34]
+    copies = (
+        pltpu.make_async_copy(w2_hbm, w2, w2_sem),
+        pltpu.make_async_copy(cot_hbm, cot, cot_sem),
+    )
+
     @pl.when(step == 0)
     def _():
+        for copy in copies:
+            copy.start()
         for s in range(SLOTS):
             at = pl.ds(80 * s, 80)
             lines[at, :] = jnp.where((sc[SLOTS + s] & 4) != 0, moved[at, :], own_rows[at, :]).astype(F32)
@@ -187,6 +197,8 @@
         acc[...] = jnp.zeros_like(acc)
         grads[...] = jnp.zeros_like(grads)
         carry[...] = jnp.zeros_like(carry)
+        for copy in copies:
+            copy.wait()
 
     base = pl.multiple_of(step * BLK, BLK)
     pre_e = dot(xbig[pl.ds(base, BLK + 16), :], wbig[:, :CH])
@@ -203,7 +215,7 @@
     drop = row == segs[0][1] + segs[0][2] - 1
     for _s, off, n in segs[1:]:
         drop = drop | (row == off + n - 1)
-    grad = jnp.where(drop, 0.0, cot[...].astype(F32) * slope).astype(BF16)
+    grad = jnp.where(drop, 0.0, cot[pl.ds(base, BLK), :].astype(F32) * slope).astype(BF16)
     acc[...] += dot_t(grad, taps)
 
     third = dot_b(grad, w2[2 * CH :, :])
@@ -350,7 +362,7 @@
     return pltpu.with_memory_space_constraint(value, pltpu.VMEM)
 
 
-def window(sc, own_rows, moved, cot, wst, gain, bias, w2):
+def window(sc, own_rows, moved, params, cot, w2):
     whole = pl.BlockSpec(memory_space=pltpu.VMEM)
     shapes = [((1024, 384), F32), ((1056, 384), BF16), ((16, 384), F32)]
     return pl.pallas_call(
@@ -359,9 +371,8 @@
             num_scalar_prefetch=1,
             grid=(ROWS // BLK,),
             in_specs=[
-                whole, whole,
-                pl.BlockSpec((BLK, CH), lambda i, sc: (i, 0)),
-                whole, whole, whole, whole,
+                whole, whole, whole,
+                pl.BlockSpec(memory_space=pltpu.HBM), pl.BlockSpec(memory_space=pltpu.HBM),
             ],
             out_specs=[pl.BlockSpec(memory_space=pltpu.VMEM)] * len(shapes),
             scratch_shapes=[
@@ -379,6 +390,10 @@
                 pltpu.VMEM((8, CH), F32),
                 pltpu.VMEM((128, CH), F32),
                 pltpu.VMEM((8, CH), F32),
+                pltpu.VMEM((ROWS, CH), BF16),
+                pltpu.VMEM((3 * CH, CH), BF16),
+                pltpu.SemaphoreType.DMA,
+                pltpu.SemaphoreType.DMA,
             ],
         ),
         out_shape=[pltpu.VMEM(s, d) for s, d in shapes],
@@ -386,8 +401,8 @@
         cost_estimate=pl.CostEstimate(flops=14 * 10**9, bytes_accessed=10 * 10**6, transcendentals=0),
         name="window",
     )(
-        sc, in_vmem(own_rows), in_vmem(moved), pltpu.with_memory_space_constraint(cot, pltpu.HBM),
-        in_vmem(wst), in_vmem(gain), in_vmem(bias), in_vmem(w2),
+        sc, in_vmem(own_rows), in_vmem(moved), in_vmem(params),
+        pltpu.with_memory_space_constraint(cot, pltpu.HBM), pltpu.with_memory_space_constraint(w2, pltpu.HBM),
     )
 
 
@@ -420,6 +435,17 @@
         tail = jnp.where(lane == 32 * s, (units // 32).astype(F32), tail)
         tail = jnp.where(lane == 32 * s + 1, (units % 32).astype(F32), tail)
     out[320:336, :] = tail.astype(BF16)
+
+
+def lay_rows(lengths, waves):
+    return pl.pallas_call(
+        rows_kernel,
+        in_specs=[pl.BlockSpec(memory_space=pltpu.SMEM), pl.BlockSpec(memory_space=pltpu.VMEM)],
+        out_specs=pl.BlockSpec(memory_space=pltpu.VMEM),
+        out_shape=pltpu.VMEM((336, 128), BF16),
+        compiler_params=pltpu.CompilerParams(vmem_limit_bytes=8 * 2**20),
+        name="rows",
+    )(*(pltpu.with_memory_space_constraint(a, pltpu.HBM) for a in (lengths, waves)))
 
 
 def pick_kernel(first, sc, own, got_a, got_b, got_both, out):
@@ -448,7 +474,7 @@
 
 def route(waves, lengths, masks):
     out = [((336, 128), BF16)]
-    (value,) = small_call(rows_kernel, "rows", lengths, (waves,), out)
+    value = lay_rows(lengths, waves)
     for a, b in ((1, 8), (2, 24)):
         got = [swap(value, a), swap(value, b), swap(value, a ^ b)]
         (value,) = small_call(functools.partial(pick_kernel, a == 1), "pick%d" % a, masks, (value, *got), out)
@@ -458,17 +484,16 @@
     return value, moved, (tail[:, 0] * 32.0 + tail[:, 1]).astype(jnp.int32)
 
 
-def window_inputs(conv_first):
+def window_inputs(conv_first, gain, bias):
     w = conv_first.astype(F32)
-    even = jnp.pad(w, ((0, 6), (0, 0)))
-    odd = jnp.pad(w, ((5, 1), (0, 0)))
-    return jnp.concatenate([even, odd], axis=0)
+    rows = [jnp.pad(w, ((0, 6), (0, 0))), jnp.pad(w, ((5, 1), (0, 0))), gain[None, :], bias[None, :]]
+    return jnp.concatenate(rows + [jnp.zeros((6, CH), F32)], axis=0)
 
 
 def local(value, moved, units, masks, places, cot, conv_first, norm_gain, norm_bias, conv_second):
     sc = jnp.concatenate([units, masks, places])
-    gain, bias = norm_gain[None, :], norm_bias[None, :]
-    return sc, window(sc, value, moved, cot, window_inputs(conv_first), gain, bias, conv_second)
+    params = window_inputs(conv_first, norm_gain, norm_bias)
+    return sc, window(sc, value, moved, params, cot, conv_second)
 
 
 def per_device(waveforms, owner_of, lengths, cotangent, conv_first, norm_gain, norm_bias, conv_second):

time: 103 us -> 97.5 us (0.947)
  local copies, waits for them, and re-layouts: 4.61 us -> 1.83 us
    unnamed x10 -> x0, local copies, waits for them, and re-layouts: 4.31 us -> none
    pallas_call x1, Pallas kernels: 20.7 us -> 19.3 us  [window(): pl.pallas_call(window_kernel, grid_spec=pltpu.PrefetchScalarGridSpec(num_...]
    pallas_call x0 -> x1, Pallas kernels: none -> 1.19 us  [lay_rows(): pl.pallas_call(rows_kernel, in_specs=[pl.BlockSpec(memory_space=pltpu.SME...]
    pallas_call x8 -> x7, Pallas kernels: 6.17 us -> 5.34 us  [small_call(): pl.pallas_call(kernel, in_specs=[pl.BlockSpec(memory_space=pltpu.SMEM)] +...]
  transfers between devices with their start and end apart: 18 -> 18, of which waited for: 16 -> 16; matrix products, arithmetic and copies ran while one was open for 1% -> 2% of each run, Pallas kernels for 0% -> 0%
where the time goes in v7:
time: 97.5 us; the launch traced here: 95.8 us
  starting transfers between devices  33.2 us (34%)
  waiting for transfers between devices  33.2 us (34%)
  Pallas kernels  25.9 us (27%)
  local copies, waits for them, and re-layouts  1.83 us (2%)
    ppermute x18, waiting for transfers between devices, swap(): lax.ppermute(value, ('wide', 'bulk'), [(i, i ^ 8 * wide + bulk) for i in...  33.2 us
    ppermute x18, starting transfers between devices, swap(): lax.ppermute(value, ('wide', 'bulk'), [(i, i ^ 8 * wide + bulk) for i in...  33.2 us
    pallas_call x1, Pallas kernels, window(): pl.pallas_call(window_kernel, grid_spec=pltpu.PrefetchScalarGridSpec(num_...  19.3 us
    pallas_call x7, Pallas kernels, small_call(): pl.pallas_call(kernel, in_specs=[pl.BlockSpec(memory_space=pltpu.SMEM)] +...  5.34 us
  transfers between devices with their start and end apart: 18, of which 16 were waited for; matrix products, arithmetic and copies ran while one was open for 2% of the time, Pallas kernels for 0%

profile of v7, /device:TPU:32, one launch (start us, length us, event | category | flops | bytes accessed | tf_op | source)
XLA Modules:
  0.0 95.8 jit_solution(1445534773341281519)
XLA Ops:
  3.0 2.2 %collective-permute-start.1 = (bf16[336,128]{1,0:T(8,128)(2,1)S(1)}, bf16[336,128]{1,0:T(8,128)(2,1)S(1)}, u32[]{:S(2)}, u32[]{:S(2)}) collective-permute-start(bf16[336,128]{1,0:T(8,128)(2,1)S(1)} %rows.1.own), channel_id=1, source_target_pairs={{0,64},{1,65},{2,66},{3,67},{4,68},{5,69},{6,70},{7,71},{8,72},{9,... | collective-permute-start | bytes 258056 | tf_op jit(solution)/shard_map/ppermute | solution.py:423
  6.1 2.0 %collective-permute-done.2.got_both = bf16[336,128]{1,0:T(8,128)(2,1)S(1)} collective-permute-done((bf16[336,128]{1,0:T(8,128)(2,1)S(1)}, bf16[336,128]{1,0:T(8,128)(2,1)S(1)}, u32[]{:S(2)}, u32[]{:S(2)}) %collective-permute-start.2) | collective-permute-done | bytes 86048 | tf_op jit(solution)/shard_map/ppermute | solution.py:423
  10.4 4.4 %collective-permute-start.5 = (bf16[336,128]{1,0:T(8,128)(2,1)S(1)}, bf16[336,128]{1,0:T(8,128)(2,1)S(1)}, u32[]{:S(2)}, u32[]{:S(2)}) collective-permute-start(bf16[336,128]{1,0:T(8,128)(2,1)S(1)} %pick1.1.own), channel_id=1, source_target_pairs={{0,208},{1,209},{2,210},{3,211},{4,212},{5,213},{6,214},{7,215},{8... | collective-permute-start | bytes 258056 | tf_op jit(solution)/shard_map/ppermute | solution.py:423
  17.6 2.7 %collective-permute-done.5.got_both = bf16[336,128]{1,0:T(8,128)(2,1)S(1)} collective-permute-done((bf16[336,128]{1,0:T(8,128)(2,1)S(1)}, bf16[336,128]{1,0:T(8,128)(2,1)S(1)}, u32[]{:S(2)}, u32[]{:S(2)}) %collective-permute-start.5) | collective-permute-done | bytes 86048 | tf_op jit(solution)/shard_map/ppermute | solution.py:423
  22.0 5.7 %collective-permute-start.6 = (bf16[336,128]{1,0:T(8,128)(2,1)S(1)}, bf16[336,128]{1,0:T(8,128)(2,1)S(1)}, u32[]{:S(2)}, u32[]{:S(2)}) collective-permute-start(bf16[336,128]{1,0:T(8,128)(2,1)S(1)} %pick2.1.own_rows), channel_id=1, source_target_pairs={{0,56},{1,57},{2,58},{3,59},{4,60},{5,61},{6,62},{7,63},{8,48},{9,... | collective-permute-start | bytes 258056 | tf_op jit(solution)/shard_map/ppermute | solution.py:423
  27.7 2.4 %collective-permute-done.6.moved = bf16[336,128]{1,0:T(8,128)(2,1)S(1)} collective-permute-done((bf16[336,128]{1,0:T(8,128)(2,1)S(1)}, bf16[336,128]{1,0:T(8,128)(2,1)S(1)}, u32[]{:S(2)}, u32[]{:S(2)}) %collective-permute-start.6) | collective-permute-done | bytes 86048 | tf_op jit(solution)/shard_map/ppermute | solution.py:423
  30.6 19.3 %window.1 = (f32[1024,384]{1,0:T(8,128)S(1)}, bf16[1056,384]{1,0:T(8,128)(2,1)S(1)}, f32[16,384]{1,0:T(8,128)S(1)}) custom-call(s32[17]{0:T(128)S(1)} %concatenate.6.sc, bf16[336,128]{1,0:T(8,128)(2,1)S(1)} %pick2.1.own_rows, bf16[336,128]{1,0:T(8,128)(2,1)S(1)} %collective-permute-done.6.moved, f32[40,512]{1,0:T(8,128)S(1)} %concatenate.7.params, ...), custom_call_target="tpu_custom_call" | custom-call | flops 14000000000 | bytes 10000000 | tf_op jit(solution)/shard_map/window/pallas_call | solution.py:368
  50.0 2.3 %collective-permute-done.7.refs_0_ = bf16[1056,384]{1,0:T(8,128)(2,1)S(1)} collective-permute-done((bf16[1056,384]{1,0:T(8,128)(2,1)S(1)}, bf16[1056,384]{1,0:T(8,128)(2,1)S(1)}, u32[]{:S(2)}, u32[]{:S(2)}) %collective-permute-start.7) | collective-permute-done | bytes 811040 | tf_op jit(solution)/shard_map/ppermute | solution.py:423
  53.6 1.5 %collective-permute-start.9 = (bf16[288,384]{1,0:T(8,128)(2,1)S(1)}, bf16[288,384]{1,0:T(8,128)(2,1)S(1)}, u32[]{:S(2)}, u32[]{:S(2)}) collective-permute-start(bf16[288,384]{1,0:T(8,128)(2,1)S(1)} %get-tuple-element.35), channel_id=1, source_target_pairs={{0,2},{1,3},{2,0},{3,1},{4,6},{5,7},{6,4},{7,5},{8,10},{9,11},{10,... | collective-permute-start | bytes 663560 | tf_op jit(solution)/shard_map/ppermute | solution.py:423
  55.1 1.6 %collective-permute-start.10 = (bf16[288,384]{1,0:T(8,128)(2,1)S(1)}, bf16[288,384]{1,0:T(8,128)(2,1)S(1)}, u32[]{:S(2)}, u32[]{:S(2)}) collective-permute-start(bf16[288,384]{1,0:T(8,128)(2,1)S(1)} %get-tuple-element.36), channel_id=1, source_target_pairs={{0,66},{1,67},{2,64},{3,65},{4,70},{5,71},{6,68},{7,69},{8,74},{9,... | collective-permute-start | bytes 663560 | tf_op jit(solution)/shard_map/ppermute | solution.py:423
  56.7 4.0 %collective-permute-done.8.refs_0_ = bf16[288,384]{1,0:T(8,128)(2,1)S(1)} collective-permute-done((bf16[288,384]{1,0:T(8,128)(2,1)S(1)}, bf16[288,384]{1,0:T(8,128)(2,1)S(1)}, u32[]{:S(2)}, u32[]{:S(2)}) %collective-permute-start.8) | collective-permute-done | bytes 221216 | tf_op jit(solution)/shard_map/ppermute | solution.py:423
  60.7 1.2 %collective-permute-done.9.refs_1_ = bf16[288,384]{1,0:T(8,128)(2,1)S(1)} collective-permute-done((bf16[288,384]{1,0:T(8,128)(2,1)S(1)}, bf16[288,384]{1,0:T(8,128)(2,1)S(1)}, u32[]{:S(2)}, u32[]{:S(2)}) %collective-permute-start.9) | collective-permute-done | bytes 221216 | tf_op jit(solution)/shard_map/ppermute | solution.py:423
  61.9 4.7 %collective-permute-done.10.refs_2_ = bf16[288,384]{1,0:T(8,128)(2,1)S(1)} collective-permute-done((bf16[288,384]{1,0:T(8,128)(2,1)S(1)}, bf16[288,384]{1,0:T(8,128)(2,1)S(1)}, u32[]{:S(2)}, u32[]{:S(2)}) %collective-permute-start.10) | collective-permute-done | bytes 221216 | tf_op jit(solution)/shard_map/ppermute | solution.py:423
  67.3 1.9 %collective-permute-start.11 = (bf16[96,384]{1,0:T(8,128)(2,1)S(1)}, bf16[96,384]{1,0:T(8,128)(2,1)S(1)}, u32[]{:S(2)}, u32[]{:S(2)}) collective-permute-start(bf16[96,384]{1,0:T(8,128)(2,1)S(1)} %get-tuple-element.39), channel_id=1, source_target_pairs={{0,192},{1,193},{2,194},{3,195},{4,196},{5,197},{6,198},{7,199},{8... | collective-permute-start | bytes 221192 | tf_op jit(solution)/shard_map/ppermute | solution.py:423
  69.2 2.8 %collective-permute-start.12 = (bf16[96,384]{1,0:T(8,128)(2,1)S(1)}, bf16[96,384]{1,0:T(8,128)(2,1)S(1)}, u32[]{:S(2)}, u32[]{:S(2)}) collective-permute-start(bf16[96,384]{1,0:T(8,128)(2,1)S(1)} %get-tuple-element.40), channel_id=1, source_target_pairs={{0,6},{1,7},{2,4},{3,5},{4,2},{5,3},{6,0},{7,1},{8,14},{9,15},{10,... | collective-permute-start | bytes 221192 | tf_op jit(solution)/shard_map/ppermute | solution.py:423
  71.9 1.3 %collective-permute-start.13 = (bf16[96,384]{1,0:T(8,128)(2,1)S(1)}, bf16[96,384]{1,0:T(8,128)(2,1)S(1)}, u32[]{:S(2)}, u32[]{:S(2)}) collective-permute-start(bf16[96,384]{1,0:T(8,128)(2,1)S(1)} %get-tuple-element.41), channel_id=1, source_target_pairs={{0,198},{1,199},{2,196},{3,197},{4,194},{5,195},{6,192},{7,193},{8... | collective-permute-start | bytes 221192 | tf_op jit(solution)/shard_map/ppermute | solution.py:423
  73.3 1.5 %collective-permute-done.12.r1 = bf16[96,384]{1,0:T(8,128)(2,1)S(1)} collective-permute-done((bf16[96,384]{1,0:T(8,128)(2,1)S(1)}, bf16[96,384]{1,0:T(8,128)(2,1)S(1)}, u32[]{:S(2)}, u32[]{:S(2)}) %collective-permute-start.12) | collective-permute-done | bytes 73760 | tf_op jit(solution)/shard_map/ppermute | solution.py:423
  74.7 4.9 %collective-permute-done.13.r2 = bf16[96,384]{1,0:T(8,128)(2,1)S(1)} collective-permute-done((bf16[96,384]{1,0:T(8,128)(2,1)S(1)}, bf16[96,384]{1,0:T(8,128)(2,1)S(1)}, u32[]{:S(2)}, u32[]{:S(2)}) %collective-permute-start.13) | collective-permute-done | bytes 73760 | tf_op jit(solution)/shard_map/ppermute | solution.py:423
  80.4 2.2 %collective-permute-start.14 = (f32[96,128]{1,0:T(8,128)S(1)}, f32[96,128]{1,0:T(8,128)S(1)}, u32[]{:S(2)}, u32[]{:S(2)}) collective-permute-start(f32[96,128]{1,0:T(8,128)S(1)} %get-tuple-element.44), channel_id=1, source_target_pairs={{0,16},{1,17},{2,18},{3,19},{4,20},{5,21},{6,22},{7,23},{8,24},{9,... | collective-permute-start | bytes 147464 | tf_op jit(solution)/shard_map/ppermute | solution.py:423
  82.6 1.3 %collective-permute-start.16 = (f32[96,128]{1,0:T(8,128)S(1)}, f32[96,128]{1,0:T(8,128)S(1)}, u32[]{:S(2)}, u32[]{:S(2)}) collective-permute-start(f32[96,128]{1,0:T(8,128)S(1)} %get-tuple-element.46), channel_id=1, source_target_pairs={{0,24},{1,25},{2,26},{3,27},{4,28},{5,29},{6,30},{7,31},{8,16},{9,... | collective-permute-start | bytes 147464 | tf_op jit(solution)/shard_map/ppermute | solution.py:423
  84.0 1.5 %collective-permute-done.14.r0 = f32[96,128]{1,0:T(8,128)S(1)} collective-permute-done((f32[96,128]{1,0:T(8,128)S(1)}, f32[96,128]{1,0:T(8,128)S(1)}, u32[]{:S(2)}, u32[]{:S(2)}) %collective-permute-start.14) | collective-permute-done | bytes 49184 | tf_op jit(solution)/shard_map/ppermute | solution.py:423
  87.3 5.0 %collective-permute-start.17 = (f32[96,128]{1,0:T(8,128)S(1)}, f32[96,128]{1,0:T(8,128)S(1)}, u32[]{:S(2)}, u32[]{:S(2)}) collective-permute-start(f32[96,128]{1,0:T(8,128)S(1)} %get-tuple-element.49), channel_id=1, source_target_pairs={{0,56},{1,57},{2,58},{3,59},{4,60},{5,61},{6,62},{7,63},{8,48},{9,... | collective-permute-start | bytes 147464 | tf_op jit(solution)/shard_map/ppermute | solution.py:423
  92.3 2.1 %collective-permute-done.17.recv = f32[96,128]{1,0:T(8,128)S(1)} collective-permute-done((f32[96,128]{1,0:T(8,128)S(1)}, f32[96,128]{1,0:T(8,128)S(1)}, u32[]{:S(2)}, u32[]{:S(2)}) %collective-permute-start.17) | collective-permute-done | bytes 49184 | tf_op jit(solution)/shard_map/ppermute | solution.py:423
  94.5 1.3 %final.1 = (f32[48,64]{1,0:T(8,128)}, f32[10,512]{1,0:T(8,128)}, f32[1,512]{1,0:T(1,128)}, f32[1,512]{1,0:T(1,128)}) custom-call(s32[17]{0:T(128)S(1)} %concatenate.6.sc, f32[48,128]{1,0:T(8,128)S(1)} %get-tuple-element.47.keep, f32[48,128]{1,0:T(8,128)S(1)} %get-tuple-element.48.small, f32[96,128]{1,0:T(8,128)S(1)} %collective-permute-done.17.recv), custom_call_target="tpu_custom_call" | custom-call | tf_op jit(solution)/shard_map/final/pallas_call | solution.py:411
  (32 shorter events, 15.1 us)
Async XLA Ops:
  1.8 6.2 %collective-permute-start.2 = (bf16[336,128]{1,0:T(8,128)(2,1)S(1)}, bf16[336,128]{1,0:T(8,128)(2,1)S(1)}, u32[]{:S(2)}, u32[]{:S(2)}) collective-permute-start(bf16[336,128]{1,0:T(8,128)(2,1)S(1)} %rows.1.own), channel_id=1, source_target_pairs={{0,72},{1,73},{2,74},{3,75},{4,76},{5,77},{6,78},{7,79},{8,64},{9,... | collective-permute-start | bytes 258056 | tf_op jit(solution)/shard_map/ppermute | solution.py:423
  3.0 5.8 %collective-permute-start.1 = (bf16[336,128]{1,0:T(8,128)(2,1)S(1)}, bf16[336,128]{1,0:T(8,128)(2,1)S(1)}, u32[]{:S(2)}, u32[]{:S(2)}) collective-permute-start(bf16[336,128]{1,0:T(8,128)(2,1)S(1)} %rows.1.own), channel_id=1, source_target_pairs={{0,64},{1,65},{2,66},{3,67},{4,68},{5,69},{6,70},{7,71},{8,72},{9,... | collective-permute-start | bytes 258056 | tf_op jit(solution)/shard_map/ppermute | solution.py:423
  5.2 4.5 %collective-permute-start = (bf16[336,128]{1,0:T(8,128)(2,1)S(1)}, bf16[336,128]{1,0:T(8,128)(2,1)S(1)}, u32[]{:S(2)}, u32[]{:S(2)}) collective-permute-start(bf16[336,128]{1,0:T(8,128)(2,1)S(1)} %rows.1.own), channel_id=1, source_target_pairs={{0,8},{1,9},{2,10},{3,11},{4,12},{5,13},{6,14},{7,15},{8,0},{9,1},... | collective-permute-start | bytes 258056 | tf_op jit(solution)/shard_map/ppermute | solution.py:423
  10.4 9.9 %collective-permute-start.5 = (bf16[336,128]{1,0:T(8,128)(2,1)S(1)}, bf16[336,128]{1,0:T(8,128)(2,1)S(1)}, u32[]{:S(2)}, u32[]{:S(2)}) collective-permute-start(bf16[336,128]{1,0:T(8,128)(2,1)S(1)} %pick1.1.own), channel_id=1, source_target_pairs={{0,208},{1,209},{2,210},{3,211},{4,212},{5,213},{6,214},{7,215},{8... | collective-permute-start | bytes 258056 | tf_op jit(solution)/shard_map/ppermute | solution.py:423
  14.8 5.7 %collective-permute-start.4 = (bf16[336,128]{1,0:T(8,128)(2,1)S(1)}, bf16[336,128]{1,0:T(8,128)(2,1)S(1)}, u32[]{:S(2)}, u32[]{:S(2)}) collective-permute-start(bf16[336,128]{1,0:T(8,128)(2,1)S(1)} %pick1.1.own), channel_id=1, source_target_pairs={{0,192},{1,193},{2,194},{3,195},{4,196},{5,197},{6,198},{7,199},{8... | collective-permute-start | bytes 258056 | tf_op jit(solution)/shard_map/ppermute | solution.py:423
  15.7 5.6 %collective-permute-start.3 = (bf16[336,128]{1,0:T(8,128)(2,1)S(1)}, bf16[336,128]{1,0:T(8,128)(2,1)S(1)}, u32[]{:S(2)}, u32[]{:S(2)}) collective-permute-start(bf16[336,128]{1,0:T(8,128)(2,1)S(1)} %pick1.1.own), channel_id=1, source_target_pairs={{0,16},{1,17},{2,18},{3,19},{4,20},{5,21},{6,22},{7,23},{8,24},{9,... | collective-permute-start | bytes 258056 | tf_op jit(solution)/shard_map/ppermute | solution.py:423
  22.0 8.2 %collective-permute-start.6 = (bf16[336,128]{1,0:T(8,128)(2,1)S(1)}, bf16[336,128]{1,0:T(8,128)(2,1)S(1)}, u32[]{:S(2)}, u32[]{:S(2)}) collective-permute-start(bf16[336,128]{1,0:T(8,128)(2,1)S(1)} %pick2.1.own_rows), channel_id=1, source_target_pairs={{0,56},{1,57},{2,58},{3,59},{4,60},{5,61},{6,62},{7,63},{8,48},{9,... | collective-permute-start | bytes 258056 | tf_op jit(solution)/shard_map/ppermute | solution.py:423
  49.9 2.4 %collective-permute-start.7 = (bf16[1056,384]{1,0:T(8,128)(2,1)S(1)}, bf16[1056,384]{1,0:T(8,128)(2,1)S(1)}, u32[]{:S(2)}, u32[]{:S(2)}) collective-permute-start(bf16[1056,384]{1,0:T(8,128)(2,1)S(1)} %get-tuple-element.31), channel_id=1, source_target_pairs={{0,1},{1,0},{2,3},{3,2},{4,5},{5,4},{6,7},{7,6},{8,9},{9,8},{10,11... | collective-permute-start | bytes 2433032 | tf_op jit(solution)/shard_map/ppermute | solution.py:423
  53.1 7.6 %collective-permute-start.8 = (bf16[288,384]{1,0:T(8,128)(2,1)S(1)}, bf16[288,384]{1,0:T(8,128)(2,1)S(1)}, u32[]{:S(2)}, u32[]{:S(2)}) collective-permute-start(bf16[288,384]{1,0:T(8,128)(2,1)S(1)} %get-tuple-element.34), channel_id=1, source_target_pairs={{0,64},{1,65},{2,66},{3,67},{4,68},{5,69},{6,70},{7,71},{8,72},{9,... | collective-permute-start | bytes 663560 | tf_op jit(solution)/shard_map/ppermute | solution.py:423
  53.6 8.3 %collective-permute-start.9 = (bf16[288,384]{1,0:T(8,128)(2,1)S(1)}, bf16[288,384]{1,0:T(8,128)(2,1)S(1)}, u32[]{:S(2)}, u32[]{:S(2)}) collective-permute-start(bf16[288,384]{1,0:T(8,128)(2,1)S(1)} %get-tuple-element.35), channel_id=1, source_target_pairs={{0,2},{1,3},{2,0},{3,1},{4,6},{5,7},{6,4},{7,5},{8,10},{9,11},{10,... | collective-permute-start | bytes 663560 | tf_op jit(solution)/shard_map/ppermute | solution.py:423
  55.1 11.5 %collective-permute-start.10 = (bf16[288,384]{1,0:T(8,128)(2,1)S(1)}, bf16[288,384]{1,0:T(8,128)(2,1)S(1)}, u32[]{:S(2)}, u32[]{:S(2)}) collective-permute-start(bf16[288,384]{1,0:T(8,128)(2,1)S(1)} %get-tuple-element.36), channel_id=1, source_target_pairs={{0,66},{1,67},{2,64},{3,65},{4,70},{5,71},{6,68},{7,69},{8,74},{9,... | collective-permute-start | bytes 663560 | tf_op jit(solution)/shard_map/ppermute | solution.py:423
  67.3 6.0 %collective-permute-start.11 = (bf16[96,384]{1,0:T(8,128)(2,1)S(1)}, bf16[96,384]{1,0:T(8,128)(2,1)S(1)}, u32[]{:S(2)}, u32[]{:S(2)}) collective-permute-start(bf16[96,384]{1,0:T(8,128)(2,1)S(1)} %get-tuple-element.39), channel_id=1, source_target_pairs={{0,192},{1,193},{2,194},{3,195},{4,196},{5,197},{6,198},{7,199},{8... | collective-permute-start | bytes 221192 | tf_op jit(solution)/shard_map/ppermute | solution.py:423
  69.2 5.6 %collective-permute-start.12 = (bf16[96,384]{1,0:T(8,128)(2,1)S(1)}, bf16[96,384]{1,0:T(8,128)(2,1)S(1)}, u32[]{:S(2)}, u32[]{:S(2)}) collective-permute-start(bf16[96,384]{1,0:T(8,128)(2,1)S(1)} %get-tuple-element.40), channel_id=1, source_target_pairs={{0,6},{1,7},{2,4},{3,5},{4,2},{5,3},{6,0},{7,1},{8,14},{9,15},{10,... | collective-permute-start | bytes 221192 | tf_op jit(solution)/shard_map/ppermute | solution.py:423
  71.9 7.7 %collective-permute-start.13 = (bf16[96,384]{1,0:T(8,128)(2,1)S(1)}, bf16[96,384]{1,0:T(8,128)(2,1)S(1)}, u32[]{:S(2)}, u32[]{:S(2)}) collective-permute-start(bf16[96,384]{1,0:T(8,128)(2,1)S(1)} %get-tuple-element.41), channel_id=1, source_target_pairs={{0,198},{1,199},{2,196},{3,197},{4,194},{5,195},{6,192},{7,193},{8... | collective-permute-start | bytes 221192 | tf_op jit(solution)/shard_map/ppermute | solution.py:423
  80.4 5.1 %collective-permute-start.14 = (f32[96,128]{1,0:T(8,128)S(1)}, f32[96,128]{1,0:T(8,128)S(1)}, u32[]{:S(2)}, u32[]{:S(2)}) collective-permute-start(f32[96,128]{1,0:T(8,128)S(1)} %get-tuple-element.44), channel_id=1, source_target_pairs={{0,16},{1,17},{2,18},{3,19},{4,20},{5,21},{6,22},{7,23},{8,24},{9,... | collective-permute-start | bytes 147464 | tf_op jit(solution)/shard_map/ppermute | solution.py:423
  82.6 4.1 %collective-permute-start.15 = (f32[96,128]{1,0:T(8,128)S(1)}, f32[96,128]{1,0:T(8,128)S(1)}, u32[]{:S(2)}, u32[]{:S(2)}) collective-permute-start(f32[96,128]{1,0:T(8,128)S(1)} %get-tuple-element.45), channel_id=1, source_target_pairs={{0,8},{1,9},{2,10},{3,11},{4,12},{5,13},{6,14},{7,15},{8,0},{9,1},... | collective-permute-start | bytes 147464 | tf_op jit(solution)/shard_map/ppermute | solution.py:423
  82.6 4.1 %collective-permute-start.16 = (f32[96,128]{1,0:T(8,128)S(1)}, f32[96,128]{1,0:T(8,128)S(1)}, u32[]{:S(2)}, u32[]{:S(2)}) collective-permute-start(f32[96,128]{1,0:T(8,128)S(1)} %get-tuple-element.46), channel_id=1, source_target_pairs={{0,24},{1,25},{2,26},{3,27},{4,28},{5,29},{6,30},{7,31},{8,16},{9,... | collective-permute-start | bytes 147464 | tf_op jit(solution)/shard_map/ppermute | solution.py:423
  87.3 7.2 %collective-permute-start.17 = (f32[96,128]{1,0:T(8,128)S(1)}, f32[96,128]{1,0:T(8,128)S(1)}, u32[]{:S(2)}, u32[]{:S(2)}) collective-permute-start(f32[96,128]{1,0:T(8,128)S(1)} %get-tuple-element.49), channel_id=1, source_target_pairs={{0,56},{1,57},{2,58},{3,59},{4,60},{5,61},{6,62},{7,63},{8,48},{9,... | collective-permute-start | bytes 147464 | tf_op jit(solution)/shard_map/ppermute | solution.py:423

commit v8 on v7

--- a/solution.py
+++ b/solution.py
@@ -285,12 +285,12 @@
 
 def quarters(sc, at):
     a, b = sc[at], sc[at + 1]
-    return 2 * a + b, (2 * a + 1 - b, 2 * (1 - a) + b, 2 * (1 - a) + 1 - b)
+    return 2 * a + b, (2 * (1 - a) + 1 - b, 2 * a + 1 - b, 2 * (1 - a) + b)
 
 
 def add_small(small, recvs, at):
     r = [received_small(recv, at) for recv in recvs]
-    return small[...] + r[0] if len(r) == 1 else (small[...] + r[0]) + (r[1] + r[2])
+    return small[...] + r[0] if len(r) == 1 else (small[...] + r[1]) + (r[2] + r[0])
 
 
 def combine_kernel(n, recvs, flag, sc, keep, small, *refs):
@@ -515,12 +515,12 @@
         out = [((n // 4, 384), F32), ((16, 384), F32)] + [((n // 4 + 32, 384), BF16)] * 3
         kernel = functools.partial(combine_kernel, n, len(recv), flag)
         keep, small, *sends = small_call(kernel, "combine%d" % n, sc, (keep, small, *recv), out)
-        recv = [swap(sends[0], y), swap(sends[1], 0, x), swap(sends[2], y, x)]
+        recv = [swap(sends[0], y, x), swap(sends[1], y), swap(sends[2], 0, x)]
     out = [((48, 128), F32), ((48, 128), F32)] + [((96, 128), F32)] * 3
     keep, small, *sends = small_call(
         turn_kernel, "turn", sc, (keep, small, *recv), out, [pltpu.VMEM((192, 128), F32)]
     )
-    recv = [swap(sends[0], 2), swap(sends[1], 1), swap(sends[2], 3)]
+    recv = [swap(sends[0], 3), swap(sends[1], 2), swap(sends[2], 1)]
     keep, small, send = small_call(last_kernel, "last", sc, (keep, small, *recv), out[:3])
     recv = swap(send, 7)
     out = [((48, 64), F32), ((10, CH), F32), ((1, CH), F32), ((1, CH), F32)]

time: 97.5 us -> 96.6 us (level); the launches traced: 95.8 us -> 96.2 us
  transfers between devices with their start and end apart: 18 -> 18, of which waited for: 16 -> 17; matrix products, arithmetic and copies ran while one was open for 2% -> 2% of each run, Pallas kernels for 0% -> 0%
where the time goes in v8:
time: 96.6 us; the launch traced here: 96.2 us
  starting transfers between devices  33.9 us (35%)
  waiting for transfers between devices  33 us (34%)
  Pallas kernels  25.9 us (27%)
  local copies, waits for them, and re-layouts  1.83 us (2%)
    ppermute x18, starting transfers between devices, swap(): lax.ppermute(value, ('wide', 'bulk'), [(i, i ^ 8 * wide + bulk) for i in...  33.9 us
    ppermute x18, waiting for transfers between devices, swap(): lax.ppermute(value, ('wide', 'bulk'), [(i, i ^ 8 * wide + bulk) for i in...  33 us
    pallas_call x1, Pallas kernels, window(): pl.pallas_call(window_kernel, grid_spec=pltpu.PrefetchScalarGridSpec(num_...  19.3 us
    pallas_call x7, Pallas kernels, small_call(): pl.pallas_call(kernel, in_specs=[pl.BlockSpec(memory_space=pltpu.SMEM)] +...  5.34 us
  transfers between devices with their start and end apart: 18, of which 17 were waited for; matrix products, arithmetic and copies ran while one was open for 2% of the time, Pallas kernels for 0%

profile of v8, /device:TPU:32, one launch (start us, length us, event | category | flops | bytes accessed | tf_op | source)
XLA Modules:
  0.0 96.2 jit_solution(451656102067485658)
XLA Ops:
  1.8 1.2 %collective-permute-start.2 = (bf16[336,128]{1,0:T(8,128)(2,1)S(1)}, bf16[336,128]{1,0:T(8,128)(2,1)S(1)}, u32[]{:S(2)}, u32[]{:S(2)}) collective-permute-start(bf16[336,128]{1,0:T(8,128)(2,1)S(1)} %rows.1.own), channel_id=1, source_target_pairs={{0,72},{1,73},{2,74},{3,75},{4,76},{5,77},{6,78},{7,79},{8,64},{9,... | collective-permute-start | bytes 258056 | tf_op jit(solution)/shard_map/ppermute | solution.py:423
  3.0 2.2 %collective-permute-start.1 = (bf16[336,128]{1,0:T(8,128)(2,1)S(1)}, bf16[336,128]{1,0:T(8,128)(2,1)S(1)}, u32[]{:S(2)}, u32[]{:S(2)}) collective-permute-start(bf16[336,128]{1,0:T(8,128)(2,1)S(1)} %rows.1.own), channel_id=1, source_target_pairs={{0,64},{1,65},{2,66},{3,67},{4,68},{5,69},{6,70},{7,71},{8,72},{9,... | collective-permute-start | bytes 258056 | tf_op jit(solution)/shard_map/ppermute | solution.py:423
  6.1 2.0 %collective-permute-done.2.got_both = bf16[336,128]{1,0:T(8,128)(2,1)S(1)} collective-permute-done((bf16[336,128]{1,0:T(8,128)(2,1)S(1)}, bf16[336,128]{1,0:T(8,128)(2,1)S(1)}, u32[]{:S(2)}, u32[]{:S(2)}) %collective-permute-start.2) | collective-permute-done | bytes 86048 | tf_op jit(solution)/shard_map/ppermute | solution.py:423
  10.4 4.4 %collective-permute-start.5 = (bf16[336,128]{1,0:T(8,128)(2,1)S(1)}, bf16[336,128]{1,0:T(8,128)(2,1)S(1)}, u32[]{:S(2)}, u32[]{:S(2)}) collective-permute-start(bf16[336,128]{1,0:T(8,128)(2,1)S(1)} %pick1.1.own), channel_id=1, source_target_pairs={{0,208},{1,209},{2,210},{3,211},{4,212},{5,213},{6,214},{7,215},{8... | collective-permute-start | bytes 258056 | tf_op jit(solution)/shard_map/ppermute | solution.py:423
  17.6 2.7 %collective-permute-done.5.got_both = bf16[336,128]{1,0:T(8,128)(2,1)S(1)} collective-permute-done((bf16[336,128]{1,0:T(8,128)(2,1)S(1)}, bf16[336,128]{1,0:T(8,128)(2,1)S(1)}, u32[]{:S(2)}, u32[]{:S(2)}) %collective-permute-start.5) | collective-permute-done | bytes 86048 | tf_op jit(solution)/shard_map/ppermute | solution.py:423
  22.0 5.7 %collective-permute-start.6 = (bf16[336,128]{1,0:T(8,128)(2,1)S(1)}, bf16[336,128]{1,0:T(8,128)(2,1)S(1)}, u32[]{:S(2)}, u32[]{:S(2)}) collective-permute-start(bf16[336,128]{1,0:T(8,128)(2,1)S(1)} %pick2.1.own_rows), channel_id=1, source_target_pairs={{0,56},{1,57},{2,58},{3,59},{4,60},{5,61},{6,62},{7,63},{8,48},{9,... | collective-permute-start | bytes 258056 | tf_op jit(solution)/shard_map/ppermute | solution.py:423
  27.7 2.4 %collective-permute-done.6.moved = bf16[336,128]{1,0:T(8,128)(2,1)S(1)} collective-permute-done((bf16[336,128]{1,0:T(8,128)(2,1)S(1)}, bf16[336,128]{1,0:T(8,128)(2,1)S(1)}, u32[]{:S(2)}, u32[]{:S(2)}) %collective-permute-start.6) | collective-permute-done | bytes 86048 | tf_op jit(solution)/shard_map/ppermute | solution.py:423
  30.6 19.3 %window.1 = (f32[1024,384]{1,0:T(8,128)S(1)}, bf16[1056,384]{1,0:T(8,128)(2,1)S(1)}, f32[16,384]{1,0:T(8,128)S(1)}) custom-call(s32[17]{0:T(128)S(1)} %concatenate.6.sc, bf16[336,128]{1,0:T(8,128)(2,1)S(1)} %pick2.1.own_rows, bf16[336,128]{1,0:T(8,128)(2,1)S(1)} %collective-permute-done.6.moved, f32[40,512]{1,0:T(8,128)S(1)} %concatenate.7.params, ...), custom_call_target="tpu_custom_call" | custom-call | flops 14000000000 | bytes 10000000 | tf_op jit(solution)/shard_map/window/pallas_call | solution.py:368
  50.0 2.3 %collective-permute-done.7.refs_0_ = bf16[1056,384]{1,0:T(8,128)(2,1)S(1)} collective-permute-done((bf16[1056,384]{1,0:T(8,128)(2,1)S(1)}, bf16[1056,384]{1,0:T(8,128)(2,1)S(1)}, u32[]{:S(2)}, u32[]{:S(2)}) %collective-permute-start.7) | collective-permute-done | bytes 811040 | tf_op jit(solution)/shard_map/ppermute | solution.py:423
  53.1 1.4 %collective-permute-start.8 = (bf16[288,384]{1,0:T(8,128)(2,1)S(1)}, bf16[288,384]{1,0:T(8,128)(2,1)S(1)}, u32[]{:S(2)}, u32[]{:S(2)}) collective-permute-start(bf16[288,384]{1,0:T(8,128)(2,1)S(1)} %get-tuple-element.34), channel_id=1, source_target_pairs={{0,66},{1,67},{2,64},{3,65},{4,70},{5,71},{6,68},{7,69},{8,74},{9,... | collective-permute-start | bytes 663560 | tf_op jit(solution)/shard_map/ppermute | solution.py:423
  54.5 1.6 %collective-permute-start.9 = (bf16[288,384]{1,0:T(8,128)(2,1)S(1)}, bf16[288,384]{1,0:T(8,128)(2,1)S(1)}, u32[]{:S(2)}, u32[]{:S(2)}) collective-permute-start(bf16[288,384]{1,0:T(8,128)(2,1)S(1)} %get-tuple-element.35), channel_id=1, source_target_pairs={{0,64},{1,65},{2,66},{3,67},{4,68},{5,69},{6,70},{7,71},{8,72},{9,... | collective-permute-start | bytes 663560 | tf_op jit(solution)/shard_map/ppermute | solution.py:423
  56.7 5.7 %collective-permute-done.8.refs_0_ = bf16[288,384]{1,0:T(8,128)(2,1)S(1)} collective-permute-done((bf16[288,384]{1,0:T(8,128)(2,1)S(1)}, bf16[288,384]{1,0:T(8,128)(2,1)S(1)}, u32[]{:S(2)}, u32[]{:S(2)}) %collective-permute-start.8) | collective-permute-done | bytes 221216 | tf_op jit(solution)/shard_map/ppermute | solution.py:423
  62.4 3.9 %collective-permute-done.9.refs_1_ = bf16[288,384]{1,0:T(8,128)(2,1)S(1)} collective-permute-done((bf16[288,384]{1,0:T(8,128)(2,1)S(1)}, bf16[288,384]{1,0:T(8,128)(2,1)S(1)}, u32[]{:S(2)}, u32[]{:S(2)}) %collective-permute-start.9) | collective-permute-done | bytes 221216 | tf_op jit(solution)/shard_map/ppermute | solution.py:423
  67.0 3.5 %collective-permute-start.11 = (bf16[96,384]{1,0:T(8,128)(2,1)S(1)}, bf16[96,384]{1,0:T(8,128)(2,1)S(1)}, u32[]{:S(2)}, u32[]{:S(2)}) collective-permute-start(bf16[96,384]{1,0:T(8,128)(2,1)S(1)} %get-tuple-element.39), channel_id=1, source_target_pairs={{0,198},{1,199},{2,196},{3,197},{4,194},{5,195},{6,192},{7,193},{8... | collective-permute-start | bytes 221192 | tf_op jit(solution)/shard_map/ppermute | solution.py:423
  70.5 1.5 %collective-permute-start.12 = (bf16[96,384]{1,0:T(8,128)(2,1)S(1)}, bf16[96,384]{1,0:T(8,128)(2,1)S(1)}, u32[]{:S(2)}, u32[]{:S(2)}) collective-permute-start(bf16[96,384]{1,0:T(8,128)(2,1)S(1)} %get-tuple-element.40), channel_id=1, source_target_pairs={{0,192},{1,193},{2,194},{3,195},{4,196},{5,197},{6,198},{7,199},{8... | collective-permute-start | bytes 221192 | tf_op jit(solution)/shard_map/ppermute | solution.py:423
  73.0 1.8 %collective-permute-done.11.r0 = bf16[96,384]{1,0:T(8,128)(2,1)S(1)} collective-permute-done((bf16[96,384]{1,0:T(8,128)(2,1)S(1)}, bf16[96,384]{1,0:T(8,128)(2,1)S(1)}, u32[]{:S(2)}, u32[]{:S(2)}) %collective-permute-start.11) | collective-permute-done | bytes 73760 | tf_op jit(solution)/shard_map/ppermute | solution.py:423
  74.8 1.4 %collective-permute-done.12.r1 = bf16[96,384]{1,0:T(8,128)(2,1)S(1)} collective-permute-done((bf16[96,384]{1,0:T(8,128)(2,1)S(1)}, bf16[96,384]{1,0:T(8,128)(2,1)S(1)}, u32[]{:S(2)}, u32[]{:S(2)}) %collective-permute-start.12) | collective-permute-done | bytes 73760 | tf_op jit(solution)/shard_map/ppermute | solution.py:423
  76.2 1.4 %collective-permute-done.13.r2 = bf16[96,384]{1,0:T(8,128)(2,1)S(1)} collective-permute-done((bf16[96,384]{1,0:T(8,128)(2,1)S(1)}, bf16[96,384]{1,0:T(8,128)(2,1)S(1)}, u32[]{:S(2)}, u32[]{:S(2)}) %collective-permute-start.13) | collective-permute-done | bytes 73760 | tf_op jit(solution)/shard_map/ppermute | solution.py:423
  79.3 3.7 %collective-permute-start.15 = (f32[96,128]{1,0:T(8,128)S(1)}, f32[96,128]{1,0:T(8,128)S(1)}, u32[]{:S(2)}, u32[]{:S(2)}) collective-permute-start(f32[96,128]{1,0:T(8,128)S(1)} %get-tuple-element.45), channel_id=1, source_target_pairs={{0,16},{1,17},{2,18},{3,19},{4,20},{5,21},{6,22},{7,23},{8,24},{9,... | collective-permute-start | bytes 147464 | tf_op jit(solution)/shard_map/ppermute | solution.py:423
  83.8 1.9 %collective-permute-done.15.r1 = f32[96,128]{1,0:T(8,128)S(1)} collective-permute-done((f32[96,128]{1,0:T(8,128)S(1)}, f32[96,128]{1,0:T(8,128)S(1)}, u32[]{:S(2)}, u32[]{:S(2)}) %collective-permute-start.15) | collective-permute-done | bytes 49184 | tf_op jit(solution)/shard_map/ppermute | solution.py:423
  85.7 1.5 %collective-permute-done.16.r2 = f32[96,128]{1,0:T(8,128)S(1)} collective-permute-done((f32[96,128]{1,0:T(8,128)S(1)}, f32[96,128]{1,0:T(8,128)S(1)}, u32[]{:S(2)}, u32[]{:S(2)}) %collective-permute-start.16) | collective-permute-done | bytes 49184 | tf_op jit(solution)/shard_map/ppermute | solution.py:423
  87.7 4.5 %collective-permute-start.17 = (f32[96,128]{1,0:T(8,128)S(1)}, f32[96,128]{1,0:T(8,128)S(1)}, u32[]{:S(2)}, u32[]{:S(2)}) collective-permute-start(f32[96,128]{1,0:T(8,128)S(1)} %get-tuple-element.49), channel_id=1, source_target_pairs={{0,56},{1,57},{2,58},{3,59},{4,60},{5,61},{6,62},{7,63},{8,48},{9,... | collective-permute-start | bytes 147464 | tf_op jit(solution)/shard_map/ppermute | solution.py:423
  92.3 2.7 %collective-permute-done.17.recv = f32[96,128]{1,0:T(8,128)S(1)} collective-permute-done((f32[96,128]{1,0:T(8,128)S(1)}, f32[96,128]{1,0:T(8,128)S(1)}, u32[]{:S(2)}, u32[]{:S(2)}) %collective-permute-start.17) | collective-permute-done | bytes 49184 | tf_op jit(solution)/shard_map/ppermute | solution.py:423
  94.9 1.3 %final.1 = (f32[48,64]{1,0:T(8,128)}, f32[10,512]{1,0:T(8,128)}, f32[1,512]{1,0:T(1,128)}, f32[1,512]{1,0:T(1,128)}) custom-call(s32[17]{0:T(128)S(1)} %concatenate.6.sc, f32[48,128]{1,0:T(8,128)S(1)} %get-tuple-element.47.keep, f32[48,128]{1,0:T(8,128)S(1)} %get-tuple-element.48.small, f32[96,128]{1,0:T(8,128)S(1)} %collective-permute-done.17.recv), custom_call_target="tpu_custom_call" | custom-call | tf_op jit(solution)/shard_map/final/pallas_call | solution.py:411
  (32 shorter events, 15.4 us)
Async XLA Ops:
  1.8 6.2 %collective-permute-start.2 = (bf16[336,128]{1,0:T(8,128)(2,1)S(1)}, bf16[336,128]{1,0:T(8,128)(2,1)S(1)}, u32[]{:S(2)}, u32[]{:S(2)}) collective-permute-start(bf16[336,128]{1,0:T(8,128)(2,1)S(1)} %rows.1.own), channel_id=1, source_target_pairs={{0,72},{1,73},{2,74},{3,75},{4,76},{5,77},{6,78},{7,79},{8,64},{9,... | collective-permute-start | bytes 258056 | tf_op jit(solution)/shard_map/ppermute | solution.py:423
  3.0 5.8 %collective-permute-start.1 = (bf16[336,128]{1,0:T(8,128)(2,1)S(1)}, bf16[336,128]{1,0:T(8,128)(2,1)S(1)}, u32[]{:S(2)}, u32[]{:S(2)}) collective-permute-start(bf16[336,128]{1,0:T(8,128)(2,1)S(1)} %rows.1.own), channel_id=1, source_target_pairs={{0,64},{1,65},{2,66},{3,67},{4,68},{5,69},{6,70},{7,71},{8,72},{9,... | collective-permute-start | bytes 258056 | tf_op jit(solution)/shard_map/ppermute | solution.py:423
  5.2 4.5 %collective-permute-start = (bf16[336,128]{1,0:T(8,128)(2,1)S(1)}, bf16[336,128]{1,0:T(8,128)(2,1)S(1)}, u32[]{:S(2)}, u32[]{:S(2)}) collective-permute-start(bf16[336,128]{1,0:T(8,128)(2,1)S(1)} %rows.1.own), channel_id=1, source_target_pairs={{0,8},{1,9},{2,10},{3,11},{4,12},{5,13},{6,14},{7,15},{8,0},{9,1},... | collective-permute-start | bytes 258056 | tf_op jit(solution)/shard_map/ppermute | solution.py:423
  10.4 9.9 %collective-permute-start.5 = (bf16[336,128]{1,0:T(8,128)(2,1)S(1)}, bf16[336,128]{1,0:T(8,128)(2,1)S(1)}, u32[]{:S(2)}, u32[]{:S(2)}) collective-permute-start(bf16[336,128]{1,0:T(8,128)(2,1)S(1)} %pick1.1.own), channel_id=1, source_target_pairs={{0,208},{1,209},{2,210},{3,211},{4,212},{5,213},{6,214},{7,215},{8... | collective-permute-start | bytes 258056 | tf_op jit(solution)/shard_map/ppermute | solution.py:423
  14.8 5.7 %collective-permute-start.4 = (bf16[336,128]{1,0:T(8,128)(2,1)S(1)}, bf16[336,128]{1,0:T(8,128)(2,1)S(1)}, u32[]{:S(2)}, u32[]{:S(2)}) collective-permute-start(bf16[336,128]{1,0:T(8,128)(2,1)S(1)} %pick1.1.own), channel_id=1, source_target_pairs={{0,192},{1,193},{2,194},{3,195},{4,196},{5,197},{6,198},{7,199},{8... | collective-permute-start | bytes 258056 | tf_op jit(solution)/shard_map/ppermute | solution.py:423
  15.7 5.6 %collective-permute-start.3 = (bf16[336,128]{1,0:T(8,128)(2,1)S(1)}, bf16[336,128]{1,0:T(8,128)(2,1)S(1)}, u32[]{:S(2)}, u32[]{:S(2)}) collective-permute-start(bf16[336,128]{1,0:T(8,128)(2,1)S(1)} %pick1.1.own), channel_id=1, source_target_pairs={{0,16},{1,17},{2,18},{3,19},{4,20},{5,21},{6,22},{7,23},{8,24},{9,... | collective-permute-start | bytes 258056 | tf_op jit(solution)/shard_map/ppermute | solution.py:423
  22.0 8.2 %collective-permute-start.6 = (bf16[336,128]{1,0:T(8,128)(2,1)S(1)}, bf16[336,128]{1,0:T(8,128)(2,1)S(1)}, u32[]{:S(2)}, u32[]{:S(2)}) collective-permute-start(bf16[336,128]{1,0:T(8,128)(2,1)S(1)} %pick2.1.own_rows), channel_id=1, source_target_pairs={{0,56},{1,57},{2,58},{3,59},{4,60},{5,61},{6,62},{7,63},{8,48},{9,... | collective-permute-start | bytes 258056 | tf_op jit(solution)/shard_map/ppermute | solution.py:423
  49.9 2.4 %collective-permute-start.7 = (bf16[1056,384]{1,0:T(8,128)(2,1)S(1)}, bf16[1056,384]{1,0:T(8,128)(2,1)S(1)}, u32[]{:S(2)}, u32[]{:S(2)}) collective-permute-start(bf16[1056,384]{1,0:T(8,128)(2,1)S(1)} %get-tuple-element.31), channel_id=1, source_target_pairs={{0,1},{1,0},{2,3},{3,2},{4,5},{5,4},{6,7},{7,6},{8,9},{9,8},{10,11... | collective-permute-start | bytes 2433032 | tf_op jit(solution)/shard_map/ppermute | solution.py:423
  53.1 9.3 %collective-permute-start.8 = (bf16[288,384]{1,0:T(8,128)(2,1)S(1)}, bf16[288,384]{1,0:T(8,128)(2,1)S(1)}, u32[]{:S(2)}, u32[]{:S(2)}) collective-permute-start(bf16[288,384]{1,0:T(8,128)(2,1)S(1)} %get-tuple-element.34), channel_id=1, source_target_pairs={{0,66},{1,67},{2,64},{3,65},{4,70},{5,71},{6,68},{7,69},{8,74},{9,... | collective-permute-start | bytes 663560 | tf_op jit(solution)/shard_map/ppermute | solution.py:423
  54.5 11.8 %collective-permute-start.9 = (bf16[288,384]{1,0:T(8,128)(2,1)S(1)}, bf16[288,384]{1,0:T(8,128)(2,1)S(1)}, u32[]{:S(2)}, u32[]{:S(2)}) collective-permute-start(bf16[288,384]{1,0:T(8,128)(2,1)S(1)} %get-tuple-element.35), channel_id=1, source_target_pairs={{0,64},{1,65},{2,66},{3,67},{4,68},{5,69},{6,70},{7,71},{8,72},{9,... | collective-permute-start | bytes 663560 | tf_op jit(solution)/shard_map/ppermute | solution.py:423
  56.2 10.2 %collective-permute-start.10 = (bf16[288,384]{1,0:T(8,128)(2,1)S(1)}, bf16[288,384]{1,0:T(8,128)(2,1)S(1)}, u32[]{:S(2)}, u32[]{:S(2)}) collective-permute-start(bf16[288,384]{1,0:T(8,128)(2,1)S(1)} %get-tuple-element.36), channel_id=1, source_target_pairs={{0,2},{1,3},{2,0},{3,1},{4,6},{5,7},{6,4},{7,5},{8,10},{9,11},{10,... | collective-permute-start | bytes 663560 | tf_op jit(solution)/shard_map/ppermute | solution.py:423
  67.0 7.8 %collective-permute-start.11 = (bf16[96,384]{1,0:T(8,128)(2,1)S(1)}, bf16[96,384]{1,0:T(8,128)(2,1)S(1)}, u32[]{:S(2)}, u32[]{:S(2)}) collective-permute-start(bf16[96,384]{1,0:T(8,128)(2,1)S(1)} %get-tuple-element.39), channel_id=1, source_target_pairs={{0,198},{1,199},{2,196},{3,197},{4,194},{5,195},{6,192},{7,193},{8... | collective-permute-start | bytes 221192 | tf_op jit(solution)/shard_map/ppermute | solution.py:423
  70.5 5.7 %collective-permute-start.12 = (bf16[96,384]{1,0:T(8,128)(2,1)S(1)}, bf16[96,384]{1,0:T(8,128)(2,1)S(1)}, u32[]{:S(2)}, u32[]{:S(2)}) collective-permute-start(bf16[96,384]{1,0:T(8,128)(2,1)S(1)} %get-tuple-element.40), channel_id=1, source_target_pairs={{0,192},{1,193},{2,194},{3,195},{4,196},{5,197},{6,198},{7,199},{8... | collective-permute-start | bytes 221192 | tf_op jit(solution)/shard_map/ppermute | solution.py:423
  72.0 5.6 %collective-permute-start.13 = (bf16[96,384]{1,0:T(8,128)(2,1)S(1)}, bf16[96,384]{1,0:T(8,128)(2,1)S(1)}, u32[]{:S(2)}, u32[]{:S(2)}) collective-permute-start(bf16[96,384]{1,0:T(8,128)(2,1)S(1)} %get-tuple-element.41), channel_id=1, source_target_pairs={{0,6},{1,7},{2,4},{3,5},{4,2},{5,3},{6,0},{7,1},{8,14},{9,15},{10,... | collective-permute-start | bytes 221192 | tf_op jit(solution)/shard_map/ppermute | solution.py:423
  78.3 5.4 %collective-permute-start.14 = (f32[96,128]{1,0:T(8,128)S(1)}, f32[96,128]{1,0:T(8,128)S(1)}, u32[]{:S(2)}, u32[]{:S(2)}) collective-permute-start(f32[96,128]{1,0:T(8,128)S(1)} %get-tuple-element.44), channel_id=1, source_target_pairs={{0,24},{1,25},{2,26},{3,27},{4,28},{5,29},{6,30},{7,31},{8,16},{9,... | collective-permute-start | bytes 147464 | tf_op jit(solution)/shard_map/ppermute | solution.py:423
  79.3 6.3 %collective-permute-start.15 = (f32[96,128]{1,0:T(8,128)S(1)}, f32[96,128]{1,0:T(8,128)S(1)}, u32[]{:S(2)}, u32[]{:S(2)}) collective-permute-start(f32[96,128]{1,0:T(8,128)S(1)} %get-tuple-element.45), channel_id=1, source_target_pairs={{0,16},{1,17},{2,18},{3,19},{4,20},{5,21},{6,22},{7,23},{8,24},{9,... | collective-permute-start | bytes 147464 | tf_op jit(solution)/shard_map/ppermute | solution.py:423
  83.1 4.1 %collective-permute-start.16 = (f32[96,128]{1,0:T(8,128)S(1)}, f32[96,128]{1,0:T(8,128)S(1)}, u32[]{:S(2)}, u32[]{:S(2)}) collective-permute-start(f32[96,128]{1,0:T(8,128)S(1)} %get-tuple-element.46), channel_id=1, source_target_pairs={{0,8},{1,9},{2,10},{3,11},{4,12},{5,13},{6,14},{7,15},{8,0},{9,1},... | collective-permute-start | bytes 147464 | tf_op jit(solution)/shard_map/ppermute | solution.py:423
  87.7 7.2 %collective-permute-start.17 = (f32[96,128]{1,0:T(8,128)S(1)}, f32[96,128]{1,0:T(8,128)S(1)}, u32[]{:S(2)}, u32[]{:S(2)}) collective-permute-start(f32[96,128]{1,0:T(8,128)S(1)} %get-tuple-element.49), channel_id=1, source_target_pairs={{0,56},{1,57},{2,58},{3,59},{4,60},{5,61},{6,62},{7,63},{8,48},{9,... | collective-permute-start | bytes 147464 | tf_op jit(solution)/shard_map/ppermute | solution.py:423

commit v9 on v8

--- a/solution.py
+++ b/solution.py
@@ -475,7 +475,7 @@
 def route(waves, lengths, masks):
     out = [((336, 128), BF16)]
     value = lay_rows(lengths, waves)
-    for a, b in ((1, 8), (2, 24)):
+    for a, b in ((2, 24), (1, 8)):
         got = [swap(value, a), swap(value, b), swap(value, a ^ b)]
         (value,) = small_call(functools.partial(pick_kernel, a == 1), "pick%d" % a, masks, (value, *got), out)
     moved = swap(value, 7)

time: 96.6 us -> 96.6 us (level)
  no operation moved by 1% of the time
where the time goes in v9:
time: 96.6 us; the launch traced here: 96.2 us
  starting transfers between devices  34.3 us (36%)
  waiting for transfers between devices  32.7 us (34%)
  Pallas kernels  25.9 us (27%)
  local copies, waits for them, and re-layouts  1.83 us (2%)
    ppermute x18, starting transfers between devices, swap(): lax.ppermute(value, ('wide', 'bulk'), [(i, i ^ 8 * wide + bulk) for i in...  34.3 us
    ppermute x18, waiting for transfers between devices, swap(): lax.ppermute(value, ('wide', 'bulk'), [(i, i ^ 8 * wide + bulk) for i in...  32.7 us
    pallas_call x1, Pallas kernels, window(): pl.pallas_call(window_kernel, grid_spec=pltpu.PrefetchScalarGridSpec(num_...  19.3 us
    pallas_call x7, Pallas kernels, small_call(): pl.pallas_call(kernel, in_specs=[pl.BlockSpec(memory_space=pltpu.SMEM)] +...  5.34 us
  transfers between devices with their start and end apart: 18, of which 17 were waited for; matrix products, arithmetic and copies ran while one was open for 2% of the time, Pallas kernels for 0%

profile of v9, /device:TPU:32, one launch (start us, length us, event | category | flops | bytes accessed | tf_op | source)
XLA Modules:
  0.0 96.2 jit_solution(8534506565155747091)
XLA Ops:
  0.6 1.2 %rows.1.own = bf16[336,128]{1,0:T(8,128)(2,1)S(1)} custom-call(s32[4]{0:T(128)} %bitcast.22, bf16[4,10240]{1,0:T(4,128)(2,1)} %bitcast.19), custom_call_target="tpu_custom_call" | custom-call | tf_op jit(solution)/shard_map/rows/pallas_call | solution.py:441
  1.8 5.8 %collective-permute-start.2 = (bf16[336,128]{1,0:T(8,128)(2,1)S(1)}, bf16[336,128]{1,0:T(8,128)(2,1)S(1)}, u32[]{:S(2)}, u32[]{:S(2)}) collective-permute-start(bf16[336,128]{1,0:T(8,128)(2,1)S(1)} %rows.1.own), channel_id=1, source_target_pairs={{0,208},{1,209},{2,210},{3,211},{4,212},{5,213},{6,214},{7,215},{8... | collective-permute-start | bytes 258056 | tf_op jit(solution)/shard_map/ppermute | solution.py:423
  9.0 3.8 %collective-permute-done.2.got_both = bf16[336,128]{1,0:T(8,128)(2,1)S(1)} collective-permute-done((bf16[336,128]{1,0:T(8,128)(2,1)S(1)}, bf16[336,128]{1,0:T(8,128)(2,1)S(1)}, u32[]{:S(2)}, u32[]{:S(2)}) %collective-permute-start.2) | collective-permute-done | bytes 86048 | tf_op jit(solution)/shard_map/ppermute | solution.py:423
  15.7 1.9 %collective-permute-start.4 = (bf16[336,128]{1,0:T(8,128)(2,1)S(1)}, bf16[336,128]{1,0:T(8,128)(2,1)S(1)}, u32[]{:S(2)}, u32[]{:S(2)}) collective-permute-start(bf16[336,128]{1,0:T(8,128)(2,1)S(1)} %pick2.1.own), channel_id=1, source_target_pairs={{0,64},{1,65},{2,66},{3,67},{4,68},{5,69},{6,70},{7,71},{8,72},{9,... | collective-permute-start | bytes 258056 | tf_op jit(solution)/shard_map/ppermute | solution.py:423
  20.3 1.3 %collective-permute-done.5.got_both = bf16[336,128]{1,0:T(8,128)(2,1)S(1)} collective-permute-done((bf16[336,128]{1,0:T(8,128)(2,1)S(1)}, bf16[336,128]{1,0:T(8,128)(2,1)S(1)}, u32[]{:S(2)}, u32[]{:S(2)}) %collective-permute-start.5) | collective-permute-done | bytes 86048 | tf_op jit(solution)/shard_map/ppermute | solution.py:423
  22.7 6.8 %collective-permute-start.6 = (bf16[336,128]{1,0:T(8,128)(2,1)S(1)}, bf16[336,128]{1,0:T(8,128)(2,1)S(1)}, u32[]{:S(2)}, u32[]{:S(2)}) collective-permute-start(bf16[336,128]{1,0:T(8,128)(2,1)S(1)} %pick1.1.own_rows), channel_id=1, source_target_pairs={{0,56},{1,57},{2,58},{3,59},{4,60},{5,61},{6,62},{7,63},{8,48},{9,... | collective-permute-start | bytes 258056 | tf_op jit(solution)/shard_map/ppermute | solution.py:423
  29.6 2.4 %collective-permute-done.6.moved = bf16[336,128]{1,0:T(8,128)(2,1)S(1)} collective-permute-done((bf16[336,128]{1,0:T(8,128)(2,1)S(1)}, bf16[336,128]{1,0:T(8,128)(2,1)S(1)}, u32[]{:S(2)}, u32[]{:S(2)}) %collective-permute-start.6) | collective-permute-done | bytes 86048 | tf_op jit(solution)/shard_map/ppermute | solution.py:423
  32.5 19.3 %window.1 = (f32[1024,384]{1,0:T(8,128)S(1)}, bf16[1056,384]{1,0:T(8,128)(2,1)S(1)}, f32[16,384]{1,0:T(8,128)S(1)}) custom-call(s32[17]{0:T(128)S(1)} %concatenate.6.sc, bf16[336,128]{1,0:T(8,128)(2,1)S(1)} %pick1.1.own_rows, bf16[336,128]{1,0:T(8,128)(2,1)S(1)} %collective-permute-done.6.moved, f32[40,512]{1,0:T(8,128)S(1)} %concatenate.7.params, ...), custom_call_target="tpu_custom_call" | custom-call | flops 14000000000 | bytes 10000000 | tf_op jit(solution)/shard_map/window/pallas_call | solution.py:368
  51.9 2.3 %collective-permute-done.7.refs_0_ = bf16[1056,384]{1,0:T(8,128)(2,1)S(1)} collective-permute-done((bf16[1056,384]{1,0:T(8,128)(2,1)S(1)}, bf16[1056,384]{1,0:T(8,128)(2,1)S(1)}, u32[]{:S(2)}, u32[]{:S(2)}) %collective-permute-start.7) | collective-permute-done | bytes 811040 | tf_op jit(solution)/shard_map/ppermute | solution.py:423
  55.0 1.3 %collective-permute-start.8 = (bf16[288,384]{1,0:T(8,128)(2,1)S(1)}, bf16[288,384]{1,0:T(8,128)(2,1)S(1)}, u32[]{:S(2)}, u32[]{:S(2)}) collective-permute-start(bf16[288,384]{1,0:T(8,128)(2,1)S(1)} %get-tuple-element.34), channel_id=1, source_target_pairs={{0,66},{1,67},{2,64},{3,65},{4,70},{5,71},{6,68},{7,69},{8,74},{9,... | collective-permute-start | bytes 663560 | tf_op jit(solution)/shard_map/ppermute | solution.py:423
  56.3 1.8 %collective-permute-start.9 = (bf16[288,384]{1,0:T(8,128)(2,1)S(1)}, bf16[288,384]{1,0:T(8,128)(2,1)S(1)}, u32[]{:S(2)}, u32[]{:S(2)}) collective-permute-start(bf16[288,384]{1,0:T(8,128)(2,1)S(1)} %get-tuple-element.35), channel_id=1, source_target_pairs={{0,64},{1,65},{2,66},{3,67},{4,68},{5,69},{6,70},{7,71},{8,72},{9,... | collective-permute-start | bytes 663560 | tf_op jit(solution)/shard_map/ppermute | solution.py:423
  58.6 5.7 %collective-permute-done.8.refs_0_ = bf16[288,384]{1,0:T(8,128)(2,1)S(1)} collective-permute-done((bf16[288,384]{1,0:T(8,128)(2,1)S(1)}, bf16[288,384]{1,0:T(8,128)(2,1)S(1)}, u32[]{:S(2)}, u32[]{:S(2)}) %collective-permute-start.8) | collective-permute-done | bytes 221216 | tf_op jit(solution)/shard_map/ppermute | solution.py:423
  64.3 3.9 %collective-permute-done.9.refs_1_ = bf16[288,384]{1,0:T(8,128)(2,1)S(1)} collective-permute-done((bf16[288,384]{1,0:T(8,128)(2,1)S(1)}, bf16[288,384]{1,0:T(8,128)(2,1)S(1)}, u32[]{:S(2)}, u32[]{:S(2)}) %collective-permute-start.9) | collective-permute-done | bytes 221216 | tf_op jit(solution)/shard_map/ppermute | solution.py:423
  68.8 3.1 %collective-permute-start.11 = (bf16[96,384]{1,0:T(8,128)(2,1)S(1)}, bf16[96,384]{1,0:T(8,128)(2,1)S(1)}, u32[]{:S(2)}, u32[]{:S(2)}) collective-permute-start(bf16[96,384]{1,0:T(8,128)(2,1)S(1)} %get-tuple-element.39), channel_id=1, source_target_pairs={{0,198},{1,199},{2,196},{3,197},{4,194},{5,195},{6,192},{7,193},{8... | collective-permute-start | bytes 221192 | tf_op jit(solution)/shard_map/ppermute | solution.py:423
  71.9 1.8 %collective-permute-start.12 = (bf16[96,384]{1,0:T(8,128)(2,1)S(1)}, bf16[96,384]{1,0:T(8,128)(2,1)S(1)}, u32[]{:S(2)}, u32[]{:S(2)}) collective-permute-start(bf16[96,384]{1,0:T(8,128)(2,1)S(1)} %get-tuple-element.40), channel_id=1, source_target_pairs={{0,192},{1,193},{2,194},{3,195},{4,196},{5,197},{6,198},{7,199},{8... | collective-permute-start | bytes 221192 | tf_op jit(solution)/shard_map/ppermute | solution.py:423
  74.8 1.8 %collective-permute-done.11.r0 = bf16[96,384]{1,0:T(8,128)(2,1)S(1)} collective-permute-done((bf16[96,384]{1,0:T(8,128)(2,1)S(1)}, bf16[96,384]{1,0:T(8,128)(2,1)S(1)}, u32[]{:S(2)}, u32[]{:S(2)}) %collective-permute-start.11) | collective-permute-done | bytes 73760 | tf_op jit(solution)/shard_map/ppermute | solution.py:423
  76.7 1.3 %collective-permute-done.12.r1 = bf16[96,384]{1,0:T(8,128)(2,1)S(1)} collective-permute-done((bf16[96,384]{1,0:T(8,128)(2,1)S(1)}, bf16[96,384]{1,0:T(8,128)(2,1)S(1)}, u32[]{:S(2)}, u32[]{:S(2)}) %collective-permute-start.12) | collective-permute-done | bytes 73760 | tf_op jit(solution)/shard_map/ppermute | solution.py:423
  78.0 1.3 %collective-permute-done.13.r2 = bf16[96,384]{1,0:T(8,128)(2,1)S(1)} collective-permute-done((bf16[96,384]{1,0:T(8,128)(2,1)S(1)}, bf16[96,384]{1,0:T(8,128)(2,1)S(1)}, u32[]{:S(2)}, u32[]{:S(2)}) %collective-permute-start.13) | collective-permute-done | bytes 73760 | tf_op jit(solution)/shard_map/ppermute | solution.py:423
  80.1 1.6 %collective-permute-start.14 = (f32[96,128]{1,0:T(8,128)S(1)}, f32[96,128]{1,0:T(8,128)S(1)}, u32[]{:S(2)}, u32[]{:S(2)}) collective-permute-start(f32[96,128]{1,0:T(8,128)S(1)} %get-tuple-element.44), channel_id=1, source_target_pairs={{0,24},{1,25},{2,26},{3,27},{4,28},{5,29},{6,30},{7,31},{8,16},{9,... | collective-permute-start | bytes 147464 | tf_op jit(solution)/shard_map/ppermute | solution.py:423
  81.7 1.4 %collective-permute-start.15 = (f32[96,128]{1,0:T(8,128)S(1)}, f32[96,128]{1,0:T(8,128)S(1)}, u32[]{:S(2)}, u32[]{:S(2)}) collective-permute-start(f32[96,128]{1,0:T(8,128)S(1)} %get-tuple-element.45), channel_id=1, source_target_pairs={{0,16},{1,17},{2,18},{3,19},{4,20},{5,21},{6,22},{7,23},{8,24},{9,... | collective-permute-start | bytes 147464 | tf_op jit(solution)/shard_map/ppermute | solution.py:423
  84.3 2.5 %collective-permute-done.15.r1 = f32[96,128]{1,0:T(8,128)S(1)} collective-permute-done((f32[96,128]{1,0:T(8,128)S(1)}, f32[96,128]{1,0:T(8,128)S(1)}, u32[]{:S(2)}, u32[]{:S(2)}) %collective-permute-start.15) | collective-permute-done | bytes 49184 | tf_op jit(solution)/shard_map/ppermute | solution.py:423
  87.8 4.2 %collective-permute-start.17 = (f32[96,128]{1,0:T(8,128)S(1)}, f32[96,128]{1,0:T(8,128)S(1)}, u32[]{:S(2)}, u32[]{:S(2)}) collective-permute-start(f32[96,128]{1,0:T(8,128)S(1)} %get-tuple-element.49), channel_id=1, source_target_pairs={{0,56},{1,57},{2,58},{3,59},{4,60},{5,61},{6,62},{7,63},{8,48},{9,... | collective-permute-start | bytes 147464 | tf_op jit(solution)/shard_map/ppermute | solution.py:423
  91.9 3.0 %collective-permute-done.17.recv = f32[96,128]{1,0:T(8,128)S(1)} collective-permute-done((f32[96,128]{1,0:T(8,128)S(1)}, f32[96,128]{1,0:T(8,128)S(1)}, u32[]{:S(2)}, u32[]{:S(2)}) %collective-permute-start.17) | collective-permute-done | bytes 49184 | tf_op jit(solution)/shard_map/ppermute | solution.py:423
  94.9 1.3 %final.1 = (f32[48,64]{1,0:T(8,128)}, f32[10,512]{1,0:T(8,128)}, f32[1,512]{1,0:T(1,128)}, f32[1,512]{1,0:T(1,128)}) custom-call(s32[17]{0:T(128)S(1)} %concatenate.6.sc, f32[48,128]{1,0:T(8,128)S(1)} %get-tuple-element.47.keep, f32[48,128]{1,0:T(8,128)S(1)} %get-tuple-element.48.small, f32[96,128]{1,0:T(8,128)S(1)} %collective-permute-done.17.recv), custom_call_target="tpu_custom_call" | custom-call | tf_op jit(solution)/shard_map/final/pallas_call | solution.py:411
  (32 shorter events, 14.7 us)
Async XLA Ops:
  1.8 10.9 %collective-permute-start.2 = (bf16[336,128]{1,0:T(8,128)(2,1)S(1)}, bf16[336,128]{1,0:T(8,128)(2,1)S(1)}, u32[]{:S(2)}, u32[]{:S(2)}) collective-permute-start(bf16[336,128]{1,0:T(8,128)(2,1)S(1)} %rows.1.own), channel_id=1, source_target_pairs={{0,208},{1,209},{2,210},{3,211},{4,212},{5,213},{6,214},{7,215},{8... | collective-permute-start | bytes 258056 | tf_op jit(solution)/shard_map/ppermute | solution.py:423
  7.6 5.7 %collective-permute-start.1 = (bf16[336,128]{1,0:T(8,128)(2,1)S(1)}, bf16[336,128]{1,0:T(8,128)(2,1)S(1)}, u32[]{:S(2)}, u32[]{:S(2)}) collective-permute-start(bf16[336,128]{1,0:T(8,128)(2,1)S(1)} %rows.1.own), channel_id=1, source_target_pairs={{0,192},{1,193},{2,194},{3,195},{4,196},{5,197},{6,198},{7,199},{8... | collective-permute-start | bytes 258056 | tf_op jit(solution)/shard_map/ppermute | solution.py:423
  7.9 6.6 %collective-permute-start = (bf16[336,128]{1,0:T(8,128)(2,1)S(1)}, bf16[336,128]{1,0:T(8,128)(2,1)S(1)}, u32[]{:S(2)}, u32[]{:S(2)}) collective-permute-start(bf16[336,128]{1,0:T(8,128)(2,1)S(1)} %rows.1.own), channel_id=1, source_target_pairs={{0,16},{1,17},{2,18},{3,19},{4,20},{5,21},{6,22},{7,23},{8,24},{9,... | collective-permute-start | bytes 258056 | tf_op jit(solution)/shard_map/ppermute | solution.py:423
  15.2 6.4 %collective-permute-start.5 = (bf16[336,128]{1,0:T(8,128)(2,1)S(1)}, bf16[336,128]{1,0:T(8,128)(2,1)S(1)}, u32[]{:S(2)}, u32[]{:S(2)}) collective-permute-start(bf16[336,128]{1,0:T(8,128)(2,1)S(1)} %pick2.1.own), channel_id=1, source_target_pairs={{0,72},{1,73},{2,74},{3,75},{4,76},{5,77},{6,78},{7,79},{8,64},{9,... | collective-permute-start | bytes 258056 | tf_op jit(solution)/shard_map/ppermute | solution.py:423
  15.7 5.9 %collective-permute-start.4 = (bf16[336,128]{1,0:T(8,128)(2,1)S(1)}, bf16[336,128]{1,0:T(8,128)(2,1)S(1)}, u32[]{:S(2)}, u32[]{:S(2)}) collective-permute-start(bf16[336,128]{1,0:T(8,128)(2,1)S(1)} %pick2.1.own), channel_id=1, source_target_pairs={{0,64},{1,65},{2,66},{3,67},{4,68},{5,69},{6,70},{7,71},{8,72},{9,... | collective-permute-start | bytes 258056 | tf_op jit(solution)/shard_map/ppermute | solution.py:423
  17.6 4.5 %collective-permute-start.3 = (bf16[336,128]{1,0:T(8,128)(2,1)S(1)}, bf16[336,128]{1,0:T(8,128)(2,1)S(1)}, u32[]{:S(2)}, u32[]{:S(2)}) collective-permute-start(bf16[336,128]{1,0:T(8,128)(2,1)S(1)} %pick2.1.own), channel_id=1, source_target_pairs={{0,8},{1,9},{2,10},{3,11},{4,12},{5,13},{6,14},{7,15},{8,0},{9,1},... | collective-permute-start | bytes 258056 | tf_op jit(solution)/shard_map/ppermute | solution.py:423
  22.7 9.3 %collective-permute-start.6 = (bf16[336,128]{1,0:T(8,128)(2,1)S(1)}, bf16[336,128]{1,0:T(8,128)(2,1)S(1)}, u32[]{:S(2)}, u32[]{:S(2)}) collective-permute-start(bf16[336,128]{1,0:T(8,128)(2,1)S(1)} %pick1.1.own_rows), channel_id=1, source_target_pairs={{0,56},{1,57},{2,58},{3,59},{4,60},{5,61},{6,62},{7,63},{8,48},{9,... | collective-permute-start | bytes 258056 | tf_op jit(solution)/shard_map/ppermute | solution.py:423
  51.8 2.4 %collective-permute-start.7 = (bf16[1056,384]{1,0:T(8,128)(2,1)S(1)}, bf16[1056,384]{1,0:T(8,128)(2,1)S(1)}, u32[]{:S(2)}, u32[]{:S(2)}) collective-permute-start(bf16[1056,384]{1,0:T(8,128)(2,1)S(1)} %get-tuple-element.31), channel_id=1, source_target_pairs={{0,1},{1,0},{2,3},{3,2},{4,5},{5,4},{6,7},{7,6},{8,9},{9,8},{10,11... | collective-permute-start | bytes 2433032 | tf_op jit(solution)/shard_map/ppermute | solution.py:423
  55.0 9.3 %collective-permute-start.8 = (bf16[288,384]{1,0:T(8,128)(2,1)S(1)}, bf16[288,384]{1,0:T(8,128)(2,1)S(1)}, u32[]{:S(2)}, u32[]{:S(2)}) collective-permute-start(bf16[288,384]{1,0:T(8,128)(2,1)S(1)} %get-tuple-element.34), channel_id=1, source_target_pairs={{0,66},{1,67},{2,64},{3,65},{4,70},{5,71},{6,68},{7,69},{8,74},{9,... | collective-permute-start | bytes 663560 | tf_op jit(solution)/shard_map/ppermute | solution.py:423
  56.3 11.9 %collective-permute-start.9 = (bf16[288,384]{1,0:T(8,128)(2,1)S(1)}, bf16[288,384]{1,0:T(8,128)(2,1)S(1)}, u32[]{:S(2)}, u32[]{:S(2)}) collective-permute-start(bf16[288,384]{1,0:T(8,128)(2,1)S(1)} %get-tuple-element.35), channel_id=1, source_target_pairs={{0,64},{1,65},{2,66},{3,67},{4,68},{5,69},{6,70},{7,71},{8,72},{9,... | collective-permute-start | bytes 663560 | tf_op jit(solution)/shard_map/ppermute | solution.py:423
  58.0 10.2 %collective-permute-start.10 = (bf16[288,384]{1,0:T(8,128)(2,1)S(1)}, bf16[288,384]{1,0:T(8,128)(2,1)S(1)}, u32[]{:S(2)}, u32[]{:S(2)}) collective-permute-start(bf16[288,384]{1,0:T(8,128)(2,1)S(1)} %get-tuple-element.36), channel_id=1, source_target_pairs={{0,2},{1,3},{2,0},{3,1},{4,6},{5,7},{6,4},{7,5},{8,10},{9,11},{10,... | collective-permute-start | bytes 663560 | tf_op jit(solution)/shard_map/ppermute | solution.py:423
  68.8 7.8 %collective-permute-start.11 = (bf16[96,384]{1,0:T(8,128)(2,1)S(1)}, bf16[96,384]{1,0:T(8,128)(2,1)S(1)}, u32[]{:S(2)}, u32[]{:S(2)}) collective-permute-start(bf16[96,384]{1,0:T(8,128)(2,1)S(1)} %get-tuple-element.39), channel_id=1, source_target_pairs={{0,198},{1,199},{2,196},{3,197},{4,194},{5,195},{6,192},{7,193},{8... | collective-permute-start | bytes 221192 | tf_op jit(solution)/shard_map/ppermute | solution.py:423
  71.9 6.1 %collective-permute-start.12 = (bf16[96,384]{1,0:T(8,128)(2,1)S(1)}, bf16[96,384]{1,0:T(8,128)(2,1)S(1)}, u32[]{:S(2)}, u32[]{:S(2)}) collective-permute-start(bf16[96,384]{1,0:T(8,128)(2,1)S(1)} %get-tuple-element.40), channel_id=1, source_target_pairs={{0,192},{1,193},{2,194},{3,195},{4,196},{5,197},{6,198},{7,199},{8... | collective-permute-start | bytes 221192 | tf_op jit(solution)/shard_map/ppermute | solution.py:423
  73.7 5.6 %collective-permute-start.13 = (bf16[96,384]{1,0:T(8,128)(2,1)S(1)}, bf16[96,384]{1,0:T(8,128)(2,1)S(1)}, u32[]{:S(2)}, u32[]{:S(2)}) collective-permute-start(bf16[96,384]{1,0:T(8,128)(2,1)S(1)} %get-tuple-element.41), channel_id=1, source_target_pairs={{0,6},{1,7},{2,4},{3,5},{4,2},{5,3},{6,0},{7,1},{8,14},{9,15},{10,... | collective-permute-start | bytes 221192 | tf_op jit(solution)/shard_map/ppermute | solution.py:423
  80.1 4.2 %collective-permute-start.14 = (f32[96,128]{1,0:T(8,128)S(1)}, f32[96,128]{1,0:T(8,128)S(1)}, u32[]{:S(2)}, u32[]{:S(2)}) collective-permute-start(f32[96,128]{1,0:T(8,128)S(1)} %get-tuple-element.44), channel_id=1, source_target_pairs={{0,24},{1,25},{2,26},{3,27},{4,28},{5,29},{6,30},{7,31},{8,16},{9,... | collective-permute-start | bytes 147464 | tf_op jit(solution)/shard_map/ppermute | solution.py:423
  81.7 5.1 %collective-permute-start.15 = (f32[96,128]{1,0:T(8,128)S(1)}, f32[96,128]{1,0:T(8,128)S(1)}, u32[]{:S(2)}, u32[]{:S(2)}) collective-permute-start(f32[96,128]{1,0:T(8,128)S(1)} %get-tuple-element.45), channel_id=1, source_target_pairs={{0,16},{1,17},{2,18},{3,19},{4,20},{5,21},{6,22},{7,23},{8,24},{9,... | collective-permute-start | bytes 147464 | tf_op jit(solution)/shard_map/ppermute | solution.py:423
  83.1 4.1 %collective-permute-start.16 = (f32[96,128]{1,0:T(8,128)S(1)}, f32[96,128]{1,0:T(8,128)S(1)}, u32[]{:S(2)}, u32[]{:S(2)}) collective-permute-start(f32[96,128]{1,0:T(8,128)S(1)} %get-tuple-element.46), channel_id=1, source_target_pairs={{0,8},{1,9},{2,10},{3,11},{4,12},{5,13},{6,14},{7,15},{8,0},{9,1},... | collective-permute-start | bytes 147464 | tf_op jit(solution)/shard_map/ppermute | solution.py:423
  87.8 7.2 %collective-permute-start.17 = (f32[96,128]{1,0:T(8,128)S(1)}, f32[96,128]{1,0:T(8,128)S(1)}, u32[]{:S(2)}, u32[]{:S(2)}) collective-permute-start(f32[96,128]{1,0:T(8,128)S(1)} %get-tuple-element.49), channel_id=1, source_target_pairs={{0,56},{1,57},{2,58},{3,59},{4,60},{5,61},{6,62},{7,63},{8,48},{9,... | collective-permute-start | bytes 147464 | tf_op jit(solution)/shard_map/ppermute | solution.py:423
